TPU v7x, 32 devices: a whole 2x2x4 slice. The times are simulated.
32 devices in a mesh: inv: 2 (over y), rcp: 4 (over z), reg: 2 (over x), tm: 2 (over core).
Axes of the slice: x: 2, y: 2, z: 4, core: 2. Of those that a mesh axis runs over, the one named last changes fastest.
Arguments:
- probes: bfloat16 [1024, 8, 2048], P(('inv', 'rcp')), parts along dimension 0, may hold values from -6 to 6
- footprint: bfloat16 [256, 16, 4, 256], P(('inv', 'rcp', 'reg'), None, 'tm'), parts along dimension 0, may hold values from 0.0029907227 to 0.099609375
- blocks: int32 [256, 16], P(('inv', 'rcp', 'reg')), parts along dimension 0, may hold values from 0 to 511, as said below
- hour_start: int32 [256], P(('inv', 'rcp', 'reg')), parts along dimension 0, may hold values from 0 to 4
- obs_weight: float32 [256], P(('inv', 'rcp', 'reg')), parts along dimension 0, may hold values from 0.5 to 4
- placement: int32 [1024], P('inv'), parts along dimension 0, may hold values from 0 to 511, as said below
Outputs:
- hessian_probe: float32 [1024, 8, 2048], P(('inv', 'rcp'), None, ('reg', 'tm')), parts along dimension 0
There are 2 independent parts, one for each index of `inv`. A program takes and returns all parts, laid end to end along the dimension named above; each array names one. Nothing has to cross between parts.
Inputs may be any that keep to these rules, and one draw needn't show every extreme that they name: Rows come in aligned blocks of 16 receptors, block d belonging to region group d % 2. Among the 256 entries of one block, at most 96 have placement[blocks] // 128 equal to any one value; in every region group one such value is taken exactly 96 times by every block of the group. Blocks may repeat. `placement`: A permutation of the 512 block rows.
All inputs are finite; a program needn't handle non-finite values.
Results may differ from a plain program's by a relative error of at most 0.0003.
Values may be sent and summed in bfloat16 or wider, within the bound.
No kernel may reach another device: no remote copies, remote signals or barrier semaphores. Data moves between devices by JAX's collectives and lax.ppermute only.
A program may use at most 64 MiB of HBM per device.

v0:
```python
import jax
import jax.numpy as jnp
from jax import lax
from jax.sharding import PartitionSpec as P


def shards(probes, footprint, blocks, hour_start, obs_weight, placement):
    owners = lax.axis_size("rcp")
    local_blocks, hour_count, row_width = probes.shape
    receptors, slot_count, half_window, block_cells = footprint.shape
    probe_count = row_width // block_cells
    entries = receptors * slot_count
    capacity = 3 * entries // (2 * owners)
    offset = lax.axis_index("tm") * half_window
    stored = placement[blocks.reshape(-1)]
    target = stored // local_blocks
    local_row = stored % local_blocks
    start_hour = jnp.repeat(hour_start + offset, slot_count)
    onehot = (target[:, None] == jnp.arange(owners, dtype=jnp.int32)[None, :]).astype(jnp.int32)
    ranking = jnp.cumsum(onehot, axis=0) - onehot
    slot_of = jnp.sum(ranking * onehot, axis=1)
    want_block = jnp.full((owners, capacity), -1, jnp.int32).at[target, slot_of].set(local_row)
    want_hour = jnp.zeros((owners, capacity), jnp.int32).at[target, slot_of].set(start_hour)
    got_block, got_hour = (
        lax.all_to_all(want_block, "rcp", split_axis=0, concat_axis=0, tiled=True),
        lax.all_to_all(want_hour, "rcp", split_axis=0, concat_axis=0, tiled=True),
    )
    hours_ahead = jnp.arange(half_window, dtype=jnp.int32)
    alive_slot = got_block >= 0
    base_row = jnp.where(alive_slot, got_block * hour_count + got_hour, 0)
    row_index = base_row[:, :, None] + hours_ahead[None, None, :]
    flat_rows = probes.reshape(local_blocks * hour_count, row_width)
    picked = jnp.where(
        alive_slot[:, :, None, None], flat_rows[row_index], jnp.zeros((), probes.dtype)
    )
    fetched = lax.all_to_all(picked, "rcp", split_axis=0, concat_axis=0, tiled=True)
    own_rows = fetched[target, slot_of].reshape(
        receptors, slot_count, half_window, probe_count, block_cells
    )
    partial_value = jnp.einsum(
        "rswc,rswkc->rk", footprint, own_rows, preferred_element_type=jnp.float32
    )
    observed = lax.psum(partial_value, "tm")
    weighted = obs_weight[:, None] * observed
    entry_terms = footprint.astype(jnp.float32)[:, :, :, None, :] * weighted[:, None, None, :, None]
    entry_terms = entry_terms.reshape(entries, half_window, row_width)
    outgoing = (
        jnp.zeros((owners, capacity, half_window, row_width), jnp.float32)
        .at[target, slot_of]
        .set(entry_terms)
    )
    incoming = lax.all_to_all(outgoing, "rcp", split_axis=0, concat_axis=0, tiled=True)
    summed = jnp.zeros((local_blocks * hour_count, row_width), jnp.float32)
    summed = summed.at[row_index.reshape(-1)].add(incoming.reshape(-1, row_width))
    result = lax.psum_scatter(
        summed.reshape(local_blocks, hour_count, row_width),
        ("reg", "tm"),
        scatter_dimension=2,
        tiled=True,
    )
    return result


def solution(mesh):
    return jax.shard_map(
        shards,
        mesh=mesh,
        in_specs=(
            P(("inv", "rcp"), None, None),
            P(("inv", "rcp", "reg"), None, "tm", None),
            P(("inv", "rcp", "reg"), None),
            P(("inv", "rcp", "reg")),
            P(("inv", "rcp", "reg")),
            P("inv"),
        ),
        out_specs=P(("inv", "rcp"), None, ("reg", "tm")),
        check_vma=False,
    )
```

profile of v0, /device:TPU:0, one launch (start us, length us, event | category | flops | bytes accessed | tf_op | source)
XLA Modules:
  0.0 517.0 jit_solution(4547546935191637373)
XLA Ops:
  6.5 0.0 copy-start
  6.5 0.8 reshape.216
  7.3 0.0 copy-done
  7.4 1.9 gather_fusion
  9.4 1.2 reduce-window.6
  10.6 0.1 slice.20
  10.7 0.1 copy.11
  10.8 0.1 copy.12
  10.9 0.1 add_bitcast_fusion
  11.0 0.6 broadcast_in_dim.19
  11.6 38.6 %scatter_fusion = s32[4,96]{1,0:T(4,128)} fusion(s32[4,96]{1,0:T(4,128)} %broadcast_in_dim.19, s32[256]{0:T(256)S(1)} %bitcast.62, s32[256]{0:T(256)S(1)} %get-tuple-element.7), kind=kCustom, calls=%fused_computation.3 | custom fusion | bytes 5120 | tf_op jit(solution)/shard_map/scatter | solution.py:22
  50.2 6.3 %all-to-all-start = ((s32[4,1,96]{2,1,0:T(1,128)}), s32[4,1,96]{2,1,0:T(1,128)S(1)}, u32[]{:S(2)}, u32[]{:S(2)}) async-start(s32[4,1,96]{2,1,0:T(1,128)} %bitcast.8), calls=%async_computation | async-start | bytes 4096 | tf_op jit(solution)/shard_map/all_to_all | solution.py:25
  56.5 0.7 broadcast_add_fusion
  57.2 0.1 broadcast_in_dim.20
  57.2 0.1 reshape.253
  57.3 0.6 broadcast.223
  57.9 38.3 %scatter_fusion.1 = s32[4,96]{1,0:T(4,128)} fusion(s32[4,96]{1,0:T(4,128)} %broadcast.223, s32[256]{0:T(256)S(1)} %bitcast.63, s32[256]{0:T(256)S(1)} %reshape.253), kind=kCustom, calls=%fused_computation.4 | custom fusion | bytes 5120 | tf_op jit(solution)/shard_map/scatter | solution.py:23
  96.2 0.0 all-to-all-done
  96.2 5.1 all-to-all-start.1
  101.3 5.5 %all-to-all-done.1 = s32[4,1,96]{2,1,0:T(1,128)S(1)} async-done(((s32[4,1,96]{2,1,0:T(1,128)}), s32[4,1,96]{2,1,0:T(1,128)S(1)}, u32[]{:S(2)}, u32[]{:S(2)}) %all-to-all-start.1) | async-done | bytes 1568 | tf_op jit(solution)/shard_map/all_to_all | solution.py:26
  106.8 0.1 compare_select_fusion
  106.9 0.1 reshape.233
  107.1 9.1 %gather_fusion.1 = bf16[768,2048]{1,0:T(8,128)(2,1)S(1)} fusion(bf16[1024,2048]{1,0:T(8,128)(2,1)} %bitcast.65, s32[1024]{0:T(1024)S(1)} %pad_clamp_fusion), kind=kCustom, calls=%fused_computation.1 | custom fusion | bytes 6294528 | tf_op jit(solution)/shard_map/gather | solution.py:34
  116.2 3.9 reshape.232
  120.0 6.5 %broadcast_select_fusion = bf16[4,96,2,2048]{3,2,1,0:T(2,128)(2,1)} fusion(bf16[4,96,2,2048]{3,2,1,0:T(2,128)(2,1)} %reshape.232, pred[4,96]{1,0:T(4,128)(4,1)S(1)} %compare_bitcast_fusion), kind=kLoop, calls=%fused_computation.7 | loop fusion | flops 1572864 | bytes 6291840 | tf_op jit(solution)/shard_map/jit(_where)/select_n | solution.py:33
  126.5 0.0 copy-start.2
  126.5 4.0 all-to-all-start.2
  130.5 0.0 copy-done.2
  130.5 2.5 mul.49
  133.1 5.9 %mul.50 = f32[256,2,2048]{2,1,0:T(2,128)} reshape(f32[16,16,2,8,256]{4,3,2,1,0:T(8,128)} %mul.49) | data formatting | bytes 8388608 | tf_op jit(solution)/shard_map/mul | solution.py:45
  138.9 60.3 %all-to-all-done.2 = bf16[4,96,2,2048]{3,2,1,0:T(2,128)(2,1)S(1)} async-done(((bf16[4,96,2,2048]{3,2,1,0:T(2,128)(2,1)}), bf16[4,96,2,2048]{3,2,1,0:T(2,128)(2,1)S(1)}, u32[]{:S(2)}, u32[]{:S(2)}) %all-to-all-start.2) | async-done | bytes 3145760 | tf_op jit(solution)/shard_map/all_to_all | solution.py:36
  199.3 12.1 %gather_fusion.2 = bf16[256,2,2048]{2,1,0:T(2,128)(2,1)} fusion(bf16[4,96,2,2048]{3,2,1,0:T(2,128)(2,1)S(1)} %all-to-all-done.2, s32[256]{0:T(256)S(1)} %bitcast.67), kind=kCustom, calls=%fused_computation.2 | custom fusion | bytes 4196352 | tf_op jit(solution)/shard_map/gather | solution.py:37
  211.3 0.0 copy-start.3
  211.4 3.2 reshape.220
  214.5 1.5 fusion.2
  216.0 2.5 psum.7
  218.4 0.0 copy-done.3
  218.4 0.1 broadcast_multiply_fusion.1
  218.5 0.2 mul.53
  218.7 0.9 copy.22
  219.6 6.5 %broadcast_multiply_fusion = f32[256,2,2048]{2,1,0:T(2,128)} fusion(f32[256,2,2048]{2,1,0:T(2,128)} %mul.50, f32[256,2048]{1,0:T(8,128)S(1)} %bitcast.68), kind=kLoop, calls=%fused_computation.12 | loop fusion | flops 1048576 | bytes 10485760 | tf_op jit(solution)/shard_map/mul | solution.py:45
  226.1 5.9 %broadcast_in_dim.25 = f32[4,96,2,2048]{3,2,1,0:T(2,128)} broadcast(f32[]{:T(128)} %constant.20.clone.1), dimensions={} | broadcast | bytes 6291460 | tf_op jit(solution)/shard_map/broadcast_in_dim | solution.py:48
  231.9 36.3 %scatter_fusion.2 = f32[4,96,2,2048]{3,2,1,0:T(2,128)} fusion(f32[4,96,2,2048]{3,2,1,0:T(2,128)} %broadcast_in_dim.25, s32[256]{0:T(256)S(1)} %bitcast.64, f32[256,2,2048]{2,1,0:T(2,128)} %broadcast_multiply_fusion), kind=kCustom, calls=%fused_computation.5 | custom fusion | bytes 12584960 | tf_op jit(solution)/shard_map/scatter | solution.py:50
  268.2 5.2 %all-to-all-start.3 = ((f32[4,96,2,2048]{3,2,1,0:T(2,128)}), f32[4,96,2,2048]{3,2,1,0:T(2,128)}, u32[]{:S(2)}, u32[]{:S(2)}) async-start(f32[4,96,2,2048]{3,2,1,0:T(2,128)} %scatter_fusion.2), calls=%async_computation.3 | async-start | bytes 12582912 | tf_op jit(solution)/shard_map/all_to_all | solution.py:52
  273.5 0.3 reduce-scatter.2.cloned.1.call-start
  273.8 0.1 iota_add_fusion
  273.9 0.2 add.154
  274.1 138.1 %all-to-all-done.3 = f32[4,96,2,2048]{3,2,1,0:T(2,128)} async-done(((f32[4,96,2,2048]{3,2,1,0:T(2,128)}), f32[4,96,2,2048]{3,2,1,0:T(2,128)}, u32[]{:S(2)}, u32[]{:S(2)}) %all-to-all-start.3) | async-done | bytes 6291488 | tf_op jit(solution)/shard_map/all_to_all | solution.py:52
  412.2 8.4 %reshape.267 = f32[768,2048]{1,0:T(8,128)} reshape(f32[4,96,2,2048]{3,2,1,0:T(2,128)} %all-to-all-done.3) | data formatting | bytes 12582912 | tf_op jit(solution)/shard_map/reshape | solution.py:54
  420.7 18.4 %scatter_custom_fusion.3 = f32[1024,2048]{1,0:T(8,128)} fusion(s32[768]{0:T(1024)S(1)} %fusion.8, f32[768,2048]{1,0:T(8,128)} %reshape.267, f32[]{:T(128)} %constant.20.clone.1), kind=kCustom, calls=%fused_computation.8 | custom fusion | flops 1572864 | bytes 8389120 | tf_op jit(solution)/shard_map/scatter-add | solution.py:54
  439.1 0.0 copy-start.1
  439.1 0.0 reduce-scatter.2.cloned.1.call-update
  439.1 71.0 %reduce-scatter.2.cloned.1.call-done = f32[128,8,512]{2,1,0:T(8,128)} async-done(((f32[128,8,2048]{2,1,0:T(8,128)}), f32[128,8,512]{2,1,0:T(8,128)}) %reduce-scatter.2.cloned.1.call-update) | async-done | bytes 2097168 | tf_op jit(solution)/shard_map/reduce_scatter | solution.py:55
  510.1 0.0 copy-done.1
  (13 shorter events, 0.2 us)
Async XLA Ops:
  6.5 0.8 copy-start
  50.2 46.0 %all-to-all-start = ((s32[4,1,96]{2,1,0:T(1,128)}), s32[4,1,96]{2,1,0:T(1,128)S(1)}, u32[]{:S(2)}, u32[]{:S(2)}) async-start(s32[4,1,96]{2,1,0:T(1,128)} %bitcast.8), calls=%async_computation | async-start | bytes 4096 | tf_op jit(solution)/shard_map/all_to_all | solution.py:25
  96.2 10.6 %all-to-all-start.1 = ((s32[4,1,96]{2,1,0:T(1,128)}), s32[4,1,96]{2,1,0:T(1,128)S(1)}, u32[]{:S(2)}, u32[]{:S(2)}) async-start(s32[4,1,96]{2,1,0:T(1,128)} %bitcast.13), calls=%async_computation.1 | async-start | bytes 4096 | tf_op jit(solution)/shard_map/all_to_all | solution.py:26
  126.5 4.0 copy-start.2
  126.5 72.8 %all-to-all-start.2 = ((bf16[4,96,2,2048]{3,2,1,0:T(2,128)(2,1)}), bf16[4,96,2,2048]{3,2,1,0:T(2,128)(2,1)S(1)}, u32[]{:S(2)}, u32[]{:S(2)}) async-start(bf16[4,96,2,2048]{3,2,1,0:T(2,128)(2,1)} %broadcast_select_fusion), calls=%async_computation.2 | async-start | bytes 6291456 | tf_op jit(solution)/shard_map/all_to_all | solution.py:36
  211.3 7.1 %copy-start.3 = (f32[16]{0:T(128)S(1)}, f32[16]{0:T(128)}, u32[]{:S(2)}) copy-start(f32[16]{0:T(128)} %param.10) | copy-start | bytes 196
  268.2 144.0 %all-to-all-start.3 = ((f32[4,96,2,2048]{3,2,1,0:T(2,128)}), f32[4,96,2,2048]{3,2,1,0:T(2,128)}, u32[]{:S(2)}, u32[]{:S(2)}) async-start(f32[4,96,2,2048]{3,2,1,0:T(2,128)} %scatter_fusion.2), calls=%async_computation.3 | async-start | bytes 12582912 | tf_op jit(solution)/shard_map/all_to_all | solution.py:52
  273.5 236.7 %reduce-scatter.2.cloned.1.call-start = ((), (), s32[]{:S(2)}) async-start(), calls=%async_computation.5 | async-start | bytes 10485760 | tf_op jit(solution)/shard_map/reduce_scatter | solution.py:55
  439.1 71.1 %copy-start.1 = (s32[512]{0:T(512)S(1)}, s32[512]{0:T(512)}, u32[]{:S(2)}) copy-start(s32[512]{0:T(512)} %param.11) | copy-start | bytes 6148
Sparse Core Ops, SparseCore 0:
  439.2 70.8 reduce-scatter.1
where the time goes:
time: 520 us; the launch traced here: 517 us
  waiting for transfers between devices  275 us (53%)
  local copies, waits for them, and re-layouts  170 us (33%)
  other arithmetic  33.8 us (6%)
  starting transfers between devices  21 us (4%)
  between operations  13.6 us (3%)
    all_to_all x1, waiting for transfers between devices, shards(): lax.all_to_all(outgoing, 'rcp', split_axis=0, concat_axis=0, tiled=True)  138 us
    reduce_scatter x1, waiting for transfers between devices, shards(): lax.psum_scatter(summed.reshape(local_blocks, hour_count, row_width), ('r...  71 us
    all_to_all x1, waiting for transfers between devices, shards(): lax.all_to_all(picked, 'rcp', split_axis=0, concat_axis=0, tiled=True)  60.3 us
    scatter x1, local copies, waits for them, and re-layouts, shards(): jnp.full((owners, capacity), -1, jnp.int32).at[target, slot_of]  38.6 us
    scatter x1, local copies, waits for them, and re-layouts, shards(): jnp.zeros((owners, capacity), jnp.int32).at[target, slot_of].set(start_hour)  38.3 us
    scatter x1, local copies, waits for them, and re-layouts, shards(): outgoing = jnp.zeros((owners, capacity, half_window, row_width), jnp.floa...  36.3 us
    scatter-add x1, other arithmetic, shards(): summed.at[row_index.reshape(-1)].add(incoming.reshape(-1, row_width))  18.4 us
    gather x2, local copies, waits for them, and re-layouts, shards(): flat_rows[row_index]  12.9 us
  transfers between devices with their start and end apart: 5, of which 4 were waited for; matrix products, arithmetic and copies ran while one was open for 9% of the time, Pallas kernels for 0%

commit v1 on v0

v1 whole, which is shorter than its diff:
```python
import functools

import jax
import jax.numpy as jnp
from jax import lax
from jax.experimental import pallas as pl
from jax.experimental.pallas import tpu as pltpu
from jax.sharding import PartitionSpec as P

F32 = jnp.float32
BF16 = jnp.bfloat16
I32 = jnp.int32
META = 16
VMEM_LIMIT = 48 * 1024 * 1024


def up(x, m):
    return (x + m - 1) // m * m


def log2(x):
    assert x & (x - 1) == 0
    return x.bit_length() - 1


def iota(shape, axis):
    return lax.broadcasted_iota(I32, shape, axis)


def mask(cond):
    return jnp.where(cond, jnp.float32(1), jnp.float32(0))


def nt(a, b):
    return lax.dot_general(a, b, (((1,), (1,)), ((), ())), preferred_element_type=F32)


def nn(a, b):
    return lax.dot_general(a, b, (((1,), (0,)), ((), ())), preferred_element_type=F32)


def pack_kernel(cfg, where_ref, blocks_ref, hour_ref, weight_ref, place_ref, fp_ref, *outs):
    n, capp, local_blocks, slots, w2 = cfg["n"], cfg["capp"], cfg["local"], cfg["slots"], cfg["w2"]
    receptors = blocks_ref.shape[0]
    cols = receptors * slots * w2
    ids = place_ref.shape[1]
    used = n * capp
    padded = up(used, 256)
    me = where_ref[0]
    tm = where_ref[1]
    lane = iota((1, cols), 1)
    entry = lane >> log2(w2)
    w_of = lane & (w2 - 1)
    s_of = entry & (slots - 1)
    r_of = entry >> log2(slots)
    b = blocks_ref[...]
    sel_s = mask(iota((slots, cols), 0) == s_of).astype(BF16)
    high = (b >> 6).astype(F32).astype(BF16)
    low = (b & 63).astype(F32).astype(BF16)
    spread = nn(high, sel_s) * 64.0 + nn(low, sel_s)
    on_row = iota((receptors, cols), 0) == r_of
    geo = jnp.sum(jnp.where(on_row, spread, 0.0), axis=0, keepdims=True).astype(I32)
    place = place_ref[...]
    row16 = iota((16, ids), 0)
    owner_tab = (place >> log2(local_blocks)).astype(F32)
    local_tab = (place & (local_blocks - 1)).astype(F32)
    tab = jnp.where(row16 == 0, owner_tab, jnp.where(row16 == 1, local_tab, 0.0)).astype(BF16)
    found = nn(tab, mask(iota((ids, cols), 0) == geo).astype(BF16))
    step = found[0:1].astype(I32) - me
    step = jnp.where(step < 0, step + n, step)
    local_row = found[1:2]
    nr = up(n, 16)
    to_owner = iota((nr, cols), 0) == step
    before = ((iota((cols, cols), 0) >> log2(w2)) < entry) & ((iota((cols, cols), 0) & (w2 - 1)) == 0)
    ranks = nn(mask(to_owner).astype(BF16), mask(before).astype(BF16))
    rank = jnp.sum(jnp.where(to_owner, ranks, 0.0), axis=0, keepdims=True).astype(I32)
    slot = step * capp + rank
    weight = weight_ref[...]
    w_hi = weight.astype(BF16).astype(F32)
    w_mid = (weight - w_hi).astype(BF16).astype(F32)
    w_lo = weight - w_hi - w_mid
    row_r = iota((16, receptors), 0)
    per_r = jnp.where(row_r == 1, hour_ref[...].astype(F32), 0.0)
    per_r = jnp.where(row_r == 3, w_hi, per_r)
    per_r = jnp.where(row_r == 4, w_mid, per_r)
    per_r = jnp.where(row_r == 5, w_lo, per_r)
    sel_r = mask(iota((receptors, cols), 0) == r_of).astype(BF16)
    values = nn(per_r.astype(BF16), sel_r)
    row_m = iota((16, cols), 0)
    values = jnp.where(row_m == 0, local_row + 1.0, values)
    values = jnp.where(row_m == 1, values + (tm * w2).astype(F32), values)
    values = jnp.where(row_m == 2, (r_of + me * receptors).astype(F32), values)
    fp = fp_ref[...]
    for w in range(w2):
        slot_w = jnp.where(w_of == w, slot, -1)
        pick = mask(iota((padded, cols), 0) == slot_w).astype(BF16)
        moved = nn(pick, fp).astype(BF16)
        for d in range(n):
            outs[d][w * capp : (w + 1) * capp, :] = moved[d * capp : (d + 1) * capp]
        if w == 0:
            meta = nt(values.astype(BF16), pick)[0:8]
            at = iota((8, padded), 1)
            for d in range(n):
                mine = jnp.where((at >= d * capp) & (at < (d + 1) * capp), meta, 0.0)
                halves = [mine[:, i : i + 256] for i in range(0, padded, 256)]
                halves += [jnp.zeros((8, 256), F32)] * (META // 8 - len(halves))
                outs[d][w2 * capp : w2 * capp + META, :] = jnp.concatenate(halves, axis=0).astype(BF16)


def pack(cfg, where, blocks, hour_start, obs_weight, placement, footprint):
    n, capp, slots, w2 = cfg["n"], cfg["capp"], cfg["slots"], cfg["w2"]
    receptors = blocks.shape[0]
    cells = footprint.shape[3]
    rows = w2 * capp + META
    vm = pl.BlockSpec(memory_space=pltpu.VMEM)
    return pl.pallas_call(
        functools.partial(pack_kernel, cfg),
        out_shape=[jax.ShapeDtypeStruct((rows, cells), BF16)] * n,
        in_specs=[pl.BlockSpec(memory_space=pltpu.SMEM)] + [vm] * 5,
        out_specs=[vm] * n,
        compiler_params=pltpu.CompilerParams(vmem_limit_bytes=VMEM_LIMIT),
        name="pack",
    )(
        where,
        blocks,
        hour_start.reshape(1, receptors),
        obs_weight.reshape(1, receptors),
        placement.reshape(1, -1),
        footprint.reshape(receptors * slots * w2, cells),
    )


def load_meta(cfg, bufs, rows):
    n, w2, capp = cfg["n"], cfg["w2"], cfg["capp"]
    total = None
    for buf, base in slots_of(bufs, rows, n):
        part = buf[base + w2 * capp : base + w2 * capp + META, :].astype(F32)
        total = part if total is None else total + part
    halves = up(n * capp, 256) // 256
    return jnp.concatenate([total[8 * i : 8 * i + 8] for i in range(halves)], axis=1)


def slots_of(bufs, rows, n):
    out = []
    for buf in bufs:
        for base in range(0, buf.shape[0], rows):
            out.append((buf, base))
    assert len(out) == n
    return out


def hour_column(meta, width):
    pick = mask(iota((8, width), 0) == 1)
    return lax.dot_general(
        meta.astype(BF16), pick.astype(BF16), (((0,), (0,)), ((), ())), preferred_element_type=F32
    )


def spread_hours(cfg, sides, metas, rows, f8_ref, base_row):
    n, w2, capp, hours, cells = cfg["n"], cfg["w2"], cfg["capp"], cfg["hours"], cfg["cells"]
    columns = [hour_column(m, cells).astype(BF16) for m in metas]
    placed = [slots_of(bufs, rows, n) for bufs in sides]
    for d in range(n):
        parts = []
        for side in range(len(sides)):
            buf, base = placed[side][d]
            first = columns[side][d * capp : (d + 1) * capp]
            for w in range(w2):
                parts.append((first + BF16(w) if w else first, buf[base + w * capp : base + (w + 1) * capp, :]))
        for h in range(hours):
            value = jnp.zeros((capp, cells), BF16)
            for first, fp in parts:
                value = jnp.where(first == BF16(h), fp, value)
            f8_ref[base_row + d * capp : base_row + (d + 1) * capp, h * cells : (h + 1) * cells] = value


def forward_kernel(cfg, nbuf, *refs):
    bufs, probes_ref, out_ref, f8_ref, meta_ref, dots_ref = (
        refs[:nbuf], refs[nbuf], refs[nbuf + 1], refs[nbuf + 2], refs[nbuf + 3], refs[nbuf + 4],
    )
    n, w2, capp, local = cfg["n"], cfg["w2"], cfg["capp"], cfg["local"]
    rows = w2 * capp + META
    used = n * capp
    k_step = probes_ref.shape[0] // local
    i = pl.program_id(0)

    @pl.when(i == 0)
    def _():
        meta = load_meta(cfg, bufs, rows)
        meta_ref[...] = meta
        spread_hours(cfg, [bufs], [meta], rows, f8_ref, 0)
        dots_ref[...] = jnp.zeros_like(dots_ref)

    own = mask(iota((local, used), 0) + 1 == meta_ref[0:1, 0:used].astype(I32))
    x = nt(probes_ref[...], f8_ref[...])
    row = iota((8, used), 0)
    acc = dots_ref[:, 0:used]
    for j in range(k_step):
        y = jnp.sum(x[j * local : (j + 1) * local] * own, axis=0, keepdims=True)
        acc = jnp.where(row == i * k_step + j, y, acc)
    dots_ref[:, 0:used] = acc

    @pl.when(i == pl.num_programs(0) - 1)
    def _():
        to_r = mask(iota((out_ref.shape[1], used), 0) == meta_ref[2:3, 0:used].astype(I32))
        out_ref[...] = lax.dot_general(
            acc, to_r, (((1,), (1,)), ((), ())), precision=lax.Precision.HIGHEST, preferred_element_type=F32
        )


def forward(cfg, bufs, probes_t):
    n, capp, hours, cells, local = cfg["n"], cfg["capp"], cfg["hours"], cfg["cells"], cfg["local"]
    used = n * capp
    vm = pl.BlockSpec(memory_space=pltpu.VMEM)
    whole = [pl.BlockSpec(b.shape, lambda i: (0, 0)) for b in bufs]
    steps = 4
    tile = probes_t.shape[0] // steps
    rp = up(n * cfg["receptors"], 128)
    return pl.pallas_call(
        functools.partial(forward_kernel, cfg, len(bufs)),
        out_shape=jax.ShapeDtypeStruct((8, rp), F32),
        grid=(steps,),
        in_specs=whole + [pl.BlockSpec((tile, hours * cells), lambda i: (i, 0))],
        out_specs=pl.BlockSpec((8, rp), lambda i: (0, 0)),
        scratch_shapes=[
            pltpu.VMEM((used, hours * cells), BF16),
            pltpu.VMEM((8, up(used, 256)), F32),
            pltpu.VMEM((8, up(used, 256)), F32),
        ],
        compiler_params=pltpu.CompilerParams(vmem_limit_bytes=VMEM_LIMIT),
        name="forward",
    )(*bufs, probes_t)


def adjoint_kernel(cfg, counts, where_ref, *refs):
    n, w2, capp, local, hours, cells = (
        cfg["n"], cfg["w2"], cfg["capp"], cfg["local"], cfg["hours"], cfg["cells"],
    )
    rows = w2 * capp + META
    used = n * capp
    kd = cfg["kd"]
    refs = list(refs)
    out_ref, f8_ref, a_ref, tiles_ref, sems = refs[-5:]
    at = 0
    for c, sides_n in enumerate(counts):
        obs = refs[at][...]
        at += 1
        sides = []
        for count in sides_n:
            sides.append(refs[at : at + count])
            at += count
        metas = [load_meta(cfg, bufs, rows) for bufs in sides]
        spread_hours(cfg, sides, metas, rows, f8_ref, c * used)
        meta = metas[0][:, 0:used]
        to_r = mask(iota((obs.shape[1], used), 0) == meta[2:3].astype(I32))
        per_entry = lax.dot_general(
            obs, to_r, (((1,), (0,)), ((), ())), precision=lax.Precision.HIGHEST, preferred_element_type=F32
        )
        per_entry = per_entry * (meta[3:4] + meta[4:5] + meta[5:6])
        own = iota((local, used), 0) + 1 == meta[0:1].astype(I32)
        row = iota((8, used), 0)
        for j in range(kd):
            term = jnp.sum(jnp.where(row == where_ref[2] * kd + j, per_entry, 0.0), axis=0, keepdims=True)
            high = term.astype(BF16).astype(F32)
            for p, part in enumerate((high, term - high)):
                a_ref[(p * kd + j) * local : (p * kd + j + 1) * local, c * used : (c + 1) * used] = jnp.where(
                    own, part, 0.0
                ).astype(BF16)
    a = a_ref[...]
    for h in range(hours):
        sums = nn(a, f8_ref[:, h * cells : (h + 1) * cells])
        for j in range(kd):
            both = sums[j * local : (j + 1) * local] + sums[(kd + j) * local : (kd + j + 1) * local]
            for t in range(cells // 128):
                tile = tiles_ref.at[j * (cells // 128) + t]
                tile[pl.ds(h, local, stride=hours), :] = both[:, t * 128 : (t + 1) * 128]
    copies = [
        pltpu.make_async_copy(tiles_ref.at[t], out_ref.at[:, pl.ds(t * 128, 128)], sems.at[t])
        for t in range(kd * cells // 128)
    ]
    for copy in copies:
        copy.start()
    for copy in copies:
        copy.wait()


def adjoint(cfg, where, columns):
    n, capp, hours, cells, local, kd = (
        cfg["n"], cfg["capp"], cfg["hours"], cfg["cells"], cfg["local"], cfg["kd"],
    )
    total = len(columns) * n * capp
    vm = pl.BlockSpec(memory_space=pltpu.VMEM)
    args, counts = [], []
    for obs, sides in columns:
        args.append(obs)
        counts.append([len(s) for s in sides])
        for s in sides:
            args += s
    return pl.pallas_call(
        functools.partial(adjoint_kernel, cfg, counts),
        out_shape=jax.ShapeDtypeStruct((local * hours, kd * cells), F32),
        in_specs=[pl.BlockSpec(memory_space=pltpu.SMEM)] + [vm] * len(args),
        out_specs=pl.BlockSpec(memory_space=pl.ANY),
        scratch_shapes=[
            pltpu.VMEM((total, hours * cells), BF16),
            pltpu.VMEM((2 * kd * local, total), BF16),
            pltpu.VMEM((kd * cells // 128, local * hours, 128), F32),
            pltpu.SemaphoreType.DMA((kd * cells // 128,)),
        ],
        compiler_params=pltpu.CompilerParams(vmem_limit_bytes=VMEM_LIMIT),
        name="adjoint",
    )(where, *args)


def shift(x, axis, d):
    n = lax.axis_size(axis)
    return lax.ppermute(x, axis, [(i, (i + d) % n) for i in range(n)])


def shards(probes, footprint, blocks, hour_start, obs_weight, placement):
    n, nreg, ntm = lax.axis_size("rcp"), lax.axis_size("reg"), lax.axis_size("tm")
    local, hours, width = probes.shape
    receptors, slots, w2, cells = footprint.shape
    k = width // cells
    cap = 3 * receptors * slots // (2 * n)
    cfg = dict(
        n=n, capp=up(cap, 16), local=local, hours=hours, cells=cells, receptors=receptors,
        slots=slots, w2=w2, kd=k // (nreg * ntm),
    )
    z, reg, tm = lax.axis_index("rcp"), lax.axis_index("reg"), lax.axis_index("tm")
    where = jnp.stack([z, tm, reg * ntm + tm]).astype(I32)
    outs = pack(cfg, where, blocks, hour_start, obs_weight, placement, footprint)
    bufs = [outs[0]] + [shift(outs[d], "rcp", d) for d in range(1, n)]
    probes_t = probes.reshape(local, hours, k, cells).transpose(2, 0, 1, 3).reshape(k * local, hours * cells)
    if n > 4:
        bufs = [jnp.concatenate(bufs, axis=0)]
    partial = forward(cfg, bufs, probes_t)
    sides = [bufs] + [[shift(b, "tm", s) for b in bufs] for s in range(1, ntm)]
    columns = [sides]
    for g in range(1, nreg):
        across = [shift(b, "reg", g) for b in bufs]
        columns.append([across] + [[shift(b, "tm", s) for b in across] for s in range(1, ntm)])
    observed = partial
    for d in range(1, n):
        observed = observed + shift(partial, "rcp", d)
    both = observed
    for s in range(1, ntm):
        both = both + shift(observed, "tm", s)
    obs = [both] + [shift(both, "reg", g) for g in range(1, nreg)]
    result = adjoint(cfg, where, list(zip(obs, columns)))
    return result.reshape(local, hours, cfg["kd"] * cells)


def solution(mesh):
    return jax.shard_map(
        shards,
        mesh=mesh,
        in_specs=(
            P(("inv", "rcp"), None, None),
            P(("inv", "rcp", "reg"), None, "tm", None),
            P(("inv", "rcp", "reg"), None),
            P(("inv", "rcp", "reg")),
            P(("inv", "rcp", "reg")),
            P("inv"),
        ),
        out_specs=P(("inv", "rcp"), None, ("reg", "tm")),
        check_vma=False,
    )
```

time: 520 us -> 49.1 us (0.09)
  waiting for transfers between devices: 275 us -> 11.8 us
  local copies, waits for them, and re-layouts: 170 us -> 7.68 us
  other arithmetic: 33.8 us -> 0.09 us
  between operations: 13.6 us -> 0.06 us
  Pallas kernels: 0 us -> 10.4 us
    all_to_all x4 -> x0, waiting for transfers between devices: 204 us -> none  [the longest x1 138 us: shards(): lax.all_to_all(outgoing, 'rcp', split_axis=0, concat_axis=0, tiled=True)]
    scatter x3 -> x0, local copies, waits for them, and re-layouts: 113 us -> none  [the longest x1 38.6 us: shards(): jnp.full((owners, capacity), -1, jnp.int32).at[target, slot_of]]
    reduce_scatter x1 -> x0, waiting for transfers between devices: 71 us -> none  [shards(): lax.psum_scatter(summed.reshape(local_blocks, hour_count, row_width), ('r...]
    gather x4 -> x0, local copies, waits for them, and re-layouts: 26.9 us -> none  [the longest x2 12.9 us: shards(): flat_rows[row_index]]
    all_to_all x4 -> x0, starting transfers between devices: 20.7 us -> none  [the longest x1 6.32 us: shards(): lax.all_to_all(want_block, 'rcp', split_axis=0, concat_axis=0, tiled=True)]
    ppermute x0 -> x20, starting transfers between devices: none -> 18.8 us  [shift(): return lax.ppermute(x, axis, [(i, (i + d) % n) for i in range(n)])]
    scatter-add x1 -> x0, other arithmetic: 18.4 us -> none  [shards(): summed.at[row_index.reshape(-1)].add(incoming.reshape(-1, row_width))]
    ppermute x0 -> x20, waiting for transfers between devices: none -> 11.8 us  [shift(): return lax.ppermute(x, axis, [(i, (i + d) % n) for i in range(n)])]
  transfers between devices with their start and end apart: 5 -> 20, of which waited for: 4 -> 10; matrix products, arithmetic and copies ran while one was open for 9% -> 8% of each run, Pallas kernels for 0% -> 0%
where the time goes in v1:
time: 49.1 us; the launch traced here: 48.8 us
  starting transfers between devices  18.8 us (38%)
  waiting for transfers between devices  11.8 us (24%)
  Pallas kernels  10.4 us (21%)
  local copies, waits for them, and re-layouts  7.68 us (16%)
    ppermute x20, starting transfers between devices, shift(): return lax.ppermute(x, axis, [(i, (i + d) % n) for i in range(n)])  18.8 us
    ppermute x20, waiting for transfers between devices, shift(): return lax.ppermute(x, axis, [(i, (i + d) % n) for i in range(n)])  11.8 us
    pallas_call x1, Pallas kernels, adjoint(): pl.pallas_call(functools.partial(adjoint_kernel, cfg, counts), out_shape=...  5.1 us
    unnamed x9, local copies, waits for them, and re-layouts  4.18 us
    pallas_call x1, Pallas kernels, forward(): pl.pallas_call(functools.partial(forward_kernel, cfg, len(bufs)), out_sha...  3.73 us
    reshape x1, local copies, waits for them, and re-layouts, shards(): probes.reshape(local, hours, k, cells).transpose(2, 0, 1, 3)  2.46 us
    pallas_call x1, Pallas kernels, pack(): pl.pallas_call(functools.partial(pack_kernel, cfg), out_shape=[jax.ShapeD...  1.61 us
    reshape x1, local copies, waits for them, and re-layouts, pack(): footprint.reshape(receptors * slots * w2, cells)  1.05 us
  transfers between devices with their start and end apart: 20, of which 10 were waited for; matrix products, arithmetic and copies ran while one was open for 8% of the time, Pallas kernels for 0%

profile of v1, /device:TPU:0, one launch (start us, length us, event | category | flops | bytes accessed | tf_op | source)
XLA Modules:
  0.0 48.8 jit_solution(12443998360542854386)
XLA Ops:
  0.0 1.1 %reshape.24.fp_ref = bf16[512,256]{1,0:T(8,128)(2,1)S(1)} reshape(bf16[16,16,2,256]{3,2,1,0:T(2,128)(2,1)} %param.7) | data formatting | bytes 524288 | tf_op jit(solution)/shard_map/reshape | solution.py:129
  1.1 0.1 pad_add_fusion.where_ref
  1.1 0.0 copy-start
  1.1 0.7 %copy-done = s32[16,16]{1,0:T(8,128)S(1)} copy-done((s32[16,16]{1,0:T(8,128)S(1)}, s32[16,16]{1,0:T(8,128)}, u32[]{:S(2)}) %copy-start) | copy-done | bytes 1048
  1.8 0.0 copy-start.1
  1.8 0.7 %copy-done.1 = s32[512]{0:T(512)S(1)} copy-done((s32[512]{0:T(512)S(1)}, s32[512]{0:T(512)}, u32[]{:S(2)}) %copy-start.1) | copy-done | bytes 2072
  2.5 0.0 copy-start.2
  2.5 0.7 %copy-done.2 = s32[16]{0:T(128)S(1)} copy-done((s32[16]{0:T(128)S(1)}, s32[16]{0:T(128)}, u32[]{:S(2)}) %copy-start.2) | copy-done | bytes 88
  3.2 0.0 copy-start.3
  3.2 0.7 %copy-done.3 = f32[16]{0:T(128)S(1)} copy-done((f32[16]{0:T(128)S(1)}, f32[16]{0:T(128)}, u32[]{:S(2)}) %copy-start.3) | copy-done | bytes 88
  3.8 1.6 %pack.1 = (bf16[208,256]{1,0:T(8,128)(2,1)S(1)}, bf16[208,256]{1,0:T(8,128)(2,1)S(1)}, bf16[208,256]{1,0:T(8,128)(2,1)S(1)}, bf16[208,256]{1,0:T(8,128)(2,1)S(1)}) custom-call(s32[3]{0:T(128)S(1)} %pad_add_fusion.where_ref, s32[16,16]{1,0:T(8,128)S(1)} %copy-done, s32[1,16]{1,0:T(1,128)S(1)} %bitcast.14, f32[1,16]{1,0:T(1,128)S(1)} %bitcast.15, ...), custom_call_target="tpu_custom_call" | custom-call | tf_op jit(solution)/shard_map/pack/pallas_call | solution.py:116
  5.5 3.1 %collective-permute-start = (bf16[208,256]{1,0:T(8,128)(2,1)S(1)}, bf16[208,256]{1,0:T(8,128)(2,1)S(1)}, u32[]{:S(2)}, u32[]{:S(2)}) collective-permute-start(bf16[208,256]{1,0:T(8,128)(2,1)S(1)} %get-tuple-element.10), channel_id=1, source_target_pairs={{0,4},{4,8},{8,12},{12,0},{1,5},{5,9},{9,13},{13,1},{2,6},{6,10},{... | collective-permute-start | bytes 319496 | tf_op jit(solution)/shard_map/ppermute | solution.py:317
  8.5 2.6 %collective-permute-start.1 = (bf16[208,256]{1,0:T(8,128)(2,1)S(1)}, bf16[208,256]{1,0:T(8,128)(2,1)S(1)}, u32[]{:S(2)}, u32[]{:S(2)}) collective-permute-start(bf16[208,256]{1,0:T(8,128)(2,1)S(1)} %get-tuple-element.11), channel_id=1, source_target_pairs={{0,8},{4,12},{8,0},{12,4},{1,9},{5,13},{9,1},{13,5},{2,10},{6,14},... | collective-permute-start | bytes 319496 | tf_op jit(solution)/shard_map/ppermute | solution.py:317
  11.1 1.3 %collective-permute-start.2 = (bf16[208,256]{1,0:T(8,128)(2,1)S(1)}, bf16[208,256]{1,0:T(8,128)(2,1)S(1)}, u32[]{:S(2)}, u32[]{:S(2)}) collective-permute-start(bf16[208,256]{1,0:T(8,128)(2,1)S(1)} %get-tuple-element.12), channel_id=1, source_target_pairs={{0,12},{4,0},{8,4},{12,8},{1,13},{5,1},{9,5},{13,9},{2,14},{6,2},{... | collective-permute-start | bytes 319496 | tf_op jit(solution)/shard_map/ppermute | solution.py:317
  12.5 2.5 %copy.7 = bf16[128,8,8,256]{3,1,0,2:T(8,128)(2,1)S(1)} copy(bf16[128,8,8,256]{3,1,2,0:T(8,128)(2,1)} %bitcast.17) | data formatting | bytes 8388608 | tf_op jit(solution)/shard_map/reshape | solution.py:334
  14.9 1.5 %copy.8 = bf16[128,8,8,256]{3,1,2,0:T(8,128)(2,1)S(1)} copy(bf16[128,8,8,256]{3,2,1,0:T(8,128)(2,1)S(1)} %bitcast.16) | data formatting | bytes 8388608
  16.4 0.0 collective-permute-done.refs_1_.refs_2_
  16.4 1.8 %collective-permute-done.1.refs_2_.refs_3_ = bf16[208,256]{1,0:T(8,128)(2,1)S(1)} collective-permute-done((bf16[208,256]{1,0:T(8,128)(2,1)S(1)}, bf16[208,256]{1,0:T(8,128)(2,1)S(1)}, u32[]{:S(2)}, u32[]{:S(2)}) %collective-permute-start.1) | collective-permute-done | bytes 106528 | tf_op jit(solution)/shard_map/ppermute | solution.py:317
  18.2 0.0 collective-permute-done.2.refs_3_.refs_4_
  18.2 3.7 %forward.1 = f32[8,128]{1,0:T(8,128)S(1)} custom-call(bf16[208,256]{1,0:T(8,128)(2,1)S(1)} %get-tuple-element.9.refs_0_.refs_1_, bf16[208,256]{1,0:T(8,128)(2,1)S(1)} %collective-permute-done.refs_1_.refs_2_, bf16[208,256]{1,0:T(8,128)(2,1)S(1)} %collective-permute-done.1.refs_2_.refs_3_, bf16[208,256]{1,0:T(8,128)(2,1)S(1)} %collective-permute-done.2.refs_3_.refs_4_, ...), custom_call_target="tpu_custom_call" | custom-call | tf_op jit(solution)/shard_map/forward/pallas_call | solution.py:219
  22.0 2.8 %collective-permute-start.3 = (f32[8,128]{1,0:T(8,128)S(1)}, f32[8,128]{1,0:T(8,128)S(1)}, u32[]{:S(2)}, u32[]{:S(2)}) collective-permute-start(f32[8,128]{1,0:T(8,128)S(1)} %forward.1), channel_id=1, source_target_pairs={{0,4},{4,8},{8,12},{12,0},{1,5},{5,9},{9,13},{13,1},{2,6},{6,10},{... | collective-permute-start | bytes 12296 | tf_op jit(solution)/shard_map/ppermute | solution.py:317
  24.7 1.6 %collective-permute-start.4 = (f32[8,128]{1,0:T(8,128)S(1)}, f32[8,128]{1,0:T(8,128)S(1)}, u32[]{:S(2)}, u32[]{:S(2)}) collective-permute-start(f32[8,128]{1,0:T(8,128)S(1)} %forward.1), channel_id=1, source_target_pairs={{0,8},{4,12},{8,0},{12,4},{1,9},{5,13},{9,1},{13,5},{2,10},{6,14},... | collective-permute-start | bytes 12296 | tf_op jit(solution)/shard_map/ppermute | solution.py:317
  26.3 0.8 %collective-permute-start.5 = (f32[8,128]{1,0:T(8,128)S(1)}, f32[8,128]{1,0:T(8,128)S(1)}, u32[]{:S(2)}, u32[]{:S(2)}) collective-permute-start(f32[8,128]{1,0:T(8,128)S(1)} %forward.1), channel_id=1, source_target_pairs={{0,12},{4,0},{8,4},{12,8},{1,13},{5,1},{9,5},{13,9},{2,14},{6,2},{... | collective-permute-start | bytes 12296 | tf_op jit(solution)/shard_map/ppermute | solution.py:317
  27.1 1.5 %collective-permute-start.12 = (bf16[208,256]{1,0:T(8,128)(2,1)S(1)}, bf16[208,256]{1,0:T(8,128)(2,1)S(1)}, u32[]{:S(2)}, u32[]{:S(2)}) collective-permute-start(bf16[208,256]{1,0:T(8,128)(2,1)S(1)} %get-tuple-element.9.refs_0_.refs_1_), channel_id=1, source_target_pairs={{0,2},{2,0},{1,3},{3,1},{4,6},{6,4},{5,7},{7,5},{8,10},{10,8},{9,1... | collective-permute-start | bytes 319496 | tf_op jit(solution)/shard_map/ppermute | solution.py:317
  28.6 0.0 collective-permute-start.7
  28.6 0.0 collective-permute-done.3
  28.6 0.6 %collective-permute-done.4 = f32[8,128]{1,0:T(8,128)S(1)} collective-permute-done((f32[8,128]{1,0:T(8,128)S(1)}, f32[8,128]{1,0:T(8,128)S(1)}, u32[]{:S(2)}, u32[]{:S(2)}) %collective-permute-start.4) | collective-permute-done | bytes 4128 | tf_op jit(solution)/shard_map/ppermute | solution.py:317
  29.2 0.7 %collective-permute-done.5 = f32[8,128]{1,0:T(8,128)S(1)} collective-permute-done((f32[8,128]{1,0:T(8,128)S(1)}, f32[8,128]{1,0:T(8,128)S(1)}, u32[]{:S(2)}, u32[]{:S(2)}) %collective-permute-start.5) | collective-permute-done | bytes 4128 | tf_op jit(solution)/shard_map/ppermute | solution.py:317
  29.9 0.0 collective-permute-start.6
  29.9 1.2 %collective-permute-done.6 = f32[8,128]{1,0:T(8,128)S(1)} collective-permute-done((f32[8,128]{1,0:T(8,128)S(1)}, f32[8,128]{1,0:T(8,128)S(1)}, u32[]{:S(2)}, u32[]{:S(2)}) %collective-permute-start.6) | collective-permute-done | bytes 4128 | tf_op jit(solution)/shard_map/ppermute | solution.py:317
  31.1 1.5 %collective-permute-start.11 = (f32[8,128]{1,0:T(8,128)S(1)}, f32[8,128]{1,0:T(8,128)S(1)}, u32[]{:S(2)}, u32[]{:S(2)}) collective-permute-start(f32[8,128]{1,0:T(8,128)S(1)} %add.19.refs_0_), channel_id=1, source_target_pairs={{0,2},{2,0},{1,3},{3,1},{4,6},{6,4},{5,7},{7,5},{8,10},{10,8},{9,1... | collective-permute-start | bytes 12296 | tf_op jit(solution)/shard_map/ppermute | solution.py:317
  32.6 0.5 %collective-permute-start.13 = (bf16[208,256]{1,0:T(8,128)(2,1)S(1)}, bf16[208,256]{1,0:T(8,128)(2,1)S(1)}, u32[]{:S(2)}, u32[]{:S(2)}) collective-permute-start(bf16[208,256]{1,0:T(8,128)(2,1)S(1)} %collective-permute-done.refs_1_.refs_2_), channel_id=1, source_target_pairs={{0,2},{2,0},{1,3},{3,1},{4,6},{6,4},{5,7},{7,5},{8,10},{10,8},{9,1... | collective-permute-start | bytes 319496 | tf_op jit(solution)/shard_map/ppermute | solution.py:317
  33.1 1.5 %collective-permute-start.14 = (bf16[208,256]{1,0:T(8,128)(2,1)S(1)}, bf16[208,256]{1,0:T(8,128)(2,1)S(1)}, u32[]{:S(2)}, u32[]{:S(2)}) collective-permute-start(bf16[208,256]{1,0:T(8,128)(2,1)S(1)} %collective-permute-done.1.refs_2_.refs_3_), channel_id=1, source_target_pairs={{0,2},{2,0},{1,3},{3,1},{4,6},{6,4},{5,7},{7,5},{8,10},{10,8},{9,1... | collective-permute-start | bytes 319496 | tf_op jit(solution)/shard_map/ppermute | solution.py:317
  34.6 0.0 collective-permute-done.12.refs_10_
  34.6 0.5 %collective-permute-start.15 = (bf16[208,256]{1,0:T(8,128)(2,1)S(1)}, bf16[208,256]{1,0:T(8,128)(2,1)S(1)}, u32[]{:S(2)}, u32[]{:S(2)}) collective-permute-start(bf16[208,256]{1,0:T(8,128)(2,1)S(1)} %collective-permute-done.2.refs_3_.refs_4_), channel_id=1, source_target_pairs={{0,2},{2,0},{1,3},{3,1},{4,6},{6,4},{5,7},{7,5},{8,10},{10,8},{9,1... | collective-permute-start | bytes 319496 | tf_op jit(solution)/shard_map/ppermute | solution.py:317
  35.2 0.0 collective-permute-done.7.refs_5_
  35.2 0.0 collective-permute-start.16
  35.2 0.0 collective-permute-done.11.refs_9_
  35.2 0.5 %collective-permute-start.10 = (bf16[208,256]{1,0:T(8,128)(2,1)S(1)}, bf16[208,256]{1,0:T(8,128)(2,1)S(1)}, u32[]{:S(2)}, u32[]{:S(2)}) collective-permute-start(bf16[208,256]{1,0:T(8,128)(2,1)S(1)} %collective-permute-done.2.refs_3_.refs_4_), channel_id=1, source_target_pairs={{0,1},{1,0},{2,3},{3,2},{4,5},{5,4},{6,7},{7,6},{8,9},{9,8},{10,11... | collective-permute-start | bytes 319496 | tf_op jit(solution)/shard_map/ppermute | solution.py:317
  35.7 2.8 %collective-permute-done.13.refs_11_ = bf16[208,256]{1,0:T(8,128)(2,1)S(1)} collective-permute-done((bf16[208,256]{1,0:T(8,128)(2,1)S(1)}, bf16[208,256]{1,0:T(8,128)(2,1)S(1)}, u32[]{:S(2)}, u32[]{:S(2)}) %collective-permute-start.13) | collective-permute-done | bytes 106528 | tf_op jit(solution)/shard_map/ppermute | solution.py:317
  38.4 0.0 collective-permute-start.8
  38.4 2.3 %collective-permute-done.14.refs_12_ = bf16[208,256]{1,0:T(8,128)(2,1)S(1)} collective-permute-done((bf16[208,256]{1,0:T(8,128)(2,1)S(1)}, bf16[208,256]{1,0:T(8,128)(2,1)S(1)}, u32[]{:S(2)}, u32[]{:S(2)}) %collective-permute-start.14) | collective-permute-done | bytes 106528 | tf_op jit(solution)/shard_map/ppermute | solution.py:317
  40.7 0.0 collective-permute-start.9
  40.7 1.2 %collective-permute-done.15.refs_13_ = bf16[208,256]{1,0:T(8,128)(2,1)S(1)} collective-permute-done((bf16[208,256]{1,0:T(8,128)(2,1)S(1)}, bf16[208,256]{1,0:T(8,128)(2,1)S(1)}, u32[]{:S(2)}, u32[]{:S(2)}) %collective-permute-start.15) | collective-permute-done | bytes 106528 | tf_op jit(solution)/shard_map/ppermute | solution.py:317
  41.9 0.0 collective-permute-start.17
  41.9 0.0 collective-permute-done.16.refs_14_
  41.9 0.5 %collective-permute-start.18 = (bf16[208,256]{1,0:T(8,128)(2,1)S(1)}, bf16[208,256]{1,0:T(8,128)(2,1)S(1)}, u32[]{:S(2)}, u32[]{:S(2)}) collective-permute-start(bf16[208,256]{1,0:T(8,128)(2,1)S(1)} %collective-permute-done.14.refs_12_), channel_id=1, source_target_pairs={{0,1},{1,0},{2,3},{3,2},{4,5},{5,4},{6,7},{7,6},{8,9},{9,8},{10,11... | collective-permute-start | bytes 319496 | tf_op jit(solution)/shard_map/ppermute | solution.py:317
  42.4 0.0 collective-permute-done.10.refs_8_
  42.4 0.1 collective-permute-start.19
  42.5 0.0 collective-permute-done.8.refs_6_
  42.5 0.0 collective-permute-done.9.refs_7_
  42.5 0.7 %collective-permute-done.17.refs_15_ = bf16[208,256]{1,0:T(8,128)(2,1)S(1)} collective-permute-done((bf16[208,256]{1,0:T(8,128)(2,1)S(1)}, bf16[208,256]{1,0:T(8,128)(2,1)S(1)}, u32[]{:S(2)}, u32[]{:S(2)}) %collective-permute-start.17) | collective-permute-done | bytes 106528 | tf_op jit(solution)/shard_map/ppermute | solution.py:317
  43.2 0.2 collective-permute-done.18.refs_16_
  43.4 0.4 collective-permute-done.19.refs_17_
  43.8 5.1 %adjoint.1 = f32[1024,512]{1,0:T(8,128)} custom-call(s32[3]{0:T(128)S(1)} %pad_add_fusion.where_ref, f32[8,128]{1,0:T(8,128)S(1)} %add.19.refs_0_, bf16[208,256]{1,0:T(8,128)(2,1)S(1)} %get-tuple-element.9.refs_0_.refs_1_, bf16[208,256]{1,0:T(8,128)(2,1)S(1)} %collective-permute-done.refs_1_.refs_2_, ...), custom_call_target="tpu_custom_call" | custom-call | tf_op jit(solution)/shard_map/adjoint/pallas_call | solution.py:299
  (2 shorter events, 0.0 us)
Async XLA Ops:
  1.1 0.7 %copy-start = (s32[16,16]{1,0:T(8,128)S(1)}, s32[16,16]{1,0:T(8,128)}, u32[]{:S(2)}) copy-start(s32[16,16]{1,0:T(8,128)} %blocks_ref.1) | copy-start | bytes 3076
  1.8 0.7 %copy-start.1 = (s32[512]{0:T(512)S(1)}, s32[512]{0:T(512)}, u32[]{:S(2)}) copy-start(s32[512]{0:T(512)} %param.11) | copy-start | bytes 6148
  2.5 0.7 %copy-start.2 = (s32[16]{0:T(128)S(1)}, s32[16]{0:T(128)}, u32[]{:S(2)}) copy-start(s32[16]{0:T(128)} %param.9) | copy-start | bytes 196
  3.2 0.7 %copy-start.3 = (f32[16]{0:T(128)S(1)}, f32[16]{0:T(128)}, u32[]{:S(2)}) copy-start(f32[16]{0:T(128)} %param.10) | copy-start | bytes 196
  5.5 11.0 %collective-permute-start = (bf16[208,256]{1,0:T(8,128)(2,1)S(1)}, bf16[208,256]{1,0:T(8,128)(2,1)S(1)}, u32[]{:S(2)}, u32[]{:S(2)}) collective-permute-start(bf16[208,256]{1,0:T(8,128)(2,1)S(1)} %get-tuple-element.10), channel_id=1, source_target_pairs={{0,4},{4,8},{8,12},{12,0},{1,5},{5,9},{9,13},{13,1},{2,6},{6,10},{... | collective-permute-start | bytes 319496 | tf_op jit(solution)/shard_map/ppermute | solution.py:317
  8.5 9.7 %collective-permute-start.1 = (bf16[208,256]{1,0:T(8,128)(2,1)S(1)}, bf16[208,256]{1,0:T(8,128)(2,1)S(1)}, u32[]{:S(2)}, u32[]{:S(2)}) collective-permute-start(bf16[208,256]{1,0:T(8,128)(2,1)S(1)} %get-tuple-element.11), channel_id=1, source_target_pairs={{0,8},{4,12},{8,0},{12,4},{1,9},{5,13},{9,1},{13,5},{2,10},{6,14},... | collective-permute-start | bytes 319496 | tf_op jit(solution)/shard_map/ppermute | solution.py:317
  11.1 7.1 %collective-permute-start.2 = (bf16[208,256]{1,0:T(8,128)(2,1)S(1)}, bf16[208,256]{1,0:T(8,128)(2,1)S(1)}, u32[]{:S(2)}, u32[]{:S(2)}) collective-permute-start(bf16[208,256]{1,0:T(8,128)(2,1)S(1)} %get-tuple-element.12), channel_id=1, source_target_pairs={{0,12},{4,0},{8,4},{12,8},{1,13},{5,1},{9,5},{13,9},{2,14},{6,2},{... | collective-permute-start | bytes 319496 | tf_op jit(solution)/shard_map/ppermute | solution.py:317
  22.0 6.7 %collective-permute-start.3 = (f32[8,128]{1,0:T(8,128)S(1)}, f32[8,128]{1,0:T(8,128)S(1)}, u32[]{:S(2)}, u32[]{:S(2)}) collective-permute-start(f32[8,128]{1,0:T(8,128)S(1)} %forward.1), channel_id=1, source_target_pairs={{0,4},{4,8},{8,12},{12,0},{1,5},{5,9},{9,13},{13,1},{2,6},{6,10},{... | collective-permute-start | bytes 12296 | tf_op jit(solution)/shard_map/ppermute | solution.py:317
  24.7 4.5 %collective-permute-start.4 = (f32[8,128]{1,0:T(8,128)S(1)}, f32[8,128]{1,0:T(8,128)S(1)}, u32[]{:S(2)}, u32[]{:S(2)}) collective-permute-start(f32[8,128]{1,0:T(8,128)S(1)} %forward.1), channel_id=1, source_target_pairs={{0,8},{4,12},{8,0},{12,4},{1,9},{5,13},{9,1},{13,5},{2,10},{6,14},... | collective-permute-start | bytes 12296 | tf_op jit(solution)/shard_map/ppermute | solution.py:317
  26.3 3.6 %collective-permute-start.5 = (f32[8,128]{1,0:T(8,128)S(1)}, f32[8,128]{1,0:T(8,128)S(1)}, u32[]{:S(2)}, u32[]{:S(2)}) collective-permute-start(f32[8,128]{1,0:T(8,128)S(1)} %forward.1), channel_id=1, source_target_pairs={{0,12},{4,0},{8,4},{12,8},{1,13},{5,1},{9,5},{13,9},{2,14},{6,2},{... | collective-permute-start | bytes 12296 | tf_op jit(solution)/shard_map/ppermute | solution.py:317
  27.1 7.5 %collective-permute-start.12 = (bf16[208,256]{1,0:T(8,128)(2,1)S(1)}, bf16[208,256]{1,0:T(8,128)(2,1)S(1)}, u32[]{:S(2)}, u32[]{:S(2)}) collective-permute-start(bf16[208,256]{1,0:T(8,128)(2,1)S(1)} %get-tuple-element.9.refs_0_.refs_1_), channel_id=1, source_target_pairs={{0,2},{2,0},{1,3},{3,1},{4,6},{6,4},{5,7},{7,5},{8,10},{10,8},{9,1... | collective-permute-start | bytes 319496 | tf_op jit(solution)/shard_map/ppermute | solution.py:317
  28.6 6.6 %collective-permute-start.7 = (bf16[208,256]{1,0:T(8,128)(2,1)S(1)}, bf16[208,256]{1,0:T(8,128)(2,1)S(1)}, u32[]{:S(2)}, u32[]{:S(2)}) collective-permute-start(bf16[208,256]{1,0:T(8,128)(2,1)S(1)} %get-tuple-element.9.refs_0_.refs_1_), channel_id=1, source_target_pairs={{0,1},{1,0},{2,3},{3,2},{4,5},{5,4},{6,7},{7,6},{8,9},{9,8},{10,11... | collective-permute-start | bytes 319496 | tf_op jit(solution)/shard_map/ppermute | solution.py:317
  29.9 1.2 %collective-permute-start.6 = (f32[8,128]{1,0:T(8,128)S(1)}, f32[8,128]{1,0:T(8,128)S(1)}, u32[]{:S(2)}, u32[]{:S(2)}) collective-permute-start(f32[8,128]{1,0:T(8,128)S(1)} %add_add_fusion), channel_id=1, source_target_pairs={{0,1},{1,0},{2,3},{3,2},{4,5},{5,4},{6,7},{7,6},{8,9},{9,8},{10,11... | collective-permute-start | bytes 12296 | tf_op jit(solution)/shard_map/ppermute | solution.py:317
  31.1 4.1 %collective-permute-start.11 = (f32[8,128]{1,0:T(8,128)S(1)}, f32[8,128]{1,0:T(8,128)S(1)}, u32[]{:S(2)}, u32[]{:S(2)}) collective-permute-start(f32[8,128]{1,0:T(8,128)S(1)} %add.19.refs_0_), channel_id=1, source_target_pairs={{0,2},{2,0},{1,3},{3,1},{4,6},{6,4},{5,7},{7,5},{8,10},{10,8},{9,1... | collective-permute-start | bytes 12296 | tf_op jit(solution)/shard_map/ppermute | solution.py:317
  32.6 5.9 %collective-permute-start.13 = (bf16[208,256]{1,0:T(8,128)(2,1)S(1)}, bf16[208,256]{1,0:T(8,128)(2,1)S(1)}, u32[]{:S(2)}, u32[]{:S(2)}) collective-permute-start(bf16[208,256]{1,0:T(8,128)(2,1)S(1)} %collective-permute-done.refs_1_.refs_2_), channel_id=1, source_target_pairs={{0,2},{2,0},{1,3},{3,1},{4,6},{6,4},{5,7},{7,5},{8,10},{10,8},{9,1... | collective-permute-start | bytes 319496 | tf_op jit(solution)/shard_map/ppermute | solution.py:317
  33.1 7.6 %collective-permute-start.14 = (bf16[208,256]{1,0:T(8,128)(2,1)S(1)}, bf16[208,256]{1,0:T(8,128)(2,1)S(1)}, u32[]{:S(2)}, u32[]{:S(2)}) collective-permute-start(bf16[208,256]{1,0:T(8,128)(2,1)S(1)} %collective-permute-done.1.refs_2_.refs_3_), channel_id=1, source_target_pairs={{0,2},{2,0},{1,3},{3,1},{4,6},{6,4},{5,7},{7,5},{8,10},{10,8},{9,1... | collective-permute-start | bytes 319496 | tf_op jit(solution)/shard_map/ppermute | solution.py:317
  34.6 7.3 %collective-permute-start.15 = (bf16[208,256]{1,0:T(8,128)(2,1)S(1)}, bf16[208,256]{1,0:T(8,128)(2,1)S(1)}, u32[]{:S(2)}, u32[]{:S(2)}) collective-permute-start(bf16[208,256]{1,0:T(8,128)(2,1)S(1)} %collective-permute-done.2.refs_3_.refs_4_), channel_id=1, source_target_pairs={{0,2},{2,0},{1,3},{3,1},{4,6},{6,4},{5,7},{7,5},{8,10},{10,8},{9,1... | collective-permute-start | bytes 319496 | tf_op jit(solution)/shard_map/ppermute | solution.py:317
  35.2 6.8 %collective-permute-start.16 = (bf16[208,256]{1,0:T(8,128)(2,1)S(1)}, bf16[208,256]{1,0:T(8,128)(2,1)S(1)}, u32[]{:S(2)}, u32[]{:S(2)}) collective-permute-start(bf16[208,256]{1,0:T(8,128)(2,1)S(1)} %collective-permute-done.12.refs_10_), channel_id=1, source_target_pairs={{0,1},{1,0},{2,3},{3,2},{4,5},{5,4},{6,7},{7,6},{8,9},{9,8},{10,11... | collective-permute-start | bytes 319496 | tf_op jit(solution)/shard_map/ppermute | solution.py:317
  35.2 7.3 %collective-permute-start.10 = (bf16[208,256]{1,0:T(8,128)(2,1)S(1)}, bf16[208,256]{1,0:T(8,128)(2,1)S(1)}, u32[]{:S(2)}, u32[]{:S(2)}) collective-permute-start(bf16[208,256]{1,0:T(8,128)(2,1)S(1)} %collective-permute-done.2.refs_3_.refs_4_), channel_id=1, source_target_pairs={{0,1},{1,0},{2,3},{3,2},{4,5},{5,4},{6,7},{7,6},{8,9},{9,8},{10,11... | collective-permute-start | bytes 319496 | tf_op jit(solution)/shard_map/ppermute | solution.py:317
  38.4 4.1 %collective-permute-start.8 = (bf16[208,256]{1,0:T(8,128)(2,1)S(1)}, bf16[208,256]{1,0:T(8,128)(2,1)S(1)}, u32[]{:S(2)}, u32[]{:S(2)}) collective-permute-start(bf16[208,256]{1,0:T(8,128)(2,1)S(1)} %collective-permute-done.refs_1_.refs_2_), channel_id=1, source_target_pairs={{0,1},{1,0},{2,3},{3,2},{4,5},{5,4},{6,7},{7,6},{8,9},{9,8},{10,11... | collective-permute-start | bytes 319496 | tf_op jit(solution)/shard_map/ppermute | solution.py:317
  40.7 1.8 %collective-permute-start.9 = (bf16[208,256]{1,0:T(8,128)(2,1)S(1)}, bf16[208,256]{1,0:T(8,128)(2,1)S(1)}, u32[]{:S(2)}, u32[]{:S(2)}) collective-permute-start(bf16[208,256]{1,0:T(8,128)(2,1)S(1)} %collective-permute-done.1.refs_2_.refs_3_), channel_id=1, source_target_pairs={{0,1},{1,0},{2,3},{3,2},{4,5},{5,4},{6,7},{7,6},{8,9},{9,8},{10,11... | collective-permute-start | bytes 319496 | tf_op jit(solution)/shard_map/ppermute | solution.py:317
  41.9 1.3 %collective-permute-start.17 = (bf16[208,256]{1,0:T(8,128)(2,1)S(1)}, bf16[208,256]{1,0:T(8,128)(2,1)S(1)}, u32[]{:S(2)}, u32[]{:S(2)}) collective-permute-start(bf16[208,256]{1,0:T(8,128)(2,1)S(1)} %collective-permute-done.13.refs_11_), channel_id=1, source_target_pairs={{0,1},{1,0},{2,3},{3,2},{4,5},{5,4},{6,7},{7,6},{8,9},{9,8},{10,11... | collective-permute-start | bytes 319496 | tf_op jit(solution)/shard_map/ppermute | solution.py:317
  41.9 1.5 %collective-permute-start.18 = (bf16[208,256]{1,0:T(8,128)(2,1)S(1)}, bf16[208,256]{1,0:T(8,128)(2,1)S(1)}, u32[]{:S(2)}, u32[]{:S(2)}) collective-permute-start(bf16[208,256]{1,0:T(8,128)(2,1)S(1)} %collective-permute-done.14.refs_12_), channel_id=1, source_target_pairs={{0,1},{1,0},{2,3},{3,2},{4,5},{5,4},{6,7},{7,6},{8,9},{9,8},{10,11... | collective-permute-start | bytes 319496 | tf_op jit(solution)/shard_map/ppermute | solution.py:317
  42.4 1.3 %collective-permute-start.19 = (bf16[208,256]{1,0:T(8,128)(2,1)S(1)}, bf16[208,256]{1,0:T(8,128)(2,1)S(1)}, u32[]{:S(2)}, u32[]{:S(2)}) collective-permute-start(bf16[208,256]{1,0:T(8,128)(2,1)S(1)} %collective-permute-done.15.refs_13_), channel_id=1, source_target_pairs={{0,1},{1,0},{2,3},{3,2},{4,5},{5,4},{6,7},{7,6},{8,9},{9,8},{10,11... | collective-permute-start | bytes 319496 | tf_op jit(solution)/shard_map/ppermute | solution.py:317

commit v2 on v1

v2 whole, which is shorter than its diff:
```python
import functools

import jax
import jax.numpy as jnp
from jax import lax
from jax.experimental import pallas as pl
from jax.experimental.pallas import tpu as pltpu
from jax.sharding import PartitionSpec as P

F32 = jnp.float32
BF16 = jnp.bfloat16
I32 = jnp.int32
META = 16
VMEM_LIMIT = 48 * 1024 * 1024


def up(x, m):
    return (x + m - 1) // m * m


def log2(x):
    assert x & (x - 1) == 0
    return x.bit_length() - 1


def iota(shape, axis):
    return lax.broadcasted_iota(I32, shape, axis)


def mask(cond):
    return jnp.where(cond, jnp.float32(1), jnp.float32(0))


def nt(a, b):
    return lax.dot_general(a, b, (((1,), (1,)), ((), ())), preferred_element_type=F32)


def nn(a, b):
    return lax.dot_general(a, b, (((1,), (0,)), ((), ())), preferred_element_type=F32)


def pack_kernel(cfg, where_ref, blocks_hbm, hour_hbm, weight_hbm, place_hbm, fp_ref, *refs):
    n, capp, local_blocks, slots, w2 = cfg["n"], cfg["capp"], cfg["local"], cfg["slots"], cfg["w2"]
    outs, (blocks_ref, hour_ref, weight_ref, place_ref, sems) = refs[:n], refs[n:]
    pairs = ((blocks_hbm, blocks_ref), (place_hbm, place_ref), (hour_hbm, hour_ref), (weight_hbm, weight_ref))
    copies = [pltpu.make_async_copy(src, dst, sems.at[i]) for i, (src, dst) in enumerate(pairs)]
    for copy in copies:
        copy.start()
    receptors = blocks_ref.shape[0]
    cols = receptors * slots * w2
    ids = place_ref.shape[1]
    used = n * capp
    padded = up(used, 256)
    half = n // 2
    me = where_ref[0]
    tm = where_ref[1]
    lane = iota((1, cols), 1)
    entry = lane >> log2(w2)
    w_of = lane & (w2 - 1)
    s_of = entry & (slots - 1)
    r_of = entry >> log2(slots)
    sel_s = mask(iota((slots, cols), 0) == s_of).astype(BF16)
    sel_r = mask(iota((receptors, cols), 0) == r_of).astype(BF16)
    before = ((iota((cols, cols), 0) >> log2(w2)) < entry) & ((iota((cols, cols), 0) & (w2 - 1)) == 0)
    before = mask(before).astype(BF16)
    for copy in copies:
        copy.wait()
    b = blocks_ref[...]
    high = (b >> 6).astype(F32).astype(BF16)
    low = (b & 63).astype(F32).astype(BF16)
    spread = nn(high, sel_s) * 64.0 + nn(low, sel_s)
    on_row = iota((receptors, cols), 0) == r_of
    geo = jnp.sum(jnp.where(on_row, spread, 0.0), axis=0, keepdims=True).astype(I32)
    place = place_ref[...]
    row16 = iota((16, ids), 0)
    owner_tab = (place >> log2(local_blocks)).astype(F32)
    local_tab = (place & (local_blocks - 1)).astype(F32)
    tab = jnp.where(row16 == 0, owner_tab, jnp.where(row16 == 1, local_tab, 0.0)).astype(BF16)
    found = nn(tab, mask(iota((ids, cols), 0) == geo).astype(BF16))
    step = found[0:1].astype(I32) - me
    step = jnp.where(step < 0, step + n, step)
    local_row = found[1:2]
    to_owner = iota((up(n, 16), cols), 0) == step
    ranks = nn(mask(to_owner).astype(BF16), before)
    rank = jnp.sum(jnp.where(to_owner, ranks, 0.0), axis=0, keepdims=True).astype(I32)
    slot = step * capp + rank
    weight = weight_ref[...]
    w_hi = weight.astype(BF16).astype(F32)
    w_mid = (weight - w_hi).astype(BF16).astype(F32)
    w_lo = weight - w_hi - w_mid
    row_r = iota((16, receptors), 0)
    per_r = jnp.where(row_r == 1, hour_ref[...].astype(F32), 0.0)
    per_r = jnp.where(row_r == 3, w_hi, per_r)
    per_r = jnp.where(row_r == 4, w_mid, per_r)
    per_r = jnp.where(row_r == 5, w_lo, per_r)
    values = nn(per_r.astype(BF16), sel_r)
    row_m = iota((16, cols), 0)
    values = jnp.where(row_m == 0, local_row + 1.0, values)
    values = jnp.where(row_m == 1, values + (tm * w2).astype(F32), values)
    values = jnp.where(row_m == 2, (r_of + me * receptors).astype(F32), values)
    fp = fp_ref[...]
    for w in range(w2):
        slot_w = jnp.where(w_of == w, slot, -1)
        pick = mask(iota((padded, cols), 0) == slot_w).astype(BF16)
        moved = nn(pick, fp).astype(BF16)
        for d in range(n):
            outs[d][w * capp : (w + 1) * capp, :] = moved[d * capp : (d + 1) * capp]
        if w == 0:
            meta = nt(values.astype(BF16), pick)
            at = iota((16, half * capp), 1)
            for d in range(n):
                base = d // half * half * capp
                place_d = d % half * capp
                mine = meta[:, base : base + half * capp]
                mine = jnp.where((at >= place_d) & (at < place_d + capp), mine, 0.0).astype(BF16)
                outs[d][w2 * capp : w2 * capp + META, :] = jnp.zeros((META, outs[d].shape[1]), BF16)
                outs[d][w2 * capp : w2 * capp + META, 0 : half * capp] = mine


def pack(cfg, where, blocks, hour_start, obs_weight, placement, footprint):
    n, capp, slots, w2 = cfg["n"], cfg["capp"], cfg["slots"], cfg["w2"]
    receptors = blocks.shape[0]
    cells = footprint.shape[3]
    rows = w2 * capp + META
    hour_start, obs_weight, placement = (
        hour_start.reshape(1, receptors), obs_weight.reshape(1, receptors), placement.reshape(1, -1),
    )
    vm = pl.BlockSpec(memory_space=pltpu.VMEM)
    return pl.pallas_call(
        functools.partial(pack_kernel, cfg),
        out_shape=[jax.ShapeDtypeStruct((rows, cells), BF16)] * n,
        in_specs=[pl.BlockSpec(memory_space=pltpu.SMEM)] + [pl.BlockSpec(memory_space=pltpu.HBM)] * 4 + [vm],
        out_specs=[vm] * n,
        scratch_shapes=[
            pltpu.VMEM(blocks.shape, I32),
            pltpu.VMEM(hour_start.shape, I32),
            pltpu.VMEM(obs_weight.shape, F32),
            pltpu.VMEM(placement.shape, I32),
            pltpu.SemaphoreType.DMA((4,)),
        ],
        compiler_params=pltpu.CompilerParams(vmem_limit_bytes=VMEM_LIMIT),
        name="pack",
    )(where, blocks, hour_start, obs_weight, placement, footprint.reshape(receptors * slots * w2, cells))


def slots_of(bufs, rows):
    return [(buf, base) for buf in bufs for base in range(0, buf.shape[0], rows)]


def load_meta(cfg, placed):
    w2, capp = cfg["w2"], cfg["capp"]
    total = None
    for buf, base in placed:
        part = buf[base + w2 * capp : base + w2 * capp + META, :].astype(F32)
        total = part if total is None else total + part
    return total[:, 0 : len(placed) * capp]


def hour_column(meta, width):
    pick = mask(iota((16, width), 0) == 1)
    return lax.dot_general(
        meta.astype(BF16), pick.astype(BF16), (((0,), (0,)), ((), ())), preferred_element_type=F32
    )


def spread_hours(cfg, sides, metas, f8_ref, base_row):
    w2, capp, hours, cells = cfg["w2"], cfg["capp"], cfg["hours"], cfg["cells"]
    columns = [hour_column(m, cells).astype(BF16) for m in metas]
    for d in range(len(sides[0])):
        parts = []
        for side in range(len(sides)):
            buf, base = sides[side][d]
            first = columns[side][d * capp : (d + 1) * capp]
            for w in range(w2):
                parts.append((first + BF16(w) if w else first, buf[base + w * capp : base + (w + 1) * capp, :]))
        for h in range(hours):
            value = jnp.zeros((capp, cells), BF16)
            for first, fp in parts:
                value = jnp.where(first == BF16(h), fp, value)
            f8_ref[base_row + d * capp : base_row + (d + 1) * capp, h * cells : (h + 1) * cells] = value


def forward_kernel(cfg, nbuf, *refs):
    bufs, (probes_ref, sofar_ref, out_ref, f8_ref) = refs[:nbuf], refs[nbuf:]
    local, k = cfg["local"], cfg["k"]
    placed = slots_of(bufs, cfg["rows"])
    meta = load_meta(cfg, placed)
    used = meta.shape[1]
    spread_hours(cfg, [placed], [meta], f8_ref, 0)
    own = iota((local, used), 0) + 1 == meta[0:1].astype(I32)
    row = iota((8, used), 0)
    dots = jnp.zeros((8, used), F32)
    f8 = f8_ref[...]
    for j in range(k):
        x = nt(probes_ref[j * local : (j + 1) * local, :], f8)
        y = jnp.sum(jnp.where(own, x, 0.0), axis=0, keepdims=True)
        dots = jnp.where(row == j, y, dots)
    to_r = mask(iota((out_ref.shape[1], used), 0) == meta[2:3].astype(I32))
    out_ref[...] = sofar_ref[...] + lax.dot_general(
        dots, to_r, (((1,), (1,)), ((), ())), precision=lax.Precision.HIGHEST, preferred_element_type=F32
    )


def forward(cfg, bufs, probes_t, sofar, name):
    n, capp, hours, cells = cfg["n"], cfg["capp"], cfg["hours"], cfg["cells"]
    used = n // 2 * capp
    vm = pl.BlockSpec(memory_space=pltpu.VMEM)
    return pl.pallas_call(
        functools.partial(forward_kernel, cfg, len(bufs)),
        out_shape=jax.ShapeDtypeStruct(sofar.shape, F32),
        in_specs=[vm] * (len(bufs) + 2),
        out_specs=vm,
        scratch_shapes=[pltpu.VMEM((used, hours * cells), BF16)],
        compiler_params=pltpu.CompilerParams(vmem_limit_bytes=VMEM_LIMIT),
        cost_estimate=pl.CostEstimate(
            flops=2 * used * probes_t.size, bytes_accessed=2 * probes_t.size, transcendentals=0
        ),
        name=name,
    )(*bufs, probes_t, sofar)


def prepare_kernel(cfg, counts, *refs):
    n, capp = cfg["n"], cfg["capp"]
    f8_ref, meta_ref, zero_ref = refs[-3:]
    zero_ref[...] = jnp.zeros_like(zero_ref)
    at = 0
    for c, halves in enumerate(counts):
        metas = []
        for i, sides_n in enumerate(halves):
            sides = []
            for count in sides_n:
                sides.append(slots_of(refs[at : at + count], cfg["rows"]))
                at += count
            side_metas = [load_meta(cfg, placed) for placed in sides]
            spread_hours(cfg, sides, side_metas, f8_ref, (2 * c + i) * (n // 2) * capp)
            metas.append(side_metas[0][0:8])
        meta_ref[:, c * n * capp : (c + 1) * n * capp] = jnp.concatenate(metas, axis=1)


def prepare(cfg, columns, zero_shape):
    n, capp, hours, cells = cfg["n"], cfg["capp"], cfg["hours"], cfg["cells"]
    total = len(columns) * n * capp
    args = [b for halves in columns for sides in halves for side in sides for b in side]
    counts = [[[len(side) for side in sides] for sides in halves] for halves in columns]
    vm = pl.BlockSpec(memory_space=pltpu.VMEM)
    return pl.pallas_call(
        functools.partial(prepare_kernel, cfg, counts),
        out_shape=[
            jax.ShapeDtypeStruct((total, hours * cells), BF16),
            jax.ShapeDtypeStruct((8, total), F32),
            jax.ShapeDtypeStruct(zero_shape, F32),
        ],
        in_specs=[vm] * len(args),
        out_specs=[vm] * 3,
        compiler_params=pltpu.CompilerParams(vmem_limit_bytes=VMEM_LIMIT),
        cost_estimate=pl.CostEstimate(flops=0, bytes_accessed=6 * total * hours * cells, transcendentals=0),
        name="prepare",
    )(*args)


def adjoint_kernel(cfg, parts, where_ref, meta_ref, f8_ref, *refs):
    n, capp, local, hours, cells, kd = (
        cfg["n"], cfg["capp"], cfg["local"], cfg["hours"], cfg["cells"], cfg["kd"],
    )
    obs_refs, (out_ref, a_ref, tiles_ref, sems) = refs[:-4], refs[-4:]
    used = n * capp
    per_k = cells // 128
    for c in range(len(obs_refs) // parts):
        obs = obs_refs[c * parts][...]
        for i in range(1, parts):
            obs = obs + obs_refs[c * parts + i][...]
        meta = meta_ref[:, c * used : (c + 1) * used]
        to_r = mask(iota((obs.shape[1], used), 0) == meta[2:3].astype(I32))
        per_entry = lax.dot_general(
            obs, to_r, (((1,), (0,)), ((), ())), precision=lax.Precision.HIGHEST, preferred_element_type=F32
        )
        per_entry = per_entry * (meta[3:4] + meta[4:5] + meta[5:6])
        own = iota((local, used), 0) + 1 == meta[0:1].astype(I32)
        row = iota((8, used), 0)
        for j in range(kd):
            term = jnp.sum(jnp.where(row == where_ref[2] * kd + j, per_entry, 0.0), axis=0, keepdims=True)
            high = term.astype(BF16).astype(F32)
            for p, part in enumerate((high, term - high)):
                a_ref[(2 * j + p) * local : (2 * j + p + 1) * local, c * used : (c + 1) * used] = jnp.where(
                    own, part, 0.0
                ).astype(BF16)
    copies = []
    for j in range(kd):
        a = a_ref[2 * j * local : 2 * (j + 1) * local, :]
        for h in range(hours):
            sums = nn(a, f8_ref[:, h * cells : (h + 1) * cells])
            both = sums[0:local] + sums[local : 2 * local]
            for t in range(per_k):
                tiles_ref.at[j * per_k + t][pl.ds(h, local, stride=hours), :] = both[:, t * 128 : (t + 1) * 128]
        for t in range(j * per_k, (j + 1) * per_k):
            copy = pltpu.make_async_copy(tiles_ref.at[t], out_ref.at[:, pl.ds(t * 128, 128)], sems.at[t])
            copy.start()
            copies.append(copy)
    for copy in copies:
        copy.wait()


def adjoint(cfg, where, f8, meta, observed):
    hours, cells, local, kd = cfg["hours"], cfg["cells"], cfg["local"], cfg["kd"]
    total = f8.shape[0]
    parts = len(observed[0])
    args = [o for column in observed for o in column]
    vm = pl.BlockSpec(memory_space=pltpu.VMEM)
    return pl.pallas_call(
        functools.partial(adjoint_kernel, cfg, parts),
        out_shape=jax.ShapeDtypeStruct((local * hours, kd * cells), F32),
        in_specs=[pl.BlockSpec(memory_space=pltpu.SMEM)] + [vm] * (2 + len(args)),
        out_specs=pl.BlockSpec(memory_space=pl.ANY),
        scratch_shapes=[
            pltpu.VMEM((2 * kd * local, total), BF16),
            pltpu.VMEM((kd * cells // 128, local * hours, 128), F32),
            pltpu.SemaphoreType.DMA((kd * cells // 128,)),
        ],
        compiler_params=pltpu.CompilerParams(vmem_limit_bytes=VMEM_LIMIT),
        name="adjoint",
    )(where, meta, f8, *args)


def shift(x, axis, d):
    n = lax.axis_size(axis)
    return lax.ppermute(x, axis, [(i, (i + d) % n) for i in range(n)])


def shift2(x, g, s):
    nreg, ntm = lax.axis_size("reg"), lax.axis_size("tm")
    pairs = [
        (r * ntm + t, (r + g) % nreg * ntm + (t + s) % ntm) for r in range(nreg) for t in range(ntm)
    ]
    return lax.ppermute(x, ("reg", "tm"), pairs)


def shards(probes, footprint, blocks, hour_start, obs_weight, placement):
    n, nreg, ntm = lax.axis_size("rcp"), lax.axis_size("reg"), lax.axis_size("tm")
    local, hours, width = probes.shape
    receptors, slots, w2, cells = footprint.shape
    k = width // cells
    capp = up(3 * receptors * slots // (2 * n), 16)
    cfg = dict(
        n=n, capp=capp, local=local, hours=hours, cells=cells, slots=slots, w2=w2, k=k,
        kd=k // (nreg * ntm), rows=w2 * capp + META,
    )
    z, reg, tm = lax.axis_index("rcp"), lax.axis_index("reg"), lax.axis_index("tm")
    where = jnp.stack([z, tm, reg * ntm + tm]).astype(I32)
    outs = pack(cfg, where, blocks, hour_start, obs_weight, placement, footprint)
    bufs = [outs[0]] + [shift(outs[d], "rcp", d) for d in range(1, n)]
    probes_t = probes.reshape(local, hours, k, cells).transpose(2, 0, 1, 3).reshape(k * local, hours * cells)
    halves = [bufs[: n // 2], bufs[n // 2 :]]
    if n > 4:
        halves = [[jnp.concatenate(half, axis=0)] for half in halves]
    partial = jnp.zeros((8, up(n * receptors, 128)), F32)
    for i, half in enumerate(halves):
        partial = forward(cfg, half, probes_t, partial, f"forward{i}")
    columns = [[[half] + [[shift(b, "tm", s) for b in half] for s in range(1, ntm)] for half in halves]]
    for g in range(1, nreg):
        across = [[shift(b, "reg", g) for b in half] for half in halves]
        columns.append([[half] + [[shift(b, "tm", s) for b in half] for s in range(1, ntm)] for half in across])
    f8, meta, zero = prepare(cfg, columns, partial.shape)
    observed = partial + zero
    for d in range(1, n):
        observed = observed + shift(partial, "rcp", d)
    observed = [[shift2(observed, g, s) if g or s else observed for s in range(ntm)] for g in range(nreg)]
    result = adjoint(cfg, where, f8, meta, observed)
    return result.reshape(local, hours, cfg["kd"] * cells)


def solution(mesh):
    return jax.shard_map(
        shards,
        mesh=mesh,
        in_specs=(
            P(("inv", "rcp"), None, None),
            P(("inv", "rcp", "reg"), None, "tm", None),
            P(("inv", "rcp", "reg"), None),
            P(("inv", "rcp", "reg")),
            P(("inv", "rcp", "reg")),
            P("inv"),
        ),
        out_specs=P(("inv", "rcp"), None, ("reg", "tm")),
        check_vma=False,
    )
```

time: 49.1 us -> 47.7 us (0.971)
  waiting for transfers between devices: 11.8 us -> 5.97 us
  starting transfers between devices: 18.8 us -> 21.9 us
  Pallas kernels: 10.4 us -> 11.7 us
    ppermute x20 -> x18, waiting for transfers between devices: 11.8 us -> 3.25 us  [shift(): return lax.ppermute(x, axis, [(i, (i + d) % n) for i in range(n)])]
    ppermute x0 -> x3, waiting for transfers between devices: none -> 2.72 us  [shift2(): return lax.ppermute(x, ('reg', 'tm'), pairs)]
    ppermute x0 -> x3, starting transfers between devices: none -> 1.86 us  [shift2(): return lax.ppermute(x, ('reg', 'tm'), pairs)]
    pallas_call x1 -> x2, Pallas kernels: 3.73 us -> 5.11 us  [forward(): pl.pallas_call(functools.partial(forward_kernel, cfg, len(bufs)), out_sha...]
    ppermute x20 -> x18, starting transfers between devices: 18.8 us -> 20 us  [shift(): return lax.ppermute(x, axis, [(i, (i + d) % n) for i in range(n)])]
    pallas_call x1 -> x2, Pallas kernels: 5.1 us -> 4.94 us  [the longest x1 3.73 us: adjoint(): pl.pallas_call(functools.partial(adjoint_kernel, cfg, parts), out_shape=j...]
  transfers between devices with their start and end apart: 20 -> 21, of which waited for: 10 -> 5; matrix products, arithmetic and copies ran while one was open for 8% -> 8% of each run, Pallas kernels for 0% -> 13%
where the time goes in v2:
time: 47.7 us; the launch traced here: 47.4 us
  starting transfers between devices  21.9 us (46%)
  Pallas kernels  11.7 us (25%)
  local copies, waits for them, and re-layouts  7.69 us (16%)
  waiting for transfers between devices  5.97 us (13%)
    ppermute x18, starting transfers between devices, shift(): return lax.ppermute(x, axis, [(i, (i + d) % n) for i in range(n)])  20 us
    pallas_call x2, Pallas kernels, forward(): pl.pallas_call(functools.partial(forward_kernel, cfg, len(bufs)), out_sha...  5.11 us
    unnamed x9, local copies, waits for them, and re-layouts  4.18 us
    pallas_call x1, Pallas kernels, adjoint(): pl.pallas_call(functools.partial(adjoint_kernel, cfg, parts), out_shape=j...  3.73 us
    ppermute x18, waiting for transfers between devices, shift(): return lax.ppermute(x, axis, [(i, (i + d) % n) for i in range(n)])  3.25 us
    ppermute x3, waiting for transfers between devices, shift2(): return lax.ppermute(x, ('reg', 'tm'), pairs)  2.72 us
    reshape x1, local copies, waits for them, and re-layouts, shards(): probes.reshape(local, hours, k, cells).transpose(2, 0, 1, 3)  2.46 us
    ppermute x3, starting transfers between devices, shift2(): return lax.ppermute(x, ('reg', 'tm'), pairs)  1.86 us
  transfers between devices with their start and end apart: 21, of which 5 were waited for; matrix products, arithmetic and copies ran while one was open for 8% of the time, Pallas kernels for 13%

profile of v2, /device:TPU:0, one launch (start us, length us, event | category | flops | bytes accessed | tf_op | source)
XLA Modules:
  0.0 47.4 jit_solution(4365236608914419691)
XLA Ops:
  0.0 1.1 %reshape.24.fp_ref = bf16[512,256]{1,0:T(8,128)(2,1)S(1)} reshape(bf16[16,16,2,256]{3,2,1,0:T(2,128)(2,1)} %param.7) | data formatting | bytes 524288 | tf_op jit(solution)/shard_map/reshape | solution.py:143
  1.1 0.1 pad_add_fusion.where_ref
  1.1 0.0 copy-start
  1.1 0.7 %copy-done = s32[16,16]{1,0:T(8,128)S(1)} copy-done((s32[16,16]{1,0:T(8,128)S(1)}, s32[16,16]{1,0:T(8,128)}, u32[]{:S(2)}) %copy-start) | copy-done | bytes 1048
  1.8 0.0 copy-start.1
  1.8 0.7 %copy-done.1 = s32[512]{0:T(512)S(1)} copy-done((s32[512]{0:T(512)S(1)}, s32[512]{0:T(512)}, u32[]{:S(2)}) %copy-start.1) | copy-done | bytes 2072
  2.5 0.0 copy-start.2
  2.5 0.7 %copy-done.2 = s32[16]{0:T(128)S(1)} copy-done((s32[16]{0:T(128)S(1)}, s32[16]{0:T(128)}, u32[]{:S(2)}) %copy-start.2) | copy-done | bytes 88
  3.2 0.0 copy-start.3
  3.2 0.7 %copy-done.3 = f32[16]{0:T(128)S(1)} copy-done((f32[16]{0:T(128)S(1)}, f32[16]{0:T(128)}, u32[]{:S(2)}) %copy-start.3) | copy-done | bytes 88
  3.8 1.7 %pack.1 = (bf16[208,256]{1,0:T(8,128)(2,1)S(1)}, bf16[208,256]{1,0:T(8,128)(2,1)S(1)}, bf16[208,256]{1,0:T(8,128)(2,1)S(1)}, bf16[208,256]{1,0:T(8,128)(2,1)S(1)}) custom-call(s32[3]{0:T(128)S(1)} %pad_add_fusion.where_ref, s32[16,16]{1,0:T(8,128)S(1)} %copy-done, s32[1,16]{1,0:T(1,128)S(1)} %bitcast.15, f32[1,16]{1,0:T(1,128)S(1)} %bitcast.16, ...), custom_call_target="tpu_custom_call" | custom-call | tf_op jit(solution)/shard_map/pack/pallas_call | solution.py:129
  5.5 3.1 %collective-permute-start = (bf16[208,256]{1,0:T(8,128)(2,1)S(1)}, bf16[208,256]{1,0:T(8,128)(2,1)S(1)}, u32[]{:S(2)}, u32[]{:S(2)}) collective-permute-start(bf16[208,256]{1,0:T(8,128)(2,1)S(1)} %get-tuple-element.13), channel_id=1, source_target_pairs={{0,4},{4,8},{8,12},{12,0},{1,5},{5,9},{9,13},{13,1},{2,6},{6,10},{... | collective-permute-start | bytes 319496 | tf_op jit(solution)/shard_map/ppermute | solution.py:326
  8.6 2.6 %collective-permute-start.3 = (bf16[208,256]{1,0:T(8,128)(2,1)S(1)}, bf16[208,256]{1,0:T(8,128)(2,1)S(1)}, u32[]{:S(2)}, u32[]{:S(2)}) collective-permute-start(bf16[208,256]{1,0:T(8,128)(2,1)S(1)} %get-tuple-element.14), channel_id=1, source_target_pairs={{0,8},{4,12},{8,0},{12,4},{1,9},{5,13},{9,1},{13,5},{2,10},{6,14},... | collective-permute-start | bytes 319496 | tf_op jit(solution)/shard_map/ppermute | solution.py:326
  11.2 1.3 %collective-permute-start.4 = (bf16[208,256]{1,0:T(8,128)(2,1)S(1)}, bf16[208,256]{1,0:T(8,128)(2,1)S(1)}, u32[]{:S(2)}, u32[]{:S(2)}) collective-permute-start(bf16[208,256]{1,0:T(8,128)(2,1)S(1)} %get-tuple-element.15), channel_id=1, source_target_pairs={{0,12},{4,0},{8,4},{12,8},{1,13},{5,1},{9,5},{13,9},{2,14},{6,2},{... | collective-permute-start | bytes 319496 | tf_op jit(solution)/shard_map/ppermute | solution.py:326
  12.6 1.5 %collective-permute-start.7 = (bf16[208,256]{1,0:T(8,128)(2,1)S(1)}, bf16[208,256]{1,0:T(8,128)(2,1)S(1)}, u32[]{:S(2)}, u32[]{:S(2)}) collective-permute-start(bf16[208,256]{1,0:T(8,128)(2,1)S(1)} %get-tuple-element.12.refs_0_), channel_id=1, source_target_pairs={{0,2},{2,0},{1,3},{3,1},{4,6},{6,4},{5,7},{7,5},{8,10},{10,8},{9,1... | collective-permute-start | bytes 319496 | tf_op jit(solution)/shard_map/ppermute | solution.py:326
  14.0 0.0 collective-permute-start.1
  14.0 0.5 %collective-permute-done.refs_1_ = bf16[208,256]{1,0:T(8,128)(2,1)S(1)} collective-permute-done((bf16[208,256]{1,0:T(8,128)(2,1)S(1)}, bf16[208,256]{1,0:T(8,128)(2,1)S(1)}, u32[]{:S(2)}, u32[]{:S(2)}) %collective-permute-start) | collective-permute-done | bytes 106528 | tf_op jit(solution)/shard_map/ppermute | solution.py:326
  14.5 1.6 %collective-permute-start.8 = (bf16[208,256]{1,0:T(8,128)(2,1)S(1)}, bf16[208,256]{1,0:T(8,128)(2,1)S(1)}, u32[]{:S(2)}, u32[]{:S(2)}) collective-permute-start(bf16[208,256]{1,0:T(8,128)(2,1)S(1)} %collective-permute-done.refs_1_), channel_id=1, source_target_pairs={{0,2},{2,0},{1,3},{3,1},{4,6},{6,4},{5,7},{7,5},{8,10},{10,8},{9,1... | collective-permute-start | bytes 319496 | tf_op jit(solution)/shard_map/ppermute | solution.py:326
  16.1 2.2 %collective-permute-done.3.refs_4_.refs_0_ = bf16[208,256]{1,0:T(8,128)(2,1)S(1)} collective-permute-done((bf16[208,256]{1,0:T(8,128)(2,1)S(1)}, bf16[208,256]{1,0:T(8,128)(2,1)S(1)}, u32[]{:S(2)}, u32[]{:S(2)}) %collective-permute-start.3) | collective-permute-done | bytes 106528 | tf_op jit(solution)/shard_map/ppermute | solution.py:326
  18.3 1.5 %collective-permute-start.11 = (bf16[208,256]{1,0:T(8,128)(2,1)S(1)}, bf16[208,256]{1,0:T(8,128)(2,1)S(1)}, u32[]{:S(2)}, u32[]{:S(2)}) collective-permute-start(bf16[208,256]{1,0:T(8,128)(2,1)S(1)} %collective-permute-done.3.refs_4_.refs_0_), channel_id=1, source_target_pairs={{0,2},{2,0},{1,3},{3,1},{4,6},{6,4},{5,7},{7,5},{8,10},{10,8},{9,1... | collective-permute-start | bytes 319496 | tf_op jit(solution)/shard_map/ppermute | solution.py:326
  19.8 0.0 collective-permute-done.4.refs_5_.refs_1_
  19.8 0.5 %collective-permute-start.12 = (bf16[208,256]{1,0:T(8,128)(2,1)S(1)}, bf16[208,256]{1,0:T(8,128)(2,1)S(1)}, u32[]{:S(2)}, u32[]{:S(2)}) collective-permute-start(bf16[208,256]{1,0:T(8,128)(2,1)S(1)} %collective-permute-done.4.refs_5_.refs_1_), channel_id=1, source_target_pairs={{0,2},{2,0},{1,3},{3,1},{4,6},{6,4},{5,7},{7,5},{8,10},{10,8},{9,1... | collective-permute-start | bytes 319496 | tf_op jit(solution)/shard_map/ppermute | solution.py:326
  20.3 0.0 collective-permute-done.7.refs_8_
  20.3 0.0 collective-permute-start.9
  20.3 0.0 collective-permute-done.1.refs_2_
  20.4 0.5 %collective-permute-start.2 = (bf16[208,256]{1,0:T(8,128)(2,1)S(1)}, bf16[208,256]{1,0:T(8,128)(2,1)S(1)}, u32[]{:S(2)}, u32[]{:S(2)}) collective-permute-start(bf16[208,256]{1,0:T(8,128)(2,1)S(1)} %collective-permute-done.refs_1_), channel_id=1, source_target_pairs={{0,1},{1,0},{2,3},{3,2},{4,5},{5,4},{6,7},{7,6},{8,9},{9,8},{10,11... | collective-permute-start | bytes 319496 | tf_op jit(solution)/shard_map/ppermute | solution.py:326
  20.9 2.5 %copy.7 = bf16[128,8,8,256]{3,1,0,2:T(8,128)(2,1)S(1)} copy(bf16[128,8,8,256]{3,1,2,0:T(8,128)(2,1)} %bitcast.18) | data formatting | bytes 8388608 | tf_op jit(solution)/shard_map/reshape | solution.py:351
  23.3 1.5 %copy.8 = bf16[128,8,8,256]{3,1,2,0:T(8,128)(2,1)S(1)} copy(bf16[128,8,8,256]{3,2,1,0:T(8,128)(2,1)S(1)} %bitcast.17) | data formatting | bytes 8388608
  24.8 0.0 collective-permute-done.8.refs_9_
  24.8 0.1 collective-permute-start.5
  25.0 0.0 collective-permute-done.11.refs_12_
  25.0 0.4 collective-permute-start.6
  25.4 0.0 collective-permute-done.12.refs_13_
  25.4 0.1 collective-permute-start.10
  25.5 0.0 collective-permute-done.9.refs_10_
  25.5 0.4 collective-permute-start.13
  25.9 0.0 collective-permute-done.2.refs_3_
  25.9 0.1 collective-permute-start.14
  26.0 2.5 %forward0.1.refs_3_ = f32[8,128]{1,0:T(8,128)S(1)} custom-call(bf16[208,256]{1,0:T(8,128)(2,1)S(1)} %get-tuple-element.12.refs_0_, bf16[208,256]{1,0:T(8,128)(2,1)S(1)} %collective-permute-done.refs_1_, bf16[1024,2048]{1,0:T(8,128)(2,1)S(1)} %bitcast.12, f32[8,128]{1,0:T(8,128)S(1)} %broadcast_in_dim.3.refs_3_), custom_call_target="tpu_custom_call" | custom-call | flops 805306368 | bytes 4194304 | tf_op jit(solution)/shard_map/forward0/pallas_call | solution.py:208
  28.5 2.6 %forward1.1 = f32[8,128]{1,0:T(8,128)S(1)} custom-call(bf16[208,256]{1,0:T(8,128)(2,1)S(1)} %collective-permute-done.3.refs_4_.refs_0_, bf16[208,256]{1,0:T(8,128)(2,1)S(1)} %collective-permute-done.4.refs_5_.refs_1_, bf16[1024,2048]{1,0:T(8,128)(2,1)S(1)} %bitcast.13, f32[8,128]{1,0:T(8,128)S(1)} %forward0.1.refs_3_), custom_call_target="tpu_custom_call" | custom-call | flops 805306368 | bytes 4194304 | tf_op jit(solution)/shard_map/forward1/pallas_call | solution.py:208
  31.1 0.0 collective-permute-done.5.refs_6_
  31.1 2.3 %collective-permute-start.15 = (f32[8,128]{1,0:T(8,128)S(1)}, f32[8,128]{1,0:T(8,128)S(1)}, u32[]{:S(2)}, u32[]{:S(2)}) collective-permute-start(f32[8,128]{1,0:T(8,128)S(1)} %forward1.1), channel_id=1, source_target_pairs={{0,4},{4,8},{8,12},{12,0},{1,5},{5,9},{9,13},{13,1},{2,6},{6,10},{... | collective-permute-start | bytes 12296 | tf_op jit(solution)/shard_map/ppermute | solution.py:326
  33.4 0.0 collective-permute-done.6.refs_7_
  33.4 2.1 %collective-permute-start.16 = (f32[8,128]{1,0:T(8,128)S(1)}, f32[8,128]{1,0:T(8,128)S(1)}, u32[]{:S(2)}, u32[]{:S(2)}) collective-permute-start(f32[8,128]{1,0:T(8,128)S(1)} %forward1.1), channel_id=1, source_target_pairs={{0,8},{4,12},{8,0},{12,4},{1,9},{5,13},{9,1},{13,5},{2,10},{6,14},... | collective-permute-start | bytes 12296 | tf_op jit(solution)/shard_map/ppermute | solution.py:326
  35.5 0.0 collective-permute-done.10.refs_11_
  35.5 1.8 %collective-permute-start.17 = (f32[8,128]{1,0:T(8,128)S(1)}, f32[8,128]{1,0:T(8,128)S(1)}, u32[]{:S(2)}, u32[]{:S(2)}) collective-permute-start(f32[8,128]{1,0:T(8,128)S(1)} %forward1.1), channel_id=1, source_target_pairs={{0,12},{4,0},{8,4},{12,8},{1,13},{5,1},{9,5},{13,9},{2,14},{6,2},{... | collective-permute-start | bytes 12296 | tf_op jit(solution)/shard_map/ppermute | solution.py:326
  37.3 0.0 collective-permute-done.13.refs_14_
  37.3 0.0 collective-permute-done.14.refs_15_
  37.3 1.2 %prepare.1 = (bf16[768,2048]{1,0:T(8,128)(2,1)S(1)}, f32[8,768]{1,0:T(8,128)S(1)}, f32[8,128]{1,0:T(8,128)S(1)}) custom-call(bf16[208,256]{1,0:T(8,128)(2,1)S(1)} %get-tuple-element.12.refs_0_, bf16[208,256]{1,0:T(8,128)(2,1)S(1)} %collective-permute-done.refs_1_, bf16[208,256]{1,0:T(8,128)(2,1)S(1)} %collective-permute-done.1.refs_2_, ...), custom_call_target="tpu_custom_call" | custom-call | bytes 9437184 | tf_op jit(solution)/shard_map/prepare/pallas_call | solution.py:246
  38.6 0.0 collective-permute-done.15
  38.6 0.0 collective-permute-done.16
  38.6 0.5 %collective-permute-done.17 = f32[8,128]{1,0:T(8,128)S(1)} collective-permute-done((f32[8,128]{1,0:T(8,128)S(1)}, f32[8,128]{1,0:T(8,128)S(1)}, u32[]{:S(2)}, u32[]{:S(2)}) %collective-permute-start.17) | collective-permute-done | bytes 4128 | tf_op jit(solution)/shard_map/ppermute | solution.py:326
  39.1 0.0 collective-permute-start.18
  39.1 1.5 %collective-permute-start.19 = (f32[8,128]{1,0:T(8,128)S(1)}, f32[8,128]{1,0:T(8,128)S(1)}, u32[]{:S(2)}, u32[]{:S(2)}) collective-permute-start(f32[8,128]{1,0:T(8,128)S(1)} %add_add_fusion.refs_0_), channel_id=1, source_target_pairs={{0,2},{1,3},{2,0},{3,1},{4,6},{5,7},{6,4},{7,5},{8,10},{9,11},{10,... | collective-permute-start | bytes 12296 | tf_op jit(solution)/shard_map/ppermute | solution.py:334
  40.7 0.3 collective-permute-start.20
  41.0 0.0 collective-permute-done.18.refs_1_
  41.0 1.8 %collective-permute-done.19.refs_2_ = f32[8,128]{1,0:T(8,128)S(1)} collective-permute-done((f32[8,128]{1,0:T(8,128)S(1)}, f32[8,128]{1,0:T(8,128)S(1)}, u32[]{:S(2)}, u32[]{:S(2)}) %collective-permute-start.19) | collective-permute-done | bytes 4128 | tf_op jit(solution)/shard_map/ppermute | solution.py:334
  42.8 0.9 %collective-permute-done.20.refs_3_ = f32[8,128]{1,0:T(8,128)S(1)} collective-permute-done((f32[8,128]{1,0:T(8,128)S(1)}, f32[8,128]{1,0:T(8,128)S(1)}, u32[]{:S(2)}, u32[]{:S(2)}) %collective-permute-start.20) | collective-permute-done | bytes 4128 | tf_op jit(solution)/shard_map/ppermute | solution.py:334
  43.7 3.7 %adjoint.1 = f32[1024,512]{1,0:T(8,128)} custom-call(s32[3]{0:T(128)S(1)} %pad_add_fusion.where_ref, f32[8,768]{1,0:T(8,128)S(1)} %get-tuple-element.16.meta_ref, bf16[768,2048]{1,0:T(8,128)(2,1)S(1)} %get-tuple-element.17.f8_ref, f32[8,128]{1,0:T(8,128)S(1)} %add_add_fusion.refs_0_, f32[8,128]{1,0:T(8,128)S(1)} %collective-permute-done.18.refs_1_, ...), custom_call_target="tpu_custom_call" | custom-call | tf_op jit(solution)/shard_map/adjoint/pallas_call | solution.py:309
  (2 shorter events, 0.0 us)
Async XLA Ops:
  1.1 0.7 %copy-start = (s32[16,16]{1,0:T(8,128)S(1)}, s32[16,16]{1,0:T(8,128)}, u32[]{:S(2)}) copy-start(s32[16,16]{1,0:T(8,128)} %blocks_hbm.1) | copy-start | bytes 3076
  1.8 0.7 %copy-start.1 = (s32[512]{0:T(512)S(1)}, s32[512]{0:T(512)}, u32[]{:S(2)}) copy-start(s32[512]{0:T(512)} %param.11) | copy-start | bytes 6148
  2.5 0.7 %copy-start.2 = (s32[16]{0:T(128)S(1)}, s32[16]{0:T(128)}, u32[]{:S(2)}) copy-start(s32[16]{0:T(128)} %param.9) | copy-start | bytes 196
  3.2 0.7 %copy-start.3 = (f32[16]{0:T(128)S(1)}, f32[16]{0:T(128)}, u32[]{:S(2)}) copy-start(f32[16]{0:T(128)} %param.10) | copy-start | bytes 196
  5.5 9.0 %collective-permute-start = (bf16[208,256]{1,0:T(8,128)(2,1)S(1)}, bf16[208,256]{1,0:T(8,128)(2,1)S(1)}, u32[]{:S(2)}, u32[]{:S(2)}) collective-permute-start(bf16[208,256]{1,0:T(8,128)(2,1)S(1)} %get-tuple-element.13), channel_id=1, source_target_pairs={{0,4},{4,8},{8,12},{12,0},{1,5},{5,9},{9,13},{13,1},{2,6},{6,10},{... | collective-permute-start | bytes 319496 | tf_op jit(solution)/shard_map/ppermute | solution.py:326
  8.6 9.7 %collective-permute-start.3 = (bf16[208,256]{1,0:T(8,128)(2,1)S(1)}, bf16[208,256]{1,0:T(8,128)(2,1)S(1)}, u32[]{:S(2)}, u32[]{:S(2)}) collective-permute-start(bf16[208,256]{1,0:T(8,128)(2,1)S(1)} %get-tuple-element.14), channel_id=1, source_target_pairs={{0,8},{4,12},{8,0},{12,4},{1,9},{5,13},{9,1},{13,5},{2,10},{6,14},... | collective-permute-start | bytes 319496 | tf_op jit(solution)/shard_map/ppermute | solution.py:326
  11.2 8.6 %collective-permute-start.4 = (bf16[208,256]{1,0:T(8,128)(2,1)S(1)}, bf16[208,256]{1,0:T(8,128)(2,1)S(1)}, u32[]{:S(2)}, u32[]{:S(2)}) collective-permute-start(bf16[208,256]{1,0:T(8,128)(2,1)S(1)} %get-tuple-element.15), channel_id=1, source_target_pairs={{0,12},{4,0},{8,4},{12,8},{1,13},{5,1},{9,5},{13,9},{2,14},{6,2},{... | collective-permute-start | bytes 319496 | tf_op jit(solution)/shard_map/ppermute | solution.py:326
  12.6 7.8 %collective-permute-start.7 = (bf16[208,256]{1,0:T(8,128)(2,1)S(1)}, bf16[208,256]{1,0:T(8,128)(2,1)S(1)}, u32[]{:S(2)}, u32[]{:S(2)}) collective-permute-start(bf16[208,256]{1,0:T(8,128)(2,1)S(1)} %get-tuple-element.12.refs_0_), channel_id=1, source_target_pairs={{0,2},{2,0},{1,3},{3,1},{4,6},{6,4},{5,7},{7,5},{8,10},{10,8},{9,1... | collective-permute-start | bytes 319496 | tf_op jit(solution)/shard_map/ppermute | solution.py:326
  14.0 6.3 %collective-permute-start.1 = (bf16[208,256]{1,0:T(8,128)(2,1)S(1)}, bf16[208,256]{1,0:T(8,128)(2,1)S(1)}, u32[]{:S(2)}, u32[]{:S(2)}) collective-permute-start(bf16[208,256]{1,0:T(8,128)(2,1)S(1)} %get-tuple-element.12.refs_0_), channel_id=1, source_target_pairs={{0,1},{1,0},{2,3},{3,2},{4,5},{5,4},{6,7},{7,6},{8,9},{9,8},{10,11... | collective-permute-start | bytes 319496 | tf_op jit(solution)/shard_map/ppermute | solution.py:326
  14.5 10.3 %collective-permute-start.8 = (bf16[208,256]{1,0:T(8,128)(2,1)S(1)}, bf16[208,256]{1,0:T(8,128)(2,1)S(1)}, u32[]{:S(2)}, u32[]{:S(2)}) collective-permute-start(bf16[208,256]{1,0:T(8,128)(2,1)S(1)} %collective-permute-done.refs_1_), channel_id=1, source_target_pairs={{0,2},{2,0},{1,3},{3,1},{4,6},{6,4},{5,7},{7,5},{8,10},{10,8},{9,1... | collective-permute-start | bytes 319496 | tf_op jit(solution)/shard_map/ppermute | solution.py:326
  18.3 6.6 %collective-permute-start.11 = (bf16[208,256]{1,0:T(8,128)(2,1)S(1)}, bf16[208,256]{1,0:T(8,128)(2,1)S(1)}, u32[]{:S(2)}, u32[]{:S(2)}) collective-permute-start(bf16[208,256]{1,0:T(8,128)(2,1)S(1)} %collective-permute-done.3.refs_4_.refs_0_), channel_id=1, source_target_pairs={{0,2},{2,0},{1,3},{3,1},{4,6},{6,4},{5,7},{7,5},{8,10},{10,8},{9,1... | collective-permute-start | bytes 319496 | tf_op jit(solution)/shard_map/ppermute | solution.py:326
  19.8 5.6 %collective-permute-start.12 = (bf16[208,256]{1,0:T(8,128)(2,1)S(1)}, bf16[208,256]{1,0:T(8,128)(2,1)S(1)}, u32[]{:S(2)}, u32[]{:S(2)}) collective-permute-start(bf16[208,256]{1,0:T(8,128)(2,1)S(1)} %collective-permute-done.4.refs_5_.refs_1_), channel_id=1, source_target_pairs={{0,2},{2,0},{1,3},{3,1},{4,6},{6,4},{5,7},{7,5},{8,10},{10,8},{9,1... | collective-permute-start | bytes 319496 | tf_op jit(solution)/shard_map/ppermute | solution.py:326
  20.3 5.1 %collective-permute-start.9 = (bf16[208,256]{1,0:T(8,128)(2,1)S(1)}, bf16[208,256]{1,0:T(8,128)(2,1)S(1)}, u32[]{:S(2)}, u32[]{:S(2)}) collective-permute-start(bf16[208,256]{1,0:T(8,128)(2,1)S(1)} %collective-permute-done.7.refs_8_), channel_id=1, source_target_pairs={{0,1},{1,0},{2,3},{3,2},{4,5},{5,4},{6,7},{7,6},{8,9},{9,8},{10,11... | collective-permute-start | bytes 319496 | tf_op jit(solution)/shard_map/ppermute | solution.py:326
  20.4 5.6 %collective-permute-start.2 = (bf16[208,256]{1,0:T(8,128)(2,1)S(1)}, bf16[208,256]{1,0:T(8,128)(2,1)S(1)}, u32[]{:S(2)}, u32[]{:S(2)}) collective-permute-start(bf16[208,256]{1,0:T(8,128)(2,1)S(1)} %collective-permute-done.refs_1_), channel_id=1, source_target_pairs={{0,1},{1,0},{2,3},{3,2},{4,5},{5,4},{6,7},{7,6},{8,9},{9,8},{10,11... | collective-permute-start | bytes 319496 | tf_op jit(solution)/shard_map/ppermute | solution.py:326
  24.8 6.3 %collective-permute-start.5 = (bf16[208,256]{1,0:T(8,128)(2,1)S(1)}, bf16[208,256]{1,0:T(8,128)(2,1)S(1)}, u32[]{:S(2)}, u32[]{:S(2)}) collective-permute-start(bf16[208,256]{1,0:T(8,128)(2,1)S(1)} %collective-permute-done.3.refs_4_.refs_0_), channel_id=1, source_target_pairs={{0,1},{1,0},{2,3},{3,2},{4,5},{5,4},{6,7},{7,6},{8,9},{9,8},{10,11... | collective-permute-start | bytes 319496 | tf_op jit(solution)/shard_map/ppermute | solution.py:326
  25.0 8.4 %collective-permute-start.6 = (bf16[208,256]{1,0:T(8,128)(2,1)S(1)}, bf16[208,256]{1,0:T(8,128)(2,1)S(1)}, u32[]{:S(2)}, u32[]{:S(2)}) collective-permute-start(bf16[208,256]{1,0:T(8,128)(2,1)S(1)} %collective-permute-done.4.refs_5_.refs_1_), channel_id=1, source_target_pairs={{0,1},{1,0},{2,3},{3,2},{4,5},{5,4},{6,7},{7,6},{8,9},{9,8},{10,11... | collective-permute-start | bytes 319496 | tf_op jit(solution)/shard_map/ppermute | solution.py:326
  25.4 10.1 %collective-permute-start.10 = (bf16[208,256]{1,0:T(8,128)(2,1)S(1)}, bf16[208,256]{1,0:T(8,128)(2,1)S(1)}, u32[]{:S(2)}, u32[]{:S(2)}) collective-permute-start(bf16[208,256]{1,0:T(8,128)(2,1)S(1)} %collective-permute-done.8.refs_9_), channel_id=1, source_target_pairs={{0,1},{1,0},{2,3},{3,2},{4,5},{5,4},{6,7},{7,6},{8,9},{9,8},{10,11... | collective-permute-start | bytes 319496 | tf_op jit(solution)/shard_map/ppermute | solution.py:326
  25.5 11.8 %collective-permute-start.13 = (bf16[208,256]{1,0:T(8,128)(2,1)S(1)}, bf16[208,256]{1,0:T(8,128)(2,1)S(1)}, u32[]{:S(2)}, u32[]{:S(2)}) collective-permute-start(bf16[208,256]{1,0:T(8,128)(2,1)S(1)} %collective-permute-done.11.refs_12_), channel_id=1, source_target_pairs={{0,1},{1,0},{2,3},{3,2},{4,5},{5,4},{6,7},{7,6},{8,9},{9,8},{10,11... | collective-permute-start | bytes 319496 | tf_op jit(solution)/shard_map/ppermute | solution.py:326
  25.9 11.4 %collective-permute-start.14 = (bf16[208,256]{1,0:T(8,128)(2,1)S(1)}, bf16[208,256]{1,0:T(8,128)(2,1)S(1)}, u32[]{:S(2)}, u32[]{:S(2)}) collective-permute-start(bf16[208,256]{1,0:T(8,128)(2,1)S(1)} %collective-permute-done.12.refs_13_), channel_id=1, source_target_pairs={{0,1},{1,0},{2,3},{3,2},{4,5},{5,4},{6,7},{7,6},{8,9},{9,8},{10,11... | collective-permute-start | bytes 319496 | tf_op jit(solution)/shard_map/ppermute | solution.py:326
  31.1 7.4 %collective-permute-start.15 = (f32[8,128]{1,0:T(8,128)S(1)}, f32[8,128]{1,0:T(8,128)S(1)}, u32[]{:S(2)}, u32[]{:S(2)}) collective-permute-start(f32[8,128]{1,0:T(8,128)S(1)} %forward1.1), channel_id=1, source_target_pairs={{0,4},{4,8},{8,12},{12,0},{1,5},{5,9},{9,13},{13,1},{2,6},{6,10},{... | collective-permute-start | bytes 12296 | tf_op jit(solution)/shard_map/ppermute | solution.py:326
  33.4 5.2 %collective-permute-start.16 = (f32[8,128]{1,0:T(8,128)S(1)}, f32[8,128]{1,0:T(8,128)S(1)}, u32[]{:S(2)}, u32[]{:S(2)}) collective-permute-start(f32[8,128]{1,0:T(8,128)S(1)} %forward1.1), channel_id=1, source_target_pairs={{0,8},{4,12},{8,0},{12,4},{1,9},{5,13},{9,1},{13,5},{2,10},{6,14},... | collective-permute-start | bytes 12296 | tf_op jit(solution)/shard_map/ppermute | solution.py:326
  35.5 3.6 %collective-permute-start.17 = (f32[8,128]{1,0:T(8,128)S(1)}, f32[8,128]{1,0:T(8,128)S(1)}, u32[]{:S(2)}, u32[]{:S(2)}) collective-permute-start(f32[8,128]{1,0:T(8,128)S(1)} %forward1.1), channel_id=1, source_target_pairs={{0,12},{4,0},{8,4},{12,8},{1,13},{5,1},{9,5},{13,9},{2,14},{6,2},{... | collective-permute-start | bytes 12296 | tf_op jit(solution)/shard_map/ppermute | solution.py:326
  39.1 1.9 %collective-permute-start.18 = (f32[8,128]{1,0:T(8,128)S(1)}, f32[8,128]{1,0:T(8,128)S(1)}, u32[]{:S(2)}, u32[]{:S(2)}) collective-permute-start(f32[8,128]{1,0:T(8,128)S(1)} %add_add_fusion.refs_0_), channel_id=1, source_target_pairs={{0,1},{1,0},{2,3},{3,2},{4,5},{5,4},{6,7},{7,6},{8,9},{9,8},{10,11... | collective-permute-start | bytes 12296 | tf_op jit(solution)/shard_map/ppermute | solution.py:334
  39.1 3.7 %collective-permute-start.19 = (f32[8,128]{1,0:T(8,128)S(1)}, f32[8,128]{1,0:T(8,128)S(1)}, u32[]{:S(2)}, u32[]{:S(2)}) collective-permute-start(f32[8,128]{1,0:T(8,128)S(1)} %add_add_fusion.refs_0_), channel_id=1, source_target_pairs={{0,2},{1,3},{2,0},{3,1},{4,6},{5,7},{6,4},{7,5},{8,10},{9,11},{10,... | collective-permute-start | bytes 12296 | tf_op jit(solution)/shard_map/ppermute | solution.py:334
  40.7 3.0 %collective-permute-start.20 = (f32[8,128]{1,0:T(8,128)S(1)}, f32[8,128]{1,0:T(8,128)S(1)}, u32[]{:S(2)}, u32[]{:S(2)}) collective-permute-start(f32[8,128]{1,0:T(8,128)S(1)} %add_add_fusion.refs_0_), channel_id=1, source_target_pairs={{0,3},{1,2},{2,1},{3,0},{4,7},{5,6},{6,5},{7,4},{8,11},{9,10},{10,... | collective-permute-start | bytes 12296 | tf_op jit(solution)/shard_map/ppermute | solution.py:334

commit v3 on v2

--- a/solution.py
+++ b/solution.py
@@ -12,6 +12,7 @@
 I32 = jnp.int32
 META = 16
 VMEM_LIMIT = 48 * 1024 * 1024
+FORWARD_BYTES = 0
 
 
 def up(x, m):
@@ -39,16 +40,12 @@
     return lax.dot_general(a, b, (((1,), (0,)), ((), ())), preferred_element_type=F32)
 
 
-def pack_kernel(cfg, where_ref, blocks_hbm, hour_hbm, weight_hbm, place_hbm, fp_ref, *refs):
+def pack_kernel(cfg, where_ref, small_ref, fp_ref, *outs):
     n, capp, local_blocks, slots, w2 = cfg["n"], cfg["capp"], cfg["local"], cfg["slots"], cfg["w2"]
-    outs, (blocks_ref, hour_ref, weight_ref, place_ref, sems) = refs[:n], refs[n:]
-    pairs = ((blocks_hbm, blocks_ref), (place_hbm, place_ref), (hour_hbm, hour_ref), (weight_hbm, weight_ref))
-    copies = [pltpu.make_async_copy(src, dst, sems.at[i]) for i, (src, dst) in enumerate(pairs)]
-    for copy in copies:
-        copy.start()
-    receptors = blocks_ref.shape[0]
+    receptors = cfg["receptors"]
     cols = receptors * slots * w2
-    ids = place_ref.shape[1]
+    ids = small_ref.shape[1]
+    at_place = receptors
     used = n * capp
     padded = up(used, 256)
     half = n // 2
@@ -63,15 +60,13 @@
     sel_r = mask(iota((receptors, cols), 0) == r_of).astype(BF16)
     before = ((iota((cols, cols), 0) >> log2(w2)) < entry) & ((iota((cols, cols), 0) & (w2 - 1)) == 0)
     before = mask(before).astype(BF16)
-    for copy in copies:
-        copy.wait()
-    b = blocks_ref[...]
+    b = small_ref[0:receptors, 0:slots].astype(I32)
     high = (b >> 6).astype(F32).astype(BF16)
     low = (b & 63).astype(F32).astype(BF16)
     spread = nn(high, sel_s) * 64.0 + nn(low, sel_s)
     on_row = iota((receptors, cols), 0) == r_of
     geo = jnp.sum(jnp.where(on_row, spread, 0.0), axis=0, keepdims=True).astype(I32)
-    place = place_ref[...]
+    place = small_ref[at_place : at_place + 1, :].astype(I32)
     row16 = iota((16, ids), 0)
     owner_tab = (place >> log2(local_blocks)).astype(F32)
     local_tab = (place & (local_blocks - 1)).astype(F32)
@@ -84,12 +79,13 @@
     ranks = nn(mask(to_owner).astype(BF16), before)
     rank = jnp.sum(jnp.where(to_owner, ranks, 0.0), axis=0, keepdims=True).astype(I32)
     slot = step * capp + rank
-    weight = weight_ref[...]
+    hour = small_ref[at_place + 1 : at_place + 2, 0:receptors]
+    weight = small_ref[at_place + 2 : at_place + 3, 0:receptors]
     w_hi = weight.astype(BF16).astype(F32)
     w_mid = (weight - w_hi).astype(BF16).astype(F32)
     w_lo = weight - w_hi - w_mid
     row_r = iota((16, receptors), 0)
-    per_r = jnp.where(row_r == 1, hour_ref[...].astype(F32), 0.0)
+    per_r = jnp.where(row_r == 1, hour, 0.0)
     per_r = jnp.where(row_r == 3, w_hi, per_r)
     per_r = jnp.where(row_r == 4, w_mid, per_r)
     per_r = jnp.where(row_r == 5, w_lo, per_r)
@@ -122,25 +118,24 @@
     receptors = blocks.shape[0]
     cells = footprint.shape[3]
     rows = w2 * capp + META
-    hour_start, obs_weight, placement = (
-        hour_start.reshape(1, receptors), obs_weight.reshape(1, receptors), placement.reshape(1, -1),
-    )
+    ids = placement.shape[0]
+    height = up(receptors + 3, 8)
+
+    def put(x, at):
+        x = x.astype(F32)
+        return jnp.pad(x, ((at, height - at - x.shape[0]), (0, ids - x.shape[1])))
+
+    small = put(blocks, 0) + put(placement[None], receptors)
+    small = small + put(hour_start[None], receptors + 1) + put(obs_weight[None], receptors + 2)
     vm = pl.BlockSpec(memory_space=pltpu.VMEM)
     return pl.pallas_call(
         functools.partial(pack_kernel, cfg),
         out_shape=[jax.ShapeDtypeStruct((rows, cells), BF16)] * n,
-        in_specs=[pl.BlockSpec(memory_space=pltpu.SMEM)] + [pl.BlockSpec(memory_space=pltpu.HBM)] * 4 + [vm],
+        in_specs=[pl.BlockSpec(memory_space=pltpu.SMEM), vm, vm],
         out_specs=[vm] * n,
-        scratch_shapes=[
-            pltpu.VMEM(blocks.shape, I32),
-            pltpu.VMEM(hour_start.shape, I32),
-            pltpu.VMEM(obs_weight.shape, F32),
-            pltpu.VMEM(placement.shape, I32),
-            pltpu.SemaphoreType.DMA((4,)),
-        ],
         compiler_params=pltpu.CompilerParams(vmem_limit_bytes=VMEM_LIMIT),
         name="pack",
-    )(where, blocks, hour_start, obs_weight, placement, footprint.reshape(receptors * slots * w2, cells))
+    )(where, small, footprint.reshape(receptors * slots * w2, cells))
 
 
 def slots_of(bufs, rows):
@@ -180,13 +175,39 @@
             f8_ref[base_row + d * capp : base_row + (d + 1) * capp, h * cells : (h + 1) * cells] = value
 
 
-def forward_kernel(cfg, nbuf, *refs):
-    bufs, (probes_ref, sofar_ref, out_ref, f8_ref) = refs[:nbuf], refs[nbuf:]
-    local, k = cfg["local"], cfg["k"]
-    placed = slots_of(bufs, cfg["rows"])
-    meta = load_meta(cfg, placed)
+def after_kernel(x_ref, unread_ref, out_ref):
+    out_ref[...] = x_ref[...]
+
+
+def after(x, first):
+    return pl.pallas_call(
+        after_kernel,
+        out_shape=jax.ShapeDtypeStruct(x.shape, x.dtype),
+        grid=(1,),
+        in_specs=[pl.BlockSpec(x.shape, lambda i: (0, 0)), pl.BlockSpec((16, 128), lambda i: (0, 0))],
+        out_specs=pl.BlockSpec(x.shape, lambda i: (0, 0)),
+        compiler_params=pltpu.CompilerParams(vmem_limit_bytes=4 * 1024 * 1024),
+        cost_estimate=pl.CostEstimate(flops=0, bytes_accessed=2 * x.size, transcendentals=0),
+        name="after",
+    )(x, first)
+
+
+def forward_kernel(cfg, counts, *refs):
+    local, k, rows, capp = cfg["local"], cfg["k_core"], cfg["rows"], cfg["capp"]
+    half = cfg["n"] // 2 * capp
+    probes_ref, out_ref, f8_ref = refs[-3:]
+    at = 0
+    firsts = []
+    for i, sides_n in enumerate(counts):
+        sides = []
+        for count in sides_n:
+            sides.append(slots_of(refs[at : at + count], rows))
+            at += count
+        metas = [load_meta(cfg, placed) for placed in sides]
+        spread_hours(cfg, sides, metas, f8_ref, i * half)
+        firsts.append(metas[0][0:8])
+    meta = jnp.concatenate(firsts, axis=1)
     used = meta.shape[1]
-    spread_hours(cfg, [placed], [meta], f8_ref, 0)
     own = iota((local, used), 0) + 1 == meta[0:1].astype(I32)
     row = iota((8, used), 0)
     dots = jnp.zeros((8, used), F32)
@@ -196,27 +217,26 @@
         y = jnp.sum(jnp.where(own, x, 0.0), axis=0, keepdims=True)
         dots = jnp.where(row == j, y, dots)
     to_r = mask(iota((out_ref.shape[1], used), 0) == meta[2:3].astype(I32))
-    out_ref[...] = sofar_ref[...] + lax.dot_general(
+    out_ref[...] = lax.dot_general(
         dots, to_r, (((1,), (1,)), ((), ())), precision=lax.Precision.HIGHEST, preferred_element_type=F32
     )
 
 
-def forward(cfg, bufs, probes_t, sofar, name):
+def forward(cfg, own, probes_t, out_shape):
     n, capp, hours, cells = cfg["n"], cfg["capp"], cfg["hours"], cfg["cells"]
-    used = n // 2 * capp
+    args = [b for half in own for side in half for b in side]
+    counts = [[len(side) for side in half] for half in own]
     vm = pl.BlockSpec(memory_space=pltpu.VMEM)
     return pl.pallas_call(
-        functools.partial(forward_kernel, cfg, len(bufs)),
-        out_shape=jax.ShapeDtypeStruct(sofar.shape, F32),
-        in_specs=[vm] * (len(bufs) + 2),
+        functools.partial(forward_kernel, cfg, counts),
+        out_shape=jax.ShapeDtypeStruct(out_shape, F32),
+        in_specs=[vm] * (len(args) + 1),
         out_specs=vm,
-        scratch_shapes=[pltpu.VMEM((used, hours * cells), BF16)],
+        scratch_shapes=[pltpu.VMEM((n * capp, hours * cells), BF16)],
         compiler_params=pltpu.CompilerParams(vmem_limit_bytes=VMEM_LIMIT),
-        cost_estimate=pl.CostEstimate(
-            flops=2 * used * probes_t.size, bytes_accessed=2 * probes_t.size, transcendentals=0
-        ),
-        name=name,
-    )(*bufs, probes_t, sofar)
+        cost_estimate=pl.CostEstimate(flops=0, bytes_accessed=FORWARD_BYTES, transcendentals=0),
+        name="forward",
+    )(*args, probes_t)
 
 
 def prepare_kernel(cfg, counts, *refs):
@@ -326,46 +346,44 @@
     return lax.ppermute(x, axis, [(i, (i + d) % n) for i in range(n)])
 
 
-def shift2(x, g, s):
-    nreg, ntm = lax.axis_size("reg"), lax.axis_size("tm")
-    pairs = [
-        (r * ntm + t, (r + g) % nreg * ntm + (t + s) % ntm) for r in range(nreg) for t in range(ntm)
-    ]
-    return lax.ppermute(x, ("reg", "tm"), pairs)
-
-
 def shards(probes, footprint, blocks, hour_start, obs_weight, placement):
     n, nreg, ntm = lax.axis_size("rcp"), lax.axis_size("reg"), lax.axis_size("tm")
     local, hours, width = probes.shape
     receptors, slots, w2, cells = footprint.shape
     k = width // cells
+    kd = k // (nreg * ntm)
     capp = up(3 * receptors * slots // (2 * n), 16)
     cfg = dict(
-        n=n, capp=capp, local=local, hours=hours, cells=cells, slots=slots, w2=w2, k=k,
-        kd=k // (nreg * ntm), rows=w2 * capp + META,
+        n=n, capp=capp, local=local, hours=hours, cells=cells, receptors=receptors, slots=slots, w2=w2,
+        kd=kd, k_core=nreg * kd, rows=w2 * capp + META,
     )
     z, reg, tm = lax.axis_index("rcp"), lax.axis_index("reg"), lax.axis_index("tm")
-    where = jnp.stack([z, tm, reg * ntm + tm]).astype(I32)
+    where = jnp.stack([z, tm, reg]).astype(I32)
     outs = pack(cfg, where, blocks, hour_start, obs_weight, placement, footprint)
-    bufs = [outs[0]] + [shift(outs[d], "rcp", d) for d in range(1, n)]
-    probes_t = probes.reshape(local, hours, k, cells).transpose(2, 0, 1, 3).reshape(k * local, hours * cells)
+    probes_t = lax.dynamic_index_in_dim(probes.reshape(local, hours, nreg, ntm, kd, cells), tm, 3, keepdims=False)
+    probes_t = probes_t.transpose(2, 3, 0, 1, 4).reshape(nreg * kd * local, hours * cells)
+
+    def with_cores(half):
+        return [half] + [[shift(b, "tm", s) for b in half] for s in range(1, ntm)]
+
+    mine = after(outs[0], probes_t)
+    bufs = [mine] + [shift(outs[d], "rcp", d) for d in range(1, n)]
     halves = [bufs[: n // 2], bufs[n // 2 :]]
     if n > 4:
         halves = [[jnp.concatenate(half, axis=0)] for half in halves]
-    partial = jnp.zeros((8, up(n * receptors, 128)), F32)
-    for i, half in enumerate(halves):
-        partial = forward(cfg, half, probes_t, partial, f"forward{i}")
-    columns = [[[half] + [[shift(b, "tm", s) for b in half] for s in range(1, ntm)] for half in halves]]
+    own = [with_cores(half) for half in halves]
+    partial = forward(cfg, own, probes_t, (8, up(n * receptors, 128)))
+    columns = [own]
     for g in range(1, nreg):
         across = [[shift(b, "reg", g) for b in half] for half in halves]
-        columns.append([[half] + [[shift(b, "tm", s) for b in half] for s in range(1, ntm)] for half in across])
+        columns.append([with_cores(half) for half in across])
     f8, meta, zero = prepare(cfg, columns, partial.shape)
     observed = partial + zero
     for d in range(1, n):
         observed = observed + shift(partial, "rcp", d)
-    observed = [[shift2(observed, g, s) if g or s else observed for s in range(ntm)] for g in range(nreg)]
+    observed = [[shift(observed, "reg", g) if g else observed] for g in range(nreg)]
     result = adjoint(cfg, where, f8, meta, observed)
-    return result.reshape(local, hours, cfg["kd"] * cells)
+    return result.reshape(local, hours, kd * cells)
 
 
 def solution(mesh):

time: 47.7 us -> 44.9 us (0.941)
  waiting for transfers between devices: 5.97 us -> 10.3 us
  local copies, waits for them, and re-layouts: 7.69 us -> 3.66 us
  starting transfers between devices: 21.9 us -> 18.1 us
  other arithmetic: 0.09 us -> 2.79 us
  Pallas kernels: 11.7 us -> 9.67 us
    ppermute x18 -> x19, waiting for transfers between devices: 3.25 us -> 10.3 us  [shift(): return lax.ppermute(x, axis, [(i, (i + d) % n) for i in range(n)])]
    unnamed x9 -> x1, local copies, waits for them, and re-layouts: 4.18 us -> 0.67 us
    ppermute x3 -> x0, waiting for transfers between devices: 2.72 us -> none  [shift2(): return lax.ppermute(x, ('reg', 'tm'), pairs)]
    reshape x1 -> x0, local copies, waits for them, and re-layouts: 2.46 us -> none  [shards(): probes.reshape(local, hours, k, cells).transpose(2, 0, 1, 3)]
    convert_element_type x0 -> x3, other arithmetic: none -> 2.04 us  [put(): x = x.astype(F32)]
    pallas_call x2, Pallas kernels: 5.11 us -> 3.14 us  [the longest x1 3.13 us: forward(): pl.pallas_call(functools.partial(forward_kernel, cfg, counts), out_shape=...]
    dynamic_slice x0 -> x2, local copies, waits for them, and re-layouts: none -> 1.93 us  [shards(): lax.dynamic_index_in_dim(probes.reshape(local, hours, nreg, ntm, kd, cell...]
    ppermute x18 -> x19, starting transfers between devices: 20 us -> 18.1 us  [shift(): return lax.ppermute(x, axis, [(i, (i + d) % n) for i in range(n)])]
  transfers between devices with their start and end apart: 21 -> 19, of which waited for: 5 -> 8; matrix products, arithmetic and copies ran while one was open for 8% -> 6% of each run, Pallas kernels for 13% -> 10%
where the time goes in v3:
time: 44.9 us; the launch traced here: 44.6 us
  starting transfers between devices  18.1 us (40%)
  waiting for transfers between devices  10.3 us (23%)
  Pallas kernels  9.67 us (22%)
  local copies, waits for them, and re-layouts  3.66 us (8%)
  other arithmetic  2.79 us (6%)
    ppermute x19, starting transfers between devices, shift(): return lax.ppermute(x, axis, [(i, (i + d) % n) for i in range(n)])  18.1 us
    ppermute x19, waiting for transfers between devices, shift(): return lax.ppermute(x, axis, [(i, (i + d) % n) for i in range(n)])  10.3 us
    pallas_call x1, Pallas kernels, adjoint(): pl.pallas_call(functools.partial(adjoint_kernel, cfg, parts), out_shape=j...  3.69 us
    pallas_call x1, Pallas kernels, forward(): pl.pallas_call(functools.partial(forward_kernel, cfg, counts), out_shape=...  3.13 us
    convert_element_type x3, other arithmetic, put(): x = x.astype(F32)  2.04 us
    dynamic_slice x2, local copies, waits for them, and re-layouts, shards(): lax.dynamic_index_in_dim(probes.reshape(local, hours, nreg, ntm, kd, cell...  1.93 us
    pallas_call x1, Pallas kernels, pack(): pl.pallas_call(functools.partial(pack_kernel, cfg), out_shape=[jax.ShapeD...  1.62 us
    pallas_call x1, Pallas kernels, prepare(): pl.pallas_call(functools.partial(prepare_kernel, cfg, counts), out_shape=...  1.22 us
  transfers between devices with their start and end apart: 19, of which 8 were waited for; matrix products, arithmetic and copies ran while one was open for 6% of the time, Pallas kernels for 10%

profile of v3, /device:TPU:0, one launch (start us, length us, event | category | flops | bytes accessed | tf_op | source)
XLA Modules:
  0.0 44.6 jit_solution(10316507940877000339)
XLA Ops:
  0.0 1.1 %reshape.14.fp_ref = bf16[512,256]{1,0:T(8,128)(2,1)S(1)} reshape(bf16[16,16,2,256]{3,2,1,0:T(2,128)(2,1)} %param.7) | data formatting | bytes 524288 | tf_op jit(solution)/shard_map/reshape | solution.py:138
  1.1 0.7 %convert_element_type.23 = f32[16,16]{1,0:T(8,128)S(1)} convert(s32[16,16]{1,0:T(8,128)} %param.8) | non-fusion elementwise | flops 256 | bytes 2048 | tf_op jit(solution)/shard_map/convert_element_type | solution.py:125
  1.8 0.7 %convert_element_type.24 = f32[512]{0:T(512)S(1)} convert(s32[512]{0:T(512)} %param.11) | non-fusion elementwise | flops 512 | bytes 4096 | tf_op jit(solution)/shard_map/convert_element_type | solution.py:125
  2.4 0.7 %convert_bitcast_fusion = f32[1,16]{1,0:T(1,128)S(1)} fusion(s32[16]{0:T(128)} %param.9), kind=kLoop, calls=%fused_computation.3 | loop fusion | flops 16 | bytes 128 | tf_op jit(solution)/shard_map/convert_element_type | solution.py:125
  3.1 0.1 pad_add_fusion.1.where_ref
  3.2 0.7 %pad_add_fusion.small_ref = f32[24,512]{1,0:T(8,128)S(1)} fusion(f32[1,16]{1,0:T(1,128)} %bitcast.20, f32[1,16]{1,0:T(1,128)S(1)} %convert_bitcast_fusion, f32[1,512]{1,0:T(1,128)S(1)} %bitcast.19, f32[16,16]{1,0:T(8,128)S(1)} %convert_element_type.23), kind=kLoop, calls=%fused_computation | loop fusion | flops 36864 | bytes 52352 | tf_op jit(solution)/shard_map/add | solution.py:129
  3.8 1.6 %pack.1 = (bf16[208,256]{1,0:T(8,128)(2,1)S(1)}, bf16[208,256]{1,0:T(8,128)(2,1)S(1)}, bf16[208,256]{1,0:T(8,128)(2,1)S(1)}, bf16[208,256]{1,0:T(8,128)(2,1)S(1)}) custom-call(s32[3]{0:T(128)S(1)} %pad_add_fusion.1.where_ref, f32[24,512]{1,0:T(8,128)S(1)} %pad_add_fusion.small_ref, bf16[512,256]{1,0:T(8,128)(2,1)S(1)} %reshape.14.fp_ref), custom_call_target="tpu_custom_call" | custom-call | tf_op jit(solution)/shard_map/pack/pallas_call | solution.py:131
  5.5 3.1 %collective-permute-start = (bf16[208,256]{1,0:T(8,128)(2,1)S(1)}, bf16[208,256]{1,0:T(8,128)(2,1)S(1)}, u32[]{:S(2)}, u32[]{:S(2)}) collective-permute-start(bf16[208,256]{1,0:T(8,128)(2,1)S(1)} %get-tuple-element.13), channel_id=1, source_target_pairs={{0,4},{4,8},{8,12},{12,0},{1,5},{5,9},{9,13},{13,1},{2,6},{6,10},{... | collective-permute-start | bytes 319496 | tf_op jit(solution)/shard_map/ppermute | solution.py:346
  8.5 2.6 %collective-permute-start.3 = (bf16[208,256]{1,0:T(8,128)(2,1)S(1)}, bf16[208,256]{1,0:T(8,128)(2,1)S(1)}, u32[]{:S(2)}, u32[]{:S(2)}) collective-permute-start(bf16[208,256]{1,0:T(8,128)(2,1)S(1)} %get-tuple-element.14), channel_id=1, source_target_pairs={{0,8},{4,12},{8,0},{12,4},{1,9},{5,13},{9,1},{13,5},{2,10},{6,14},... | collective-permute-start | bytes 319496 | tf_op jit(solution)/shard_map/ppermute | solution.py:346
  11.1 1.8 %constant_dynamic-slice_fusion = bf16[128,8,2,1,2,256]{5,1,4,3,2,0:T(8,128)(2,1)S(1)} fusion(bf16[128,8,2,2,2,256]{5,1,4,3,2,0:T(8,128)(2,1)} %bitcast.18, s32[]{:T(128)S(6)} %select_n.4), kind=kLoop, calls=%fused_computation.4 | loop fusion | bytes 4194308 | tf_op jit(solution)/shard_map/jit(dynamic_index_in_dim)/dynamic_slice | solution.py:363
  12.9 0.1 copy.7
  13.1 0.7 %copy.8 = bf16[64,8,8,256]{3,1,2,0:T(8,128)(2,1)S(1)} copy(bf16[64,8,8,256]{3,2,1,0:T(8,128)(2,1)S(1)} %bitcast.17) | data formatting | bytes 4194304
  13.8 0.1 collective-permute-start.1
  13.9 1.4 %collective-permute-start.4 = (bf16[208,256]{1,0:T(8,128)(2,1)S(1)}, bf16[208,256]{1,0:T(8,128)(2,1)S(1)}, u32[]{:S(2)}, u32[]{:S(2)}) collective-permute-start(bf16[208,256]{1,0:T(8,128)(2,1)S(1)} %get-tuple-element.15), channel_id=1, source_target_pairs={{0,12},{4,0},{8,4},{12,8},{1,13},{5,1},{9,5},{13,9},{2,14},{6,2},{... | collective-permute-start | bytes 319496 | tf_op jit(solution)/shard_map/ppermute | solution.py:346
  15.3 1.5 %collective-permute-start.7 = (bf16[208,256]{1,0:T(8,128)(2,1)S(1)}, bf16[208,256]{1,0:T(8,128)(2,1)S(1)}, u32[]{:S(2)}, u32[]{:S(2)}) collective-permute-start(bf16[208,256]{1,0:T(8,128)(2,1)S(1)} %after.1.refs_0_), channel_id=1, source_target_pairs={{0,2},{2,0},{1,3},{3,1},{4,6},{6,4},{5,7},{7,5},{8,10},{10,8},{9,1... | collective-permute-start | bytes 319496 | tf_op jit(solution)/shard_map/ppermute | solution.py:346
  16.8 0.0 collective-permute-done.refs_1_
  16.8 0.0 collective-permute-start.2
  16.8 1.5 %collective-permute-done.3.refs_4_ = bf16[208,256]{1,0:T(8,128)(2,1)S(1)} collective-permute-done((bf16[208,256]{1,0:T(8,128)(2,1)S(1)}, bf16[208,256]{1,0:T(8,128)(2,1)S(1)}, u32[]{:S(2)}, u32[]{:S(2)}) %collective-permute-start.3) | collective-permute-done | bytes 106528 | tf_op jit(solution)/shard_map/ppermute | solution.py:346
  18.2 0.0 collective-permute-start.5
  18.2 0.0 collective-permute-done.1.refs_2_
  18.2 1.5 %collective-permute-start.8 = (bf16[208,256]{1,0:T(8,128)(2,1)S(1)}, bf16[208,256]{1,0:T(8,128)(2,1)S(1)}, u32[]{:S(2)}, u32[]{:S(2)}) collective-permute-start(bf16[208,256]{1,0:T(8,128)(2,1)S(1)} %collective-permute-done.refs_1_), channel_id=1, source_target_pairs={{0,2},{2,0},{1,3},{3,1},{4,6},{6,4},{5,7},{7,5},{8,10},{10,8},{9,1... | collective-permute-start | bytes 319496 | tf_op jit(solution)/shard_map/ppermute | solution.py:346
  19.7 0.7 %collective-permute-done.4.refs_5_ = bf16[208,256]{1,0:T(8,128)(2,1)S(1)} collective-permute-done((bf16[208,256]{1,0:T(8,128)(2,1)S(1)}, bf16[208,256]{1,0:T(8,128)(2,1)S(1)}, u32[]{:S(2)}, u32[]{:S(2)}) %collective-permute-start.4) | collective-permute-done | bytes 106528 | tf_op jit(solution)/shard_map/ppermute | solution.py:346
  20.4 1.5 %collective-permute-start.11 = (bf16[208,256]{1,0:T(8,128)(2,1)S(1)}, bf16[208,256]{1,0:T(8,128)(2,1)S(1)}, u32[]{:S(2)}, u32[]{:S(2)}) collective-permute-start(bf16[208,256]{1,0:T(8,128)(2,1)S(1)} %collective-permute-done.3.refs_4_), channel_id=1, source_target_pairs={{0,2},{2,0},{1,3},{3,1},{4,6},{6,4},{5,7},{7,5},{8,10},{10,8},{9,1... | collective-permute-start | bytes 319496 | tf_op jit(solution)/shard_map/ppermute | solution.py:346
  21.9 0.0 collective-permute-done.7.refs_8_
  21.9 0.5 %collective-permute-start.12 = (bf16[208,256]{1,0:T(8,128)(2,1)S(1)}, bf16[208,256]{1,0:T(8,128)(2,1)S(1)}, u32[]{:S(2)}, u32[]{:S(2)}) collective-permute-start(bf16[208,256]{1,0:T(8,128)(2,1)S(1)} %collective-permute-done.4.refs_5_), channel_id=1, source_target_pairs={{0,2},{2,0},{1,3},{3,1},{4,6},{6,4},{5,7},{7,5},{8,10},{10,8},{9,1... | collective-permute-start | bytes 319496 | tf_op jit(solution)/shard_map/ppermute | solution.py:346
  22.4 0.0 collective-permute-done.2.refs_3_
  22.4 0.0 collective-permute-start.6
  22.4 0.0 collective-permute-done.5.refs_6_
  22.4 0.5 %collective-permute-start.9 = (bf16[208,256]{1,0:T(8,128)(2,1)S(1)}, bf16[208,256]{1,0:T(8,128)(2,1)S(1)}, u32[]{:S(2)}, u32[]{:S(2)}) collective-permute-start(bf16[208,256]{1,0:T(8,128)(2,1)S(1)} %collective-permute-done.7.refs_8_), channel_id=1, source_target_pairs={{0,1},{1,0},{2,3},{3,2},{4,5},{5,4},{6,7},{7,6},{8,9},{9,8},{10,11... | collective-permute-start | bytes 319496 | tf_op jit(solution)/shard_map/ppermute | solution.py:346
  22.9 1.1 %collective-permute-done.8.refs_9_ = bf16[208,256]{1,0:T(8,128)(2,1)S(1)} collective-permute-done((bf16[208,256]{1,0:T(8,128)(2,1)S(1)}, bf16[208,256]{1,0:T(8,128)(2,1)S(1)}, u32[]{:S(2)}, u32[]{:S(2)}) %collective-permute-start.8) | collective-permute-done | bytes 106528 | tf_op jit(solution)/shard_map/ppermute | solution.py:346
  24.0 0.0 collective-permute-start.10
  24.0 2.3 %collective-permute-done.11.refs_12_ = bf16[208,256]{1,0:T(8,128)(2,1)S(1)} collective-permute-done((bf16[208,256]{1,0:T(8,128)(2,1)S(1)}, bf16[208,256]{1,0:T(8,128)(2,1)S(1)}, u32[]{:S(2)}, u32[]{:S(2)}) %collective-permute-start.11) | collective-permute-done | bytes 106528 | tf_op jit(solution)/shard_map/ppermute | solution.py:346
  26.3 0.0 collective-permute-start.13
  26.3 1.9 %collective-permute-done.12.refs_13_ = bf16[208,256]{1,0:T(8,128)(2,1)S(1)} collective-permute-done((bf16[208,256]{1,0:T(8,128)(2,1)S(1)}, bf16[208,256]{1,0:T(8,128)(2,1)S(1)}, u32[]{:S(2)}, u32[]{:S(2)}) %collective-permute-start.12) | collective-permute-done | bytes 106528 | tf_op jit(solution)/shard_map/ppermute | solution.py:346
  28.2 0.0 collective-permute-start.14
  28.2 0.0 collective-permute-done.6.refs_7_
  28.2 3.1 %forward.1 = f32[8,128]{1,0:T(8,128)S(1)} custom-call(bf16[208,256]{1,0:T(8,128)(2,1)S(1)} %after.1.refs_0_, bf16[208,256]{1,0:T(8,128)(2,1)S(1)} %collective-permute-done.refs_1_, bf16[208,256]{1,0:T(8,128)(2,1)S(1)} %collective-permute-done.1.refs_2_, bf16[208,256]{1,0:T(8,128)(2,1)S(1)} %collective-permute-done.2.refs_3_, ...), custom_call_target="tpu_custom_call" | custom-call | tf_op jit(solution)/shard_map/forward/pallas_call | solution.py:230
  31.3 0.0 collective-permute-start.15
  31.3 0.0 collective-permute-done.9.refs_10_
  31.3 2.1 %collective-permute-start.16 = (f32[8,128]{1,0:T(8,128)S(1)}, f32[8,128]{1,0:T(8,128)S(1)}, u32[]{:S(2)}, u32[]{:S(2)}) collective-permute-start(f32[8,128]{1,0:T(8,128)S(1)} %forward.1), channel_id=1, source_target_pairs={{0,8},{4,12},{8,0},{12,4},{1,9},{5,13},{9,1},{13,5},{2,10},{6,14},... | collective-permute-start | bytes 12296 | tf_op jit(solution)/shard_map/ppermute | solution.py:346
  33.4 0.0 collective-permute-done.10.refs_11_
  33.4 1.8 %collective-permute-start.17 = (f32[8,128]{1,0:T(8,128)S(1)}, f32[8,128]{1,0:T(8,128)S(1)}, u32[]{:S(2)}, u32[]{:S(2)}) collective-permute-start(f32[8,128]{1,0:T(8,128)S(1)} %forward.1), channel_id=1, source_target_pairs={{0,12},{4,0},{8,4},{12,8},{1,13},{5,1},{9,5},{13,9},{2,14},{6,2},{... | collective-permute-start | bytes 12296 | tf_op jit(solution)/shard_map/ppermute | solution.py:346
  35.2 0.0 collective-permute-done.13.refs_14_
  35.2 0.0 collective-permute-done.14.refs_15_
  35.2 1.2 %prepare.1 = (bf16[768,2048]{1,0:T(8,128)(2,1)S(1)}, f32[8,768]{1,0:T(8,128)S(1)}, f32[8,128]{1,0:T(8,128)S(1)}) custom-call(bf16[208,256]{1,0:T(8,128)(2,1)S(1)} %after.1.refs_0_, bf16[208,256]{1,0:T(8,128)(2,1)S(1)} %collective-permute-done.refs_1_, bf16[208,256]{1,0:T(8,128)(2,1)S(1)} %collective-permute-done.1.refs_2_, ...), custom_call_target="tpu_custom_call" | custom-call | bytes 9437184 | tf_op jit(solution)/shard_map/prepare/pallas_call | solution.py:266
  36.5 0.3 collective-permute-done.15
  36.7 0.0 collective-permute-done.16
  36.7 0.6 %collective-permute-done.17 = f32[8,128]{1,0:T(8,128)S(1)} collective-permute-done((f32[8,128]{1,0:T(8,128)S(1)}, f32[8,128]{1,0:T(8,128)S(1)}, u32[]{:S(2)}, u32[]{:S(2)}) %collective-permute-start.17) | collective-permute-done | bytes 4128 | tf_op jit(solution)/shard_map/ppermute | solution.py:346
  37.3 1.5 %collective-permute-start.18 = (f32[8,128]{1,0:T(8,128)S(1)}, f32[8,128]{1,0:T(8,128)S(1)}, u32[]{:S(2)}, u32[]{:S(2)}) collective-permute-start(f32[8,128]{1,0:T(8,128)S(1)} %add_add_fusion.refs_0_), channel_id=1, source_target_pairs={{0,2},{2,0},{1,3},{3,1},{4,6},{6,4},{5,7},{7,5},{8,10},{10,8},{9,1... | collective-permute-start | bytes 12296 | tf_op jit(solution)/shard_map/ppermute | solution.py:346
  38.8 2.1 %collective-permute-done.18.refs_1_ = f32[8,128]{1,0:T(8,128)S(1)} collective-permute-done((f32[8,128]{1,0:T(8,128)S(1)}, f32[8,128]{1,0:T(8,128)S(1)}, u32[]{:S(2)}, u32[]{:S(2)}) %collective-permute-start.18) | collective-permute-done | bytes 4128 | tf_op jit(solution)/shard_map/ppermute | solution.py:346
  40.9 3.7 %adjoint.1 = f32[1024,512]{1,0:T(8,128)} custom-call(s32[3]{0:T(128)S(1)} %pad_add_fusion.1.where_ref, f32[8,768]{1,0:T(8,128)S(1)} %get-tuple-element.16.meta_ref, bf16[768,2048]{1,0:T(8,128)(2,1)S(1)} %get-tuple-element.17.f8_ref, f32[8,128]{1,0:T(8,128)S(1)} %add_add_fusion.refs_0_, f32[8,128]{1,0:T(8,128)S(1)} %collective-permute-done.18.refs_1_), custom_call_target="tpu_custom_call" | custom-call | tf_op jit(solution)/shard_map/adjoint/pallas_call | solution.py:329
  (2 shorter events, 0.0 us)
Async XLA Ops:
  5.5 11.3 %collective-permute-start = (bf16[208,256]{1,0:T(8,128)(2,1)S(1)}, bf16[208,256]{1,0:T(8,128)(2,1)S(1)}, u32[]{:S(2)}, u32[]{:S(2)}) collective-permute-start(bf16[208,256]{1,0:T(8,128)(2,1)S(1)} %get-tuple-element.13), channel_id=1, source_target_pairs={{0,4},{4,8},{8,12},{12,0},{1,5},{5,9},{9,13},{13,1},{2,6},{6,10},{... | collective-permute-start | bytes 319496 | tf_op jit(solution)/shard_map/ppermute | solution.py:346
  8.5 9.7 %collective-permute-start.3 = (bf16[208,256]{1,0:T(8,128)(2,1)S(1)}, bf16[208,256]{1,0:T(8,128)(2,1)S(1)}, u32[]{:S(2)}, u32[]{:S(2)}) collective-permute-start(bf16[208,256]{1,0:T(8,128)(2,1)S(1)} %get-tuple-element.14), channel_id=1, source_target_pairs={{0,8},{4,12},{8,0},{12,4},{1,9},{5,13},{9,1},{13,5},{2,10},{6,14},... | collective-permute-start | bytes 319496 | tf_op jit(solution)/shard_map/ppermute | solution.py:346
  13.8 4.4 %collective-permute-start.1 = (bf16[208,256]{1,0:T(8,128)(2,1)S(1)}, bf16[208,256]{1,0:T(8,128)(2,1)S(1)}, u32[]{:S(2)}, u32[]{:S(2)}) collective-permute-start(bf16[208,256]{1,0:T(8,128)(2,1)S(1)} %after.1.refs_0_), channel_id=1, source_target_pairs={{0,1},{1,0},{2,3},{3,2},{4,5},{5,4},{6,7},{7,6},{8,9},{9,8},{10,11... | collective-permute-start | bytes 319496 | tf_op jit(solution)/shard_map/ppermute | solution.py:346
  13.9 6.5 %collective-permute-start.4 = (bf16[208,256]{1,0:T(8,128)(2,1)S(1)}, bf16[208,256]{1,0:T(8,128)(2,1)S(1)}, u32[]{:S(2)}, u32[]{:S(2)}) collective-permute-start(bf16[208,256]{1,0:T(8,128)(2,1)S(1)} %get-tuple-element.15), channel_id=1, source_target_pairs={{0,12},{4,0},{8,4},{12,8},{1,13},{5,1},{9,5},{13,9},{2,14},{6,2},{... | collective-permute-start | bytes 319496 | tf_op jit(solution)/shard_map/ppermute | solution.py:346
  15.3 6.6 %collective-permute-start.7 = (bf16[208,256]{1,0:T(8,128)(2,1)S(1)}, bf16[208,256]{1,0:T(8,128)(2,1)S(1)}, u32[]{:S(2)}, u32[]{:S(2)}) collective-permute-start(bf16[208,256]{1,0:T(8,128)(2,1)S(1)} %after.1.refs_0_), channel_id=1, source_target_pairs={{0,2},{2,0},{1,3},{3,1},{4,6},{6,4},{5,7},{7,5},{8,10},{10,8},{9,1... | collective-permute-start | bytes 319496 | tf_op jit(solution)/shard_map/ppermute | solution.py:346
  16.8 5.7 %collective-permute-start.2 = (bf16[208,256]{1,0:T(8,128)(2,1)S(1)}, bf16[208,256]{1,0:T(8,128)(2,1)S(1)}, u32[]{:S(2)}, u32[]{:S(2)}) collective-permute-start(bf16[208,256]{1,0:T(8,128)(2,1)S(1)} %collective-permute-done.refs_1_), channel_id=1, source_target_pairs={{0,1},{1,0},{2,3},{3,2},{4,5},{5,4},{6,7},{7,6},{8,9},{9,8},{10,11... | collective-permute-start | bytes 319496 | tf_op jit(solution)/shard_map/ppermute | solution.py:346
  18.2 4.2 %collective-permute-start.5 = (bf16[208,256]{1,0:T(8,128)(2,1)S(1)}, bf16[208,256]{1,0:T(8,128)(2,1)S(1)}, u32[]{:S(2)}, u32[]{:S(2)}) collective-permute-start(bf16[208,256]{1,0:T(8,128)(2,1)S(1)} %collective-permute-done.3.refs_4_), channel_id=1, source_target_pairs={{0,1},{1,0},{2,3},{3,2},{4,5},{5,4},{6,7},{7,6},{8,9},{9,8},{10,11... | collective-permute-start | bytes 319496 | tf_op jit(solution)/shard_map/ppermute | solution.py:346
  18.2 5.8 %collective-permute-start.8 = (bf16[208,256]{1,0:T(8,128)(2,1)S(1)}, bf16[208,256]{1,0:T(8,128)(2,1)S(1)}, u32[]{:S(2)}, u32[]{:S(2)}) collective-permute-start(bf16[208,256]{1,0:T(8,128)(2,1)S(1)} %collective-permute-done.refs_1_), channel_id=1, source_target_pairs={{0,2},{2,0},{1,3},{3,1},{4,6},{6,4},{5,7},{7,5},{8,10},{10,8},{9,1... | collective-permute-start | bytes 319496 | tf_op jit(solution)/shard_map/ppermute | solution.py:346
  20.4 5.9 %collective-permute-start.11 = (bf16[208,256]{1,0:T(8,128)(2,1)S(1)}, bf16[208,256]{1,0:T(8,128)(2,1)S(1)}, u32[]{:S(2)}, u32[]{:S(2)}) collective-permute-start(bf16[208,256]{1,0:T(8,128)(2,1)S(1)} %collective-permute-done.3.refs_4_), channel_id=1, source_target_pairs={{0,2},{2,0},{1,3},{3,1},{4,6},{6,4},{5,7},{7,5},{8,10},{10,8},{9,1... | collective-permute-start | bytes 319496 | tf_op jit(solution)/shard_map/ppermute | solution.py:346
  21.9 6.3 %collective-permute-start.12 = (bf16[208,256]{1,0:T(8,128)(2,1)S(1)}, bf16[208,256]{1,0:T(8,128)(2,1)S(1)}, u32[]{:S(2)}, u32[]{:S(2)}) collective-permute-start(bf16[208,256]{1,0:T(8,128)(2,1)S(1)} %collective-permute-done.4.refs_5_), channel_id=1, source_target_pairs={{0,2},{2,0},{1,3},{3,1},{4,6},{6,4},{5,7},{7,5},{8,10},{10,8},{9,1... | collective-permute-start | bytes 319496 | tf_op jit(solution)/shard_map/ppermute | solution.py:346
  22.4 5.8 %collective-permute-start.6 = (bf16[208,256]{1,0:T(8,128)(2,1)S(1)}, bf16[208,256]{1,0:T(8,128)(2,1)S(1)}, u32[]{:S(2)}, u32[]{:S(2)}) collective-permute-start(bf16[208,256]{1,0:T(8,128)(2,1)S(1)} %collective-permute-done.4.refs_5_), channel_id=1, source_target_pairs={{0,1},{1,0},{2,3},{3,2},{4,5},{5,4},{6,7},{7,6},{8,9},{9,8},{10,11... | collective-permute-start | bytes 319496 | tf_op jit(solution)/shard_map/ppermute | solution.py:346
  22.4 8.9 %collective-permute-start.9 = (bf16[208,256]{1,0:T(8,128)(2,1)S(1)}, bf16[208,256]{1,0:T(8,128)(2,1)S(1)}, u32[]{:S(2)}, u32[]{:S(2)}) collective-permute-start(bf16[208,256]{1,0:T(8,128)(2,1)S(1)} %collective-permute-done.7.refs_8_), channel_id=1, source_target_pairs={{0,1},{1,0},{2,3},{3,2},{4,5},{5,4},{6,7},{7,6},{8,9},{9,8},{10,11... | collective-permute-start | bytes 319496 | tf_op jit(solution)/shard_map/ppermute | solution.py:346
  24.0 9.4 %collective-permute-start.10 = (bf16[208,256]{1,0:T(8,128)(2,1)S(1)}, bf16[208,256]{1,0:T(8,128)(2,1)S(1)}, u32[]{:S(2)}, u32[]{:S(2)}) collective-permute-start(bf16[208,256]{1,0:T(8,128)(2,1)S(1)} %collective-permute-done.8.refs_9_), channel_id=1, source_target_pairs={{0,1},{1,0},{2,3},{3,2},{4,5},{5,4},{6,7},{7,6},{8,9},{9,8},{10,11... | collective-permute-start | bytes 319496 | tf_op jit(solution)/shard_map/ppermute | solution.py:346
  26.3 9.0 %collective-permute-start.13 = (bf16[208,256]{1,0:T(8,128)(2,1)S(1)}, bf16[208,256]{1,0:T(8,128)(2,1)S(1)}, u32[]{:S(2)}, u32[]{:S(2)}) collective-permute-start(bf16[208,256]{1,0:T(8,128)(2,1)S(1)} %collective-permute-done.11.refs_12_), channel_id=1, source_target_pairs={{0,1},{1,0},{2,3},{3,2},{4,5},{5,4},{6,7},{7,6},{8,9},{9,8},{10,11... | collective-permute-start | bytes 319496 | tf_op jit(solution)/shard_map/ppermute | solution.py:346
  28.2 7.1 %collective-permute-start.14 = (bf16[208,256]{1,0:T(8,128)(2,1)S(1)}, bf16[208,256]{1,0:T(8,128)(2,1)S(1)}, u32[]{:S(2)}, u32[]{:S(2)}) collective-permute-start(bf16[208,256]{1,0:T(8,128)(2,1)S(1)} %collective-permute-done.12.refs_13_), channel_id=1, source_target_pairs={{0,1},{1,0},{2,3},{3,2},{4,5},{5,4},{6,7},{7,6},{8,9},{9,8},{10,11... | collective-permute-start | bytes 319496 | tf_op jit(solution)/shard_map/ppermute | solution.py:346
  31.3 5.4 %collective-permute-start.15 = (f32[8,128]{1,0:T(8,128)S(1)}, f32[8,128]{1,0:T(8,128)S(1)}, u32[]{:S(2)}, u32[]{:S(2)}) collective-permute-start(f32[8,128]{1,0:T(8,128)S(1)} %forward.1), channel_id=1, source_target_pairs={{0,4},{4,8},{8,12},{12,0},{1,5},{5,9},{9,13},{13,1},{2,6},{6,10},{... | collective-permute-start | bytes 12296 | tf_op jit(solution)/shard_map/ppermute | solution.py:346
  31.3 5.4 %collective-permute-start.16 = (f32[8,128]{1,0:T(8,128)S(1)}, f32[8,128]{1,0:T(8,128)S(1)}, u32[]{:S(2)}, u32[]{:S(2)}) collective-permute-start(f32[8,128]{1,0:T(8,128)S(1)} %forward.1), channel_id=1, source_target_pairs={{0,8},{4,12},{8,0},{12,4},{1,9},{5,13},{9,1},{13,5},{2,10},{6,14},... | collective-permute-start | bytes 12296 | tf_op jit(solution)/shard_map/ppermute | solution.py:346
  33.4 3.9 %collective-permute-start.17 = (f32[8,128]{1,0:T(8,128)S(1)}, f32[8,128]{1,0:T(8,128)S(1)}, u32[]{:S(2)}, u32[]{:S(2)}) collective-permute-start(f32[8,128]{1,0:T(8,128)S(1)} %forward.1), channel_id=1, source_target_pairs={{0,12},{4,0},{8,4},{12,8},{1,13},{5,1},{9,5},{13,9},{2,14},{6,2},{... | collective-permute-start | bytes 12296 | tf_op jit(solution)/shard_map/ppermute | solution.py:346
  37.3 3.6 %collective-permute-start.18 = (f32[8,128]{1,0:T(8,128)S(1)}, f32[8,128]{1,0:T(8,128)S(1)}, u32[]{:S(2)}, u32[]{:S(2)}) collective-permute-start(f32[8,128]{1,0:T(8,128)S(1)} %add_add_fusion.refs_0_), channel_id=1, source_target_pairs={{0,2},{2,0},{1,3},{3,1},{4,6},{6,4},{5,7},{7,5},{8,10},{10,8},{9,1... | collective-permute-start | bytes 12296 | tf_op jit(solution)/shard_map/ppermute | solution.py:346

commit v4 on v3

--- a/solution.py
+++ b/solution.py
@@ -122,11 +122,10 @@
     height = up(receptors + 3, 8)
 
     def put(x, at):
-        x = x.astype(F32)
         return jnp.pad(x, ((at, height - at - x.shape[0]), (0, ids - x.shape[1])))
 
-    small = put(blocks, 0) + put(placement[None], receptors)
-    small = small + put(hour_start[None], receptors + 1) + put(obs_weight[None], receptors + 2)
+    small = put(blocks, 0) + put(placement[None], receptors) + put(hour_start[None], receptors + 1)
+    small = small.astype(F32) + put(obs_weight[None], receptors + 2)
     vm = pl.BlockSpec(memory_space=pltpu.VMEM)
     return pl.pallas_call(
         functools.partial(pack_kernel, cfg),
@@ -192,10 +191,31 @@
     )(x, first)
 
 
+def stack_kernel(count, *refs):
+    out_ref, at = refs[-1], 0
+    for ref in refs[:count]:
+        out_ref[at : at + ref.shape[0], :] = ref[...]
+        at += ref.shape[0]
+
+
+def stack(bufs, *unread):
+    vm = pl.BlockSpec(memory_space=pltpu.VMEM)
+    rows = sum(b.shape[0] for b in bufs)
+    return pl.pallas_call(
+        functools.partial(stack_kernel, len(bufs)),
+        out_shape=jax.ShapeDtypeStruct((rows, bufs[0].shape[1]), BF16),
+        in_specs=[vm] * (len(bufs) + len(unread)),
+        out_specs=vm,
+        compiler_params=pltpu.CompilerParams(vmem_limit_bytes=16 * 1024 * 1024),
+        cost_estimate=pl.CostEstimate(flops=0, bytes_accessed=0, transcendentals=0),
+        name="stack",
+    )(*bufs, *unread)
+
+
 def forward_kernel(cfg, counts, *refs):
     local, k, rows, capp = cfg["local"], cfg["k_core"], cfg["rows"], cfg["capp"]
     half = cfg["n"] // 2 * capp
-    probes_ref, out_ref, f8_ref = refs[-3:]
+    out_ref, f8_ref = refs[-2:]
     at = 0
     firsts = []
     for i, sides_n in enumerate(counts):
@@ -206,6 +226,7 @@
         metas = [load_meta(cfg, placed) for placed in sides]
         spread_hours(cfg, sides, metas, f8_ref, i * half)
         firsts.append(metas[0][0:8])
+    probes_ref = refs[at]
     meta = jnp.concatenate(firsts, axis=1)
     used = meta.shape[1]
     own = iota((local, used), 0) + 1 == meta[0:1].astype(I32)
@@ -222,7 +243,7 @@
     )
 
 
-def forward(cfg, own, probes_t, out_shape):
+def forward(cfg, own, probes_t, out_shape, unread):
     n, capp, hours, cells = cfg["n"], cfg["capp"], cfg["hours"], cfg["cells"]
     args = [b for half in own for side in half for b in side]
     counts = [[len(side) for side in half] for half in own]
@@ -230,34 +251,35 @@
     return pl.pallas_call(
         functools.partial(forward_kernel, cfg, counts),
         out_shape=jax.ShapeDtypeStruct(out_shape, F32),
-        in_specs=[vm] * (len(args) + 1),
+        in_specs=[vm] * (len(args) + 1) + [pl.BlockSpec(memory_space=pl.ANY)] * len(unread),
         out_specs=vm,
         scratch_shapes=[pltpu.VMEM((n * capp, hours * cells), BF16)],
         compiler_params=pltpu.CompilerParams(vmem_limit_bytes=VMEM_LIMIT),
         cost_estimate=pl.CostEstimate(flops=0, bytes_accessed=FORWARD_BYTES, transcendentals=0),
         name="forward",
-    )(*args, probes_t)
+    )(*args, probes_t, *unread)
 
 
 def prepare_kernel(cfg, counts, *refs):
     n, capp = cfg["n"], cfg["capp"]
-    f8_ref, meta_ref, zero_ref = refs[-3:]
-    zero_ref[...] = jnp.zeros_like(zero_ref)
+    f8_ref, meta_ref = refs[-2:]
     at = 0
     for c, halves in enumerate(counts):
         metas = []
-        for i, sides_n in enumerate(halves):
-            sides = []
-            for count in sides_n:
-                sides.append(slots_of(refs[at : at + count], cfg["rows"]))
+        whole = [[] for _ in halves[0]]
+        for sides_n in halves:
+            for side, count in enumerate(sides_n):
+                whole[side] += slots_of(refs[at : at + count], cfg["rows"])
                 at += count
+        for i in range(2):
+            sides = [side[i * n // 2 : (i + 1) * n // 2] for side in whole]
             side_metas = [load_meta(cfg, placed) for placed in sides]
             spread_hours(cfg, sides, side_metas, f8_ref, (2 * c + i) * (n // 2) * capp)
             metas.append(side_metas[0][0:8])
         meta_ref[:, c * n * capp : (c + 1) * n * capp] = jnp.concatenate(metas, axis=1)
 
 
-def prepare(cfg, columns, zero_shape):
+def prepare(cfg, columns):
     n, capp, hours, cells = cfg["n"], cfg["capp"], cfg["hours"], cfg["cells"]
     total = len(columns) * n * capp
     args = [b for halves in columns for sides in halves for side in sides for b in side]
@@ -268,10 +290,9 @@
         out_shape=[
             jax.ShapeDtypeStruct((total, hours * cells), BF16),
             jax.ShapeDtypeStruct((8, total), F32),
-            jax.ShapeDtypeStruct(zero_shape, F32),
         ],
         in_specs=[vm] * len(args),
-        out_specs=[vm] * 3,
+        out_specs=[vm] * 2,
         compiler_params=pltpu.CompilerParams(vmem_limit_bytes=VMEM_LIMIT),
         cost_estimate=pl.CostEstimate(flops=0, bytes_accessed=6 * total * hours * cells, transcendentals=0),
         name="prepare",
@@ -367,20 +388,24 @@
         return [half] + [[shift(b, "tm", s) for b in half] for s in range(1, ntm)]
 
     mine = after(outs[0], probes_t)
-    bufs = [mine] + [shift(outs[d], "rcp", d) for d in range(1, n)]
+    arrived = [shift(outs[d], "rcp", d) for d in range(1, n)]
+    bufs = [mine] + arrived
     halves = [bufs[: n // 2], bufs[n // 2 :]]
     if n > 4:
         halves = [[jnp.concatenate(half, axis=0)] for half in halves]
     own = [with_cores(half) for half in halves]
-    partial = forward(cfg, own, probes_t, (8, up(n * receptors, 128)))
+    others = stack(arrived)
+    first = [shift(mine, "reg", g) for g in range(1, nreg)]
+    partial = forward(cfg, own, probes_t, (8, up(n * receptors, 128)), first)
+    second = [shift(others, "reg", g) for g in range(1, nreg)]
+    observed = partial
+    for d in range(1, n):
+        observed = observed + shift(partial, "rcp", d)
     columns = [own]
     for g in range(1, nreg):
-        across = [[shift(b, "reg", g) for b in half] for half in halves]
-        columns.append([with_cores(half) for half in across])
-    f8, meta, zero = prepare(cfg, columns, partial.shape)
-    observed = partial + zero
-    for d in range(1, n):
-        observed = observed + shift(partial, "rcp", d)
+        across = stack([first[g - 1], second[g - 1]], observed)
+        columns.append([with_cores([across])])
+    f8, meta = prepare(cfg, columns)
     observed = [[shift(observed, "reg", g) if g else observed] for g in range(nreg)]
     result = adjoint(cfg, where, f8, meta, observed)
     return result.reshape(local, hours, kd * cells)

time: 44.9 us -> 38.5 us (0.86)
  starting transfers between devices: 18.1 us -> 15.7 us
  waiting for transfers between devices: 10.3 us -> 8.29 us
  other arithmetic: 2.79 us -> 0.84 us
    ppermute x19 -> x14, starting transfers between devices: 18.1 us -> 15.7 us  [shift(): return lax.ppermute(x, axis, [(i, (i + d) % n) for i in range(n)])]
    ppermute x19 -> x14, waiting for transfers between devices: 10.3 us -> 8.29 us  [shift(): return lax.ppermute(x, axis, [(i, (i + d) % n) for i in range(n)])]
    convert_element_type x3 -> x0, other arithmetic: 2.04 us -> none  [put(): x = x.astype(F32)]
  transfers between devices with their start and end apart: 19 -> 14, of which waited for: 8 -> 7; matrix products, arithmetic and copies ran while one was open for 6% -> 7% of each run, Pallas kernels for 10% -> 11%
where the time goes in v4:
time: 38.5 us; the launch traced here: 38.2 us
  starting transfers between devices  15.7 us (41%)
  Pallas kernels  9.69 us (25%)
  waiting for transfers between devices  8.29 us (22%)
  local copies, waits for them, and re-layouts  3.66 us (10%)
  other arithmetic  0.84 us (2%)
    ppermute x14, starting transfers between devices, shift(): return lax.ppermute(x, axis, [(i, (i + d) % n) for i in range(n)])  15.7 us
    ppermute x14, waiting for transfers between devices, shift(): return lax.ppermute(x, axis, [(i, (i + d) % n) for i in range(n)])  8.29 us
    pallas_call x1, Pallas kernels, adjoint(): pl.pallas_call(functools.partial(adjoint_kernel, cfg, parts), out_shape=j...  3.66 us
    pallas_call x1, Pallas kernels, forward(): pl.pallas_call(functools.partial(forward_kernel, cfg, counts), out_shape=...  3.15 us
    dynamic_slice x2, local copies, waits for them, and re-layouts, shards(): lax.dynamic_index_in_dim(probes.reshape(local, hours, nreg, ntm, kd, cell...  1.93 us
    pallas_call x1, Pallas kernels, pack(): pl.pallas_call(functools.partial(pack_kernel, cfg), out_shape=[jax.ShapeD...  1.62 us
    pallas_call x1, Pallas kernels, prepare(): pl.pallas_call(functools.partial(prepare_kernel, cfg, counts), out_shape=...  1.2 us
    reshape x1, local copies, waits for them, and re-layouts, pack(): footprint.reshape(receptors * slots * w2, cells)  1.05 us
  transfers between devices with their start and end apart: 14, of which 7 were waited for; matrix products, arithmetic and copies ran while one was open for 7% of the time, Pallas kernels for 11%

profile of v4, /device:TPU:0, one launch (start us, length us, event | category | flops | bytes accessed | tf_op | source)
XLA Modules:
  0.0 38.2 jit_solution(18120251622020513629)
XLA Ops:
  0.0 1.1 %reshape.12.fp_ref = bf16[512,256]{1,0:T(8,128)(2,1)S(1)} reshape(bf16[16,16,2,256]{3,2,1,0:T(2,128)(2,1)} %param.7) | data formatting | bytes 524288 | tf_op jit(solution)/shard_map/reshape | solution.py:137
  1.1 0.1 pad_add_fusion.1.where_ref
  1.1 0.8 %pad_add_fusion.small_ref = f32[24,512]{1,0:T(8,128)S(1)} fusion(f32[1,16]{1,0:T(1,128)} %bitcast.19, s32[1,16]{1,0:T(1,128)} %bitcast.20, s32[1,512]{1,0:T(1,128)} %bitcast.18, s32[16,16]{1,0:T(8,128)} %param.8), kind=kLoop, calls=%fused_computation | loop fusion | flops 49152 | bytes 52352 | tf_op jit(solution)/shard_map/add | solution.py:128
  1.9 1.6 %pack.1 = (bf16[208,256]{1,0:T(8,128)(2,1)S(1)}, bf16[208,256]{1,0:T(8,128)(2,1)S(1)}, bf16[208,256]{1,0:T(8,128)(2,1)S(1)}, bf16[208,256]{1,0:T(8,128)(2,1)S(1)}) custom-call(s32[3]{0:T(128)S(1)} %pad_add_fusion.1.where_ref, f32[24,512]{1,0:T(8,128)S(1)} %pad_add_fusion.small_ref, bf16[512,256]{1,0:T(8,128)(2,1)S(1)} %reshape.12.fp_ref), custom_call_target="tpu_custom_call" | custom-call | tf_op jit(solution)/shard_map/pack/pallas_call | solution.py:130
  3.5 3.1 %collective-permute-start = (bf16[208,256]{1,0:T(8,128)(2,1)S(1)}, bf16[208,256]{1,0:T(8,128)(2,1)S(1)}, u32[]{:S(2)}, u32[]{:S(2)}) collective-permute-start(bf16[208,256]{1,0:T(8,128)(2,1)S(1)} %get-tuple-element.12), channel_id=1, source_target_pairs={{0,4},{4,8},{8,12},{12,0},{1,5},{5,9},{9,13},{13,1},{2,6},{6,10},{... | collective-permute-start | bytes 319496 | tf_op jit(solution)/shard_map/ppermute | solution.py:367
  6.6 2.6 %collective-permute-start.3 = (bf16[208,256]{1,0:T(8,128)(2,1)S(1)}, bf16[208,256]{1,0:T(8,128)(2,1)S(1)}, u32[]{:S(2)}, u32[]{:S(2)}) collective-permute-start(bf16[208,256]{1,0:T(8,128)(2,1)S(1)} %get-tuple-element.13), channel_id=1, source_target_pairs={{0,8},{4,12},{8,0},{12,4},{1,9},{5,13},{9,1},{13,5},{2,10},{6,14},... | collective-permute-start | bytes 319496 | tf_op jit(solution)/shard_map/ppermute | solution.py:367
  9.2 1.3 %collective-permute-start.4 = (bf16[208,256]{1,0:T(8,128)(2,1)S(1)}, bf16[208,256]{1,0:T(8,128)(2,1)S(1)}, u32[]{:S(2)}, u32[]{:S(2)}) collective-permute-start(bf16[208,256]{1,0:T(8,128)(2,1)S(1)} %get-tuple-element.14), channel_id=1, source_target_pairs={{0,12},{4,0},{8,4},{12,8},{1,13},{5,1},{9,5},{13,9},{2,14},{6,2},{... | collective-permute-start | bytes 319496 | tf_op jit(solution)/shard_map/ppermute | solution.py:367
  10.5 1.8 %constant_dynamic-slice_fusion = bf16[128,8,2,1,2,256]{5,1,4,3,2,0:T(8,128)(2,1)S(1)} fusion(bf16[128,8,2,2,2,256]{5,1,4,3,2,0:T(8,128)(2,1)} %bitcast.17, s32[]{:T(128)S(6)} %select_n.4), kind=kLoop, calls=%fused_computation.3 | loop fusion | bytes 4194308 | tf_op jit(solution)/shard_map/jit(dynamic_index_in_dim)/dynamic_slice | solution.py:384
  12.3 0.1 copy.7
  12.5 0.7 %copy.8 = bf16[64,8,8,256]{3,1,2,0:T(8,128)(2,1)S(1)} copy(bf16[64,8,8,256]{3,2,1,0:T(8,128)(2,1)S(1)} %bitcast.16) | data formatting | bytes 4194304
  13.2 1.6 %collective-permute-start.7 = (bf16[208,256]{1,0:T(8,128)(2,1)S(1)}, bf16[208,256]{1,0:T(8,128)(2,1)S(1)}, u32[]{:S(2)}, u32[]{:S(2)}) collective-permute-start(bf16[208,256]{1,0:T(8,128)(2,1)S(1)} %after.1.refs_0_), channel_id=1, source_target_pairs={{0,2},{2,0},{1,3},{3,1},{4,6},{6,4},{5,7},{7,5},{8,10},{10,8},{9,1... | collective-permute-start | bytes 319496 | tf_op jit(solution)/shard_map/ppermute | solution.py:367
  14.7 0.0 collective-permute-start.1
  14.7 0.0 collective-permute-done.refs_0_.refs_1_
  14.7 0.5 %collective-permute-start.2 = (bf16[208,256]{1,0:T(8,128)(2,1)S(1)}, bf16[208,256]{1,0:T(8,128)(2,1)S(1)}, u32[]{:S(2)}, u32[]{:S(2)}) collective-permute-start(bf16[208,256]{1,0:T(8,128)(2,1)S(1)} %collective-permute-done.refs_0_.refs_1_), channel_id=1, source_target_pairs={{0,1},{1,0},{2,3},{3,2},{4,5},{5,4},{6,7},{7,6},{8,9},{9,8},{10,11... | collective-permute-start | bytes 319496 | tf_op jit(solution)/shard_map/ppermute | solution.py:367
  15.3 1.0 %collective-permute-done.3.refs_1_.refs_4_ = bf16[208,256]{1,0:T(8,128)(2,1)S(1)} collective-permute-done((bf16[208,256]{1,0:T(8,128)(2,1)S(1)}, bf16[208,256]{1,0:T(8,128)(2,1)S(1)}, u32[]{:S(2)}, u32[]{:S(2)}) %collective-permute-start.3) | collective-permute-done | bytes 106528 | tf_op jit(solution)/shard_map/ppermute | solution.py:367
  16.3 0.0 collective-permute-start.5
  16.3 0.0 collective-permute-done.4.refs_2_.refs_5_
  16.3 0.5 %collective-permute-start.6 = (bf16[208,256]{1,0:T(8,128)(2,1)S(1)}, bf16[208,256]{1,0:T(8,128)(2,1)S(1)}, u32[]{:S(2)}, u32[]{:S(2)}) collective-permute-start(bf16[208,256]{1,0:T(8,128)(2,1)S(1)} %collective-permute-done.4.refs_2_.refs_5_), channel_id=1, source_target_pairs={{0,1},{1,0},{2,3},{3,2},{4,5},{5,4},{6,7},{7,6},{8,9},{9,8},{10,11... | collective-permute-start | bytes 319496 | tf_op jit(solution)/shard_map/ppermute | solution.py:367
  16.8 1.1 %collective-permute-done.7.refs_9_.refs_0_ = bf16[208,256]{1,0:T(8,128)(2,1)S(1)} collective-permute-done((bf16[208,256]{1,0:T(8,128)(2,1)S(1)}, bf16[208,256]{1,0:T(8,128)(2,1)S(1)}, u32[]{:S(2)}, u32[]{:S(2)}) %collective-permute-start.7) | collective-permute-done | bytes 106528 | tf_op jit(solution)/shard_map/ppermute | solution.py:367
  18.0 1.5 %collective-permute-start.8 = (bf16[624,256]{1,0:T(8,128)(2,1)S(1)}, bf16[624,256]{1,0:T(8,128)(2,1)S(1)}, u32[]{:S(2)}, u32[]{:S(2)}) collective-permute-start(bf16[624,256]{1,0:T(8,128)(2,1)S(1)} %stack.18), channel_id=1, source_target_pairs={{0,2},{2,0},{1,3},{3,1},{4,6},{6,4},{5,7},{7,5},{8,10},{10,8},{9,1... | collective-permute-start | bytes 958472 | tf_op jit(solution)/shard_map/ppermute | solution.py:367
  19.4 0.0 collective-permute-done.1.refs_2_
  19.4 0.0 collective-permute-done.2.refs_3_
  19.5 0.0 collective-permute-done.5.refs_6_
  19.5 0.0 collective-permute-done.6.refs_7_
  19.5 3.2 %forward.1 = f32[8,128]{1,0:T(8,128)S(1)} custom-call(bf16[208,256]{1,0:T(8,128)(2,1)S(1)} %after.1.refs_0_, bf16[208,256]{1,0:T(8,128)(2,1)S(1)} %collective-permute-done.refs_0_.refs_1_, bf16[208,256]{1,0:T(8,128)(2,1)S(1)} %collective-permute-done.1.refs_2_, bf16[208,256]{1,0:T(8,128)(2,1)S(1)} %collective-permute-done.2.refs_3_, ...), custom_call_target="tpu_custom_call" | custom-call | tf_op jit(solution)/shard_map/forward/pallas_call | solution.py:251
  22.6 2.8 %collective-permute-start.11 = (f32[8,128]{1,0:T(8,128)S(1)}, f32[8,128]{1,0:T(8,128)S(1)}, u32[]{:S(2)}, u32[]{:S(2)}) collective-permute-start(f32[8,128]{1,0:T(8,128)S(1)} %forward.1), channel_id=1, source_target_pairs={{0,12},{4,0},{8,4},{12,8},{1,13},{5,1},{9,5},{13,9},{2,14},{6,2},{... | collective-permute-start | bytes 12296 | tf_op jit(solution)/shard_map/ppermute | solution.py:367
  25.4 0.0 collective-permute-start.10
  25.4 0.6 %collective-permute-start.9 = (f32[8,128]{1,0:T(8,128)S(1)}, f32[8,128]{1,0:T(8,128)S(1)}, u32[]{:S(2)}, u32[]{:S(2)}) collective-permute-start(f32[8,128]{1,0:T(8,128)S(1)} %forward.1), channel_id=1, source_target_pairs={{0,4},{4,8},{8,12},{12,0},{1,5},{5,9},{9,13},{13,1},{2,6},{6,10},{... | collective-permute-start | bytes 12296 | tf_op jit(solution)/shard_map/ppermute | solution.py:367
  25.9 0.8 %collective-permute-done.11 = f32[8,128]{1,0:T(8,128)S(1)} collective-permute-done((f32[8,128]{1,0:T(8,128)S(1)}, f32[8,128]{1,0:T(8,128)S(1)}, u32[]{:S(2)}, u32[]{:S(2)}) %collective-permute-start.11) | collective-permute-done | bytes 4128 | tf_op jit(solution)/shard_map/ppermute | solution.py:367
  26.7 3.2 %collective-permute-done.10 = f32[8,128]{1,0:T(8,128)S(1)} collective-permute-done((f32[8,128]{1,0:T(8,128)S(1)}, f32[8,128]{1,0:T(8,128)S(1)}, u32[]{:S(2)}, u32[]{:S(2)}) %collective-permute-start.10) | collective-permute-done | bytes 4128 | tf_op jit(solution)/shard_map/ppermute | solution.py:367
  29.9 0.9 %collective-permute-done.9 = f32[8,128]{1,0:T(8,128)S(1)} collective-permute-done((f32[8,128]{1,0:T(8,128)S(1)}, f32[8,128]{1,0:T(8,128)S(1)}, u32[]{:S(2)}, u32[]{:S(2)}) %collective-permute-start.9) | collective-permute-done | bytes 4128 | tf_op jit(solution)/shard_map/ppermute | solution.py:367
  30.8 0.0 collective-permute-done.8.refs_1_
  30.8 0.1 collective-permute-start.12
  30.9 1.2 %collective-permute-start.13 = (f32[8,128]{1,0:T(8,128)S(1)}, f32[8,128]{1,0:T(8,128)S(1)}, u32[]{:S(2)}, u32[]{:S(2)}) collective-permute-start(f32[8,128]{1,0:T(8,128)S(1)} %add_add_fusion.refs_2_.refs_0_), channel_id=1, source_target_pairs={{0,2},{2,0},{1,3},{3,1},{4,6},{6,4},{5,7},{7,5},{8,10},{10,8},{9,1... | collective-permute-start | bytes 12296 | tf_op jit(solution)/shard_map/ppermute | solution.py:367
  32.1 0.6 %collective-permute-done.12.refs_9_ = bf16[832,256]{1,0:T(8,128)(2,1)S(1)} collective-permute-done((bf16[832,256]{1,0:T(8,128)(2,1)S(1)}, bf16[832,256]{1,0:T(8,128)(2,1)S(1)}, u32[]{:S(2)}, u32[]{:S(2)}) %collective-permute-start.12) | collective-permute-done | bytes 426016 | tf_op jit(solution)/shard_map/ppermute | solution.py:367
  32.7 1.2 %prepare.1 = (bf16[768,2048]{1,0:T(8,128)(2,1)S(1)}, f32[8,768]{1,0:T(8,128)S(1)}) custom-call(bf16[208,256]{1,0:T(8,128)(2,1)S(1)} %after.1.refs_0_, bf16[208,256]{1,0:T(8,128)(2,1)S(1)} %collective-permute-done.refs_0_.refs_1_, bf16[208,256]{1,0:T(8,128)(2,1)S(1)} %collective-permute-done.1.refs_2_, bf16[208,256]{1,0:T(8,128)(2,1)S(1)} %collective-permute-done.2.refs_3_, ...), custom_call_target="tpu_custom_call" | custom-call | bytes 9437184 | tf_op jit(solution)/shard_map/prepare/pallas_call | solution.py:288
  33.9 0.7 %collective-permute-done.13.refs_1_ = f32[8,128]{1,0:T(8,128)S(1)} collective-permute-done((f32[8,128]{1,0:T(8,128)S(1)}, f32[8,128]{1,0:T(8,128)S(1)}, u32[]{:S(2)}, u32[]{:S(2)}) %collective-permute-start.13) | collective-permute-done | bytes 4128 | tf_op jit(solution)/shard_map/ppermute | solution.py:367
  34.6 3.7 %adjoint.1 = f32[1024,512]{1,0:T(8,128)} custom-call(s32[3]{0:T(128)S(1)} %pad_add_fusion.1.where_ref, f32[8,768]{1,0:T(8,128)S(1)} %get-tuple-element.15.meta_ref, bf16[768,2048]{1,0:T(8,128)(2,1)S(1)} %get-tuple-element.16.f8_ref, f32[8,128]{1,0:T(8,128)S(1)} %add_add_fusion.refs_2_.refs_0_, f32[8,128]{1,0:T(8,128)S(1)} %collective-permute-done.13.refs_1_), custom_call_target="tpu_custom_call" | custom-call | tf_op jit(solution)/shard_map/adjoint/pallas_call | solution.py:350
  (4 shorter events, 0.1 us)
Async XLA Ops:
  3.5 11.2 %collective-permute-start = (bf16[208,256]{1,0:T(8,128)(2,1)S(1)}, bf16[208,256]{1,0:T(8,128)(2,1)S(1)}, u32[]{:S(2)}, u32[]{:S(2)}) collective-permute-start(bf16[208,256]{1,0:T(8,128)(2,1)S(1)} %get-tuple-element.12), channel_id=1, source_target_pairs={{0,4},{4,8},{8,12},{12,0},{1,5},{5,9},{9,13},{13,1},{2,6},{6,10},{... | collective-permute-start | bytes 319496 | tf_op jit(solution)/shard_map/ppermute | solution.py:367
  6.6 9.7 %collective-permute-start.3 = (bf16[208,256]{1,0:T(8,128)(2,1)S(1)}, bf16[208,256]{1,0:T(8,128)(2,1)S(1)}, u32[]{:S(2)}, u32[]{:S(2)}) collective-permute-start(bf16[208,256]{1,0:T(8,128)(2,1)S(1)} %get-tuple-element.13), channel_id=1, source_target_pairs={{0,8},{4,12},{8,0},{12,4},{1,9},{5,13},{9,1},{13,5},{2,10},{6,14},... | collective-permute-start | bytes 319496 | tf_op jit(solution)/shard_map/ppermute | solution.py:367
  9.2 7.1 %collective-permute-start.4 = (bf16[208,256]{1,0:T(8,128)(2,1)S(1)}, bf16[208,256]{1,0:T(8,128)(2,1)S(1)}, u32[]{:S(2)}, u32[]{:S(2)}) collective-permute-start(bf16[208,256]{1,0:T(8,128)(2,1)S(1)} %get-tuple-element.14), channel_id=1, source_target_pairs={{0,12},{4,0},{8,4},{12,8},{1,13},{5,1},{9,5},{13,9},{2,14},{6,2},{... | collective-permute-start | bytes 319496 | tf_op jit(solution)/shard_map/ppermute | solution.py:367
  13.2 4.8 %collective-permute-start.7 = (bf16[208,256]{1,0:T(8,128)(2,1)S(1)}, bf16[208,256]{1,0:T(8,128)(2,1)S(1)}, u32[]{:S(2)}, u32[]{:S(2)}) collective-permute-start(bf16[208,256]{1,0:T(8,128)(2,1)S(1)} %after.1.refs_0_), channel_id=1, source_target_pairs={{0,2},{2,0},{1,3},{3,1},{4,6},{6,4},{5,7},{7,5},{8,10},{10,8},{9,1... | collective-permute-start | bytes 319496 | tf_op jit(solution)/shard_map/ppermute | solution.py:367
  14.7 4.7 %collective-permute-start.1 = (bf16[208,256]{1,0:T(8,128)(2,1)S(1)}, bf16[208,256]{1,0:T(8,128)(2,1)S(1)}, u32[]{:S(2)}, u32[]{:S(2)}) collective-permute-start(bf16[208,256]{1,0:T(8,128)(2,1)S(1)} %after.1.refs_0_), channel_id=1, source_target_pairs={{0,1},{1,0},{2,3},{3,2},{4,5},{5,4},{6,7},{7,6},{8,9},{9,8},{10,11... | collective-permute-start | bytes 319496 | tf_op jit(solution)/shard_map/ppermute | solution.py:367
  14.7 4.7 %collective-permute-start.2 = (bf16[208,256]{1,0:T(8,128)(2,1)S(1)}, bf16[208,256]{1,0:T(8,128)(2,1)S(1)}, u32[]{:S(2)}, u32[]{:S(2)}) collective-permute-start(bf16[208,256]{1,0:T(8,128)(2,1)S(1)} %collective-permute-done.refs_0_.refs_1_), channel_id=1, source_target_pairs={{0,1},{1,0},{2,3},{3,2},{4,5},{5,4},{6,7},{7,6},{8,9},{9,8},{10,11... | collective-permute-start | bytes 319496 | tf_op jit(solution)/shard_map/ppermute | solution.py:367
  16.3 3.2 %collective-permute-start.5 = (bf16[208,256]{1,0:T(8,128)(2,1)S(1)}, bf16[208,256]{1,0:T(8,128)(2,1)S(1)}, u32[]{:S(2)}, u32[]{:S(2)}) collective-permute-start(bf16[208,256]{1,0:T(8,128)(2,1)S(1)} %collective-permute-done.3.refs_1_.refs_4_), channel_id=1, source_target_pairs={{0,1},{1,0},{2,3},{3,2},{4,5},{5,4},{6,7},{7,6},{8,9},{9,8},{10,11... | collective-permute-start | bytes 319496 | tf_op jit(solution)/shard_map/ppermute | solution.py:367
  16.3 3.2 %collective-permute-start.6 = (bf16[208,256]{1,0:T(8,128)(2,1)S(1)}, bf16[208,256]{1,0:T(8,128)(2,1)S(1)}, u32[]{:S(2)}, u32[]{:S(2)}) collective-permute-start(bf16[208,256]{1,0:T(8,128)(2,1)S(1)} %collective-permute-done.4.refs_2_.refs_5_), channel_id=1, source_target_pairs={{0,1},{1,0},{2,3},{3,2},{4,5},{5,4},{6,7},{7,6},{8,9},{9,8},{10,11... | collective-permute-start | bytes 319496 | tf_op jit(solution)/shard_map/ppermute | solution.py:367
  18.0 12.8 %collective-permute-start.8 = (bf16[624,256]{1,0:T(8,128)(2,1)S(1)}, bf16[624,256]{1,0:T(8,128)(2,1)S(1)}, u32[]{:S(2)}, u32[]{:S(2)}) collective-permute-start(bf16[624,256]{1,0:T(8,128)(2,1)S(1)} %stack.18), channel_id=1, source_target_pairs={{0,2},{2,0},{1,3},{3,1},{4,6},{6,4},{5,7},{7,5},{8,10},{10,8},{9,1... | collective-permute-start | bytes 958472 | tf_op jit(solution)/shard_map/ppermute | solution.py:367
  22.6 4.1 %collective-permute-start.11 = (f32[8,128]{1,0:T(8,128)S(1)}, f32[8,128]{1,0:T(8,128)S(1)}, u32[]{:S(2)}, u32[]{:S(2)}) collective-permute-start(f32[8,128]{1,0:T(8,128)S(1)} %forward.1), channel_id=1, source_target_pairs={{0,12},{4,0},{8,4},{12,8},{1,13},{5,1},{9,5},{13,9},{2,14},{6,2},{... | collective-permute-start | bytes 12296 | tf_op jit(solution)/shard_map/ppermute | solution.py:367
  25.4 4.5 %collective-permute-start.10 = (f32[8,128]{1,0:T(8,128)S(1)}, f32[8,128]{1,0:T(8,128)S(1)}, u32[]{:S(2)}, u32[]{:S(2)}) collective-permute-start(f32[8,128]{1,0:T(8,128)S(1)} %forward.1), channel_id=1, source_target_pairs={{0,8},{4,12},{8,0},{12,4},{1,9},{5,13},{9,1},{13,5},{2,10},{6,14},... | collective-permute-start | bytes 12296 | tf_op jit(solution)/shard_map/ppermute | solution.py:367
  25.4 5.4 %collective-permute-start.9 = (f32[8,128]{1,0:T(8,128)S(1)}, f32[8,128]{1,0:T(8,128)S(1)}, u32[]{:S(2)}, u32[]{:S(2)}) collective-permute-start(f32[8,128]{1,0:T(8,128)S(1)} %forward.1), channel_id=1, source_target_pairs={{0,4},{4,8},{8,12},{12,0},{1,5},{5,9},{9,13},{13,1},{2,6},{6,10},{... | collective-permute-start | bytes 12296 | tf_op jit(solution)/shard_map/ppermute | solution.py:367
  30.8 1.8 %collective-permute-start.12 = (bf16[832,256]{1,0:T(8,128)(2,1)S(1)}, bf16[832,256]{1,0:T(8,128)(2,1)S(1)}, u32[]{:S(2)}, u32[]{:S(2)}) collective-permute-start(bf16[832,256]{1,0:T(8,128)(2,1)S(1)} %stack.19.refs_8_), channel_id=1, source_target_pairs={{0,1},{1,0},{2,3},{3,2},{4,5},{5,4},{6,7},{7,6},{8,9},{9,8},{10,11... | collective-permute-start | bytes 1277960 | tf_op jit(solution)/shard_map/ppermute | solution.py:367
  30.9 3.7 %collective-permute-start.13 = (f32[8,128]{1,0:T(8,128)S(1)}, f32[8,128]{1,0:T(8,128)S(1)}, u32[]{:S(2)}, u32[]{:S(2)}) collective-permute-start(f32[8,128]{1,0:T(8,128)S(1)} %add_add_fusion.refs_2_.refs_0_), channel_id=1, source_target_pairs={{0,2},{2,0},{1,3},{3,1},{4,6},{6,4},{5,7},{7,5},{8,10},{10,8},{9,1... | collective-permute-start | bytes 12296 | tf_op jit(solution)/shard_map/ppermute | solution.py:367

commit v5 on v4

--- a/solution.py
+++ b/solution.py
@@ -12,6 +12,8 @@
 I32 = jnp.int32
 META = 16
 VMEM_LIMIT = 48 * 1024 * 1024
+GROUPS = ((0,), (1, 2, 3))
+EARLY = 0
 FORWARD_BYTES = 0
 
 
@@ -38,6 +40,17 @@
 
 def nn(a, b):
     return lax.dot_general(a, b, (((1,), (0,)), ((), ())), preferred_element_type=F32)
+
+
+def three(x):
+    high = x.astype(BF16).astype(F32)
+    mid = (x - high).astype(BF16).astype(F32)
+    return jnp.concatenate([high, mid, x - high - mid], axis=0).astype(BF16)
+
+
+def add_three(x):
+    rows = x.shape[0] // 3
+    return x[0:rows] + x[rows : 2 * rows] + x[2 * rows : 3 * rows]
 
 
 def pack_kernel(cfg, where_ref, small_ref, fp_ref, *outs):
@@ -233,14 +246,12 @@
     row = iota((8, used), 0)
     dots = jnp.zeros((8, used), F32)
     f8 = f8_ref[...]
+    x = nt(probes_ref[...], f8)
     for j in range(k):
-        x = nt(probes_ref[j * local : (j + 1) * local, :], f8)
-        y = jnp.sum(jnp.where(own, x, 0.0), axis=0, keepdims=True)
+        y = jnp.sum(jnp.where(own, x[j * local : (j + 1) * local], 0.0), axis=0, keepdims=True)
         dots = jnp.where(row == j, y, dots)
-    to_r = mask(iota((out_ref.shape[1], used), 0) == meta[2:3].astype(I32))
-    out_ref[...] = lax.dot_general(
-        dots, to_r, (((1,), (1,)), ((), ())), precision=lax.Precision.HIGHEST, preferred_element_type=F32
-    )
+    to_r = mask(iota((out_ref.shape[1], used), 0) == meta[2:3].astype(I32)).astype(BF16)
+    out_ref[...] = add_three(nt(three(dots), to_r))
 
 
 def forward(cfg, own, probes_t, out_shape, unread):
@@ -260,77 +271,113 @@
     )(*args, probes_t, *unread)
 
 
-def prepare_kernel(cfg, counts, *refs):
-    n, capp = cfg["n"], cfg["capp"]
-    f8_ref, meta_ref = refs[-2:]
+def prepare_kernel(cfg, column, counts, *refs):
+    n, capp, local = cfg["n"], cfg["capp"], cfg["local"]
+    f8_ref, own_ref, to_r_ref, weight_ref = refs[-4:]
+    used = n * capp
     at = 0
-    for c, halves in enumerate(counts):
-        metas = []
-        whole = [[] for _ in halves[0]]
-        for sides_n in halves:
-            for side, count in enumerate(sides_n):
-                whole[side] += slots_of(refs[at : at + count], cfg["rows"])
-                at += count
-        for i in range(2):
-            sides = [side[i * n // 2 : (i + 1) * n // 2] for side in whole]
-            side_metas = [load_meta(cfg, placed) for placed in sides]
-            spread_hours(cfg, sides, side_metas, f8_ref, (2 * c + i) * (n // 2) * capp)
-            metas.append(side_metas[0][0:8])
-        meta_ref[:, c * n * capp : (c + 1) * n * capp] = jnp.concatenate(metas, axis=1)
-
-
-def prepare(cfg, columns):
-    n, capp, hours, cells = cfg["n"], cfg["capp"], cfg["hours"], cfg["cells"]
-    total = len(columns) * n * capp
-    args = [b for halves in columns for sides in halves for side in sides for b in side]
-    counts = [[[len(side) for side in sides] for sides in halves] for halves in columns]
-    vm = pl.BlockSpec(memory_space=pltpu.VMEM)
-    return pl.pallas_call(
-        functools.partial(prepare_kernel, cfg, counts),
+    whole = [[] for _ in counts[0]]
+    for sides_n in counts:
+        for side, count in enumerate(sides_n):
+            whole[side] += slots_of(refs[at : at + count], cfg["rows"])
+            at += count
+    firsts = []
+    for i in range(2):
+        sides = [side[i * n // 2 : (i + 1) * n // 2] for side in whole]
+        metas = [load_meta(cfg, placed) for placed in sides]
+        spread_hours(cfg, sides, metas, f8_ref, column * used + i * (n // 2) * capp)
+        firsts.append(metas[0][0:8])
+    meta = jnp.concatenate(firsts, axis=1)
+    lanes = slice(column * used, (column + 1) * used)
+    own_ref[:, lanes] = mask(iota((local, used), 0) + 1 == meta[0:1].astype(I32)).astype(BF16)
+    to_r_ref[:, lanes] = mask(iota((to_r_ref.shape[0], used), 0) == meta[2:3].astype(I32)).astype(BF16)
+    weight_ref[:, lanes] = jnp.broadcast_to(meta[3:4] + meta[4:5] + meta[5:6], (8, used))
+
+
+def prepare(cfg, column, halves, columns, rp, before, *unread):
+    n, capp, hours, cells, local = cfg["n"], cfg["capp"], cfg["hours"], cfg["cells"], cfg["local"]
+    total = columns * n * capp
+    args = [b for sides in halves for side in sides for b in side]
+    counts = [[len(side) for side in sides] for sides in halves]
+    vm = pl.BlockSpec(memory_space=pltpu.VMEM)
+    return pl.pallas_call(
+        functools.partial(prepare_kernel, cfg, column, counts),
         out_shape=[
             jax.ShapeDtypeStruct((total, hours * cells), BF16),
+            jax.ShapeDtypeStruct((local, total), BF16),
+            jax.ShapeDtypeStruct((rp, total), BF16),
             jax.ShapeDtypeStruct((8, total), F32),
         ],
-        in_specs=[vm] * len(args),
-        out_specs=[vm] * 2,
+        in_specs=[vm] * (len(args) + len(before) + len(unread)),
+        out_specs=[vm] * 4,
+        input_output_aliases={len(args) + i: i for i in range(len(before))},
         compiler_params=pltpu.CompilerParams(vmem_limit_bytes=VMEM_LIMIT),
-        cost_estimate=pl.CostEstimate(flops=0, bytes_accessed=6 * total * hours * cells, transcendentals=0),
-        name="prepare",
-    )(*args)
-
-
-def adjoint_kernel(cfg, parts, where_ref, meta_ref, f8_ref, *refs):
+        cost_estimate=pl.CostEstimate(flops=0, bytes_accessed=3 * total * cells, transcendentals=0),
+        name=f"prepare{column}",
+    )(*args, *before, *unread)
+
+
+def fill_terms(cfg, reg, obs_ref, own, to_r, weight, a_ref, lanes):
+    local, kd = cfg["local"], cfg["kd"]
+    used = own.shape[1]
+    row = iota((8, used), 0)
+    per_entry = add_three(nn(three(obs_ref[...]), to_r)) * weight
+    for j in range(kd):
+        term = jnp.sum(jnp.where(row == reg * kd + j, per_entry, 0.0), axis=0, keepdims=True)
+        high = term.astype(BF16).astype(F32)
+        for p, part in enumerate((high, term - high)):
+            spread = jnp.broadcast_to(part.astype(BF16), (local, used))
+            a_ref[(2 * j + p) * local : (2 * j + p + 1) * local, lanes] = own * spread
+
+
+def own_adjoint_kernel(cfg, where_ref, f8_ref, own_ref, to_r_ref, weight_ref, obs_ref, out_ref, a_ref):
+    local, hours, cells, kd = cfg["local"], cfg["hours"], cfg["cells"], cfg["kd"]
+    fill_terms(cfg, where_ref[2], obs_ref, own_ref[...], to_r_ref[...], weight_ref[...], a_ref, slice(None))
+    a = a_ref[...]
+    for h in range(hours):
+        sums = nn(a, f8_ref[:, h * cells : (h + 1) * cells])
+        for j in range(kd):
+            both = sums[2 * j * local : (2 * j + 1) * local] + sums[(2 * j + 1) * local : (2 * j + 2) * local]
+            out_ref[j * local : (j + 1) * local, h * cells : (h + 1) * cells] = both
+
+
+def own_adjoint(cfg, where, operands, observed):
+    hours, cells, local, kd = cfg["hours"], cfg["cells"], cfg["local"], cfg["kd"]
+    total = operands[0].shape[0]
+    vm = pl.BlockSpec(memory_space=pltpu.VMEM)
+    return pl.pallas_call(
+        functools.partial(own_adjoint_kernel, cfg),
+        out_shape=jax.ShapeDtypeStruct((kd * local, hours * cells), F32),
+        in_specs=[pl.BlockSpec(memory_space=pltpu.SMEM)] + [vm] * 5,
+        out_specs=vm,
+        scratch_shapes=[pltpu.VMEM((2 * kd * local, total), BF16)],
+        compiler_params=pltpu.CompilerParams(vmem_limit_bytes=VMEM_LIMIT),
+        cost_estimate=pl.CostEstimate(
+            flops=4 * kd * local * total * hours * cells, bytes_accessed=2 * total * hours * cells, transcendentals=0
+        ),
+        name="own_adjoint",
+    )(where, *operands, observed)
+
+
+def adjoint_kernel(cfg, where_ref, before_ref, f8_ref, own_ref, to_r_ref, weight_ref, *refs):
     n, capp, local, hours, cells, kd = (
         cfg["n"], cfg["capp"], cfg["local"], cfg["hours"], cfg["cells"], cfg["kd"],
     )
     obs_refs, (out_ref, a_ref, tiles_ref, sems) = refs[:-4], refs[-4:]
     used = n * capp
     per_k = cells // 128
-    for c in range(len(obs_refs) // parts):
-        obs = obs_refs[c * parts][...]
-        for i in range(1, parts):
-            obs = obs + obs_refs[c * parts + i][...]
-        meta = meta_ref[:, c * used : (c + 1) * used]
-        to_r = mask(iota((obs.shape[1], used), 0) == meta[2:3].astype(I32))
-        per_entry = lax.dot_general(
-            obs, to_r, (((1,), (0,)), ((), ())), precision=lax.Precision.HIGHEST, preferred_element_type=F32
+    for c, obs_ref in enumerate(obs_refs):
+        lanes = slice(c * used, (c + 1) * used)
+        fill_terms(
+            cfg, where_ref[2], obs_ref, own_ref[:, lanes], to_r_ref[:, lanes], weight_ref[:, lanes], a_ref, lanes
         )
-        per_entry = per_entry * (meta[3:4] + meta[4:5] + meta[5:6])
-        own = iota((local, used), 0) + 1 == meta[0:1].astype(I32)
-        row = iota((8, used), 0)
-        for j in range(kd):
-            term = jnp.sum(jnp.where(row == where_ref[2] * kd + j, per_entry, 0.0), axis=0, keepdims=True)
-            high = term.astype(BF16).astype(F32)
-            for p, part in enumerate((high, term - high)):
-                a_ref[(2 * j + p) * local : (2 * j + p + 1) * local, c * used : (c + 1) * used] = jnp.where(
-                    own, part, 0.0
-                ).astype(BF16)
     copies = []
     for j in range(kd):
         a = a_ref[2 * j * local : 2 * (j + 1) * local, :]
         for h in range(hours):
             sums = nn(a, f8_ref[:, h * cells : (h + 1) * cells])
             both = sums[0:local] + sums[local : 2 * local]
+            both = both + before_ref[j * local : (j + 1) * local, h * cells : (h + 1) * cells]
             for t in range(per_k):
                 tiles_ref.at[j * per_k + t][pl.ds(h, local, stride=hours), :] = both[:, t * 128 : (t + 1) * 128]
         for t in range(j * per_k, (j + 1) * per_k):
@@ -341,16 +388,14 @@
         copy.wait()
 
 
-def adjoint(cfg, where, f8, meta, observed):
+def adjoint(cfg, where, before, operands, observed):
     hours, cells, local, kd = cfg["hours"], cfg["cells"], cfg["local"], cfg["kd"]
-    total = f8.shape[0]
-    parts = len(observed[0])
-    args = [o for column in observed for o in column]
-    vm = pl.BlockSpec(memory_space=pltpu.VMEM)
-    return pl.pallas_call(
-        functools.partial(adjoint_kernel, cfg, parts),
+    total = operands[0].shape[0]
+    vm = pl.BlockSpec(memory_space=pltpu.VMEM)
+    return pl.pallas_call(
+        functools.partial(adjoint_kernel, cfg),
         out_shape=jax.ShapeDtypeStruct((local * hours, kd * cells), F32),
-        in_specs=[pl.BlockSpec(memory_space=pltpu.SMEM)] + [vm] * (2 + len(args)),
+        in_specs=[pl.BlockSpec(memory_space=pltpu.SMEM)] + [vm] * (5 + len(observed)),
         out_specs=pl.BlockSpec(memory_space=pl.ANY),
         scratch_shapes=[
             pltpu.VMEM((2 * kd * local, total), BF16),
@@ -359,7 +404,7 @@
         ],
         compiler_params=pltpu.CompilerParams(vmem_limit_bytes=VMEM_LIMIT),
         name="adjoint",
-    )(where, meta, f8, *args)
+    )(where, before, *operands, *observed)
 
 
 def shift(x, axis, d):
@@ -388,26 +433,29 @@
         return [half] + [[shift(b, "tm", s) for b in half] for s in range(1, ntm)]
 
     mine = after(outs[0], probes_t)
-    arrived = [shift(outs[d], "rcp", d) for d in range(1, n)]
-    bufs = [mine] + arrived
+    bufs = [mine] + [shift(outs[d], "rcp", d) for d in range(1, n)]
+    raw = [outs[0]] + bufs[1:]
     halves = [bufs[: n // 2], bufs[n // 2 :]]
+    groups = GROUPS
     if n > 4:
         halves = [[jnp.concatenate(half, axis=0)] for half in halves]
+        raw, groups = [half[0] for half in halves], ((0,), (1,))
     own = [with_cores(half) for half in halves]
-    others = stack(arrived)
-    first = [shift(mine, "reg", g) for g in range(1, nreg)]
-    partial = forward(cfg, own, probes_t, (8, up(n * receptors, 128)), first)
-    second = [shift(others, "reg", g) for g in range(1, nreg)]
+    sent = [stack([raw[d] for d in group]) if len(group) > 1 else raw[group[0]] for group in groups]
+    across = [[shift(b, "reg", g) for b in sent] for g in range(1, nreg)]
+    rp = up(n * receptors, 128)
+    partial = forward(cfg, own, probes_t, (8, rp), [b for group in across for b in group[:EARLY]])
     observed = partial
     for d in range(1, n):
         observed = observed + shift(partial, "rcp", d)
-    columns = [own]
-    for g in range(1, nreg):
-        across = stack([first[g - 1], second[g - 1]], observed)
-        columns.append([with_cores([across])])
-    f8, meta = prepare(cfg, columns)
-    observed = [[shift(observed, "reg", g) if g else observed] for g in range(nreg)]
-    result = adjoint(cfg, where, f8, meta, observed)
+    operands = prepare(cfg, 0, own, 1, rp, [], partial)
+    before = own_adjoint(cfg, where, operands, observed)
+    gate, operands = operands[3], []
+    for g, group in enumerate(across):
+        group = stack(group, observed, gate)
+        operands = prepare(cfg, g, [with_cores([group])], nreg - 1, rp, operands)
+    observed = [shift(observed, "reg", g) for g in range(1, nreg)]
+    result = adjoint(cfg, where, before, operands, observed)
     return result.reshape(local, hours, kd * cells)
 
 

time: 38.5 us -> 36.9 us (0.958)
  waiting for transfers between devices: 8.29 us -> 5.74 us
  starting transfers between devices: 15.7 us -> 16.2 us
  Pallas kernels: 9.69 us -> 10.1 us
    ppermute x14, waiting for transfers between devices: 8.29 us -> 5.74 us  [shift(): return lax.ppermute(x, axis, [(i, (i + d) % n) for i in range(n)])]
    pallas_call x2 -> x4, Pallas kernels: 4.86 us -> 6.41 us  [the longest x1 3.04 us: adjoint(): pl.pallas_call(functools.partial(adjoint_kernel, cfg), out_shape=jax.Shap...]
    pallas_call x1, Pallas kernels: 3.15 us -> 2.02 us  [forward(): pl.pallas_call(functools.partial(forward_kernel, cfg, counts), out_shape=...]
    ppermute x14, starting transfers between devices: 15.7 us -> 16.2 us  [shift(): return lax.ppermute(x, axis, [(i, (i + d) % n) for i in range(n)])]
  transfers between devices with their start and end apart: 14 -> 14, of which waited for: 7 -> 3; matrix products, arithmetic and copies ran while one was open for 7% -> 7% of each run, Pallas kernels for 11% -> 15%
where the time goes in v5:
time: 36.9 us; the launch traced here: 36.7 us
  starting transfers between devices  16.2 us (44%)
  Pallas kernels  10.1 us (27%)
  waiting for transfers between devices  5.74 us (16%)
  local copies, waits for them, and re-layouts  3.66 us (10%)
  other arithmetic  0.84 us (2%)
    ppermute x14, starting transfers between devices, shift(): return lax.ppermute(x, axis, [(i, (i + d) % n) for i in range(n)])  16.2 us
    ppermute x14, waiting for transfers between devices, shift(): return lax.ppermute(x, axis, [(i, (i + d) % n) for i in range(n)])  5.74 us
    pallas_call x1, Pallas kernels, adjoint(): pl.pallas_call(functools.partial(adjoint_kernel, cfg), out_shape=jax.Shap...  3.04 us
    pallas_call x1, Pallas kernels, forward(): pl.pallas_call(functools.partial(forward_kernel, cfg, counts), out_shape=...  2.02 us
    dynamic_slice x2, local copies, waits for them, and re-layouts, shards(): lax.dynamic_index_in_dim(probes.reshape(local, hours, nreg, ntm, kd, cell...  1.93 us
    pallas_call x1, Pallas kernels, own_adjoint(): pl.pallas_call(functools.partial(own_adjoint_kernel, cfg), out_shape=jax....  1.9 us
    pallas_call x1, Pallas kernels, pack(): pl.pallas_call(functools.partial(pack_kernel, cfg), out_shape=[jax.ShapeD...  1.62 us
    pallas_call x2, Pallas kernels, prepare(): pl.pallas_call(functools.partial(prepare_kernel, cfg, column, counts), ou...  1.47 us
  transfers between devices with their start and end apart: 14, of which 3 were waited for; matrix products, arithmetic and copies ran while one was open for 7% of the time, Pallas kernels for 15%

profile of v5, /device:TPU:0, one launch (start us, length us, event | category | flops | bytes accessed | tf_op | source)
XLA Modules:
  0.0 36.7 jit_solution(6744045386485048899)
XLA Ops:
  0.0 1.1 %reshape.12.fp_ref = bf16[512,256]{1,0:T(8,128)(2,1)S(1)} reshape(bf16[16,16,2,256]{3,2,1,0:T(2,128)(2,1)} %param.7) | data formatting | bytes 524288 | tf_op jit(solution)/shard_map/reshape | solution.py:150
  1.1 0.1 pad_add_fusion.1.where_ref
  1.1 0.8 %pad_add_fusion.small_ref = f32[24,512]{1,0:T(8,128)S(1)} fusion(f32[1,16]{1,0:T(1,128)} %bitcast.19, s32[1,16]{1,0:T(1,128)} %bitcast.20, s32[1,512]{1,0:T(1,128)} %bitcast.18, s32[16,16]{1,0:T(8,128)} %param.8), kind=kLoop, calls=%fused_computation | loop fusion | flops 49152 | bytes 52352 | tf_op jit(solution)/shard_map/add | solution.py:141
  1.9 1.6 %pack.1 = (bf16[208,256]{1,0:T(8,128)(2,1)S(1)}, bf16[208,256]{1,0:T(8,128)(2,1)S(1)}, bf16[208,256]{1,0:T(8,128)(2,1)S(1)}, bf16[208,256]{1,0:T(8,128)(2,1)S(1)}) custom-call(s32[3]{0:T(128)S(1)} %pad_add_fusion.1.where_ref, f32[24,512]{1,0:T(8,128)S(1)} %pad_add_fusion.small_ref, bf16[512,256]{1,0:T(8,128)(2,1)S(1)} %reshape.12.fp_ref), custom_call_target="tpu_custom_call" | custom-call | tf_op jit(solution)/shard_map/pack/pallas_call | solution.py:143
  3.5 3.1 %collective-permute-start = (bf16[208,256]{1,0:T(8,128)(2,1)S(1)}, bf16[208,256]{1,0:T(8,128)(2,1)S(1)}, u32[]{:S(2)}, u32[]{:S(2)}) collective-permute-start(bf16[208,256]{1,0:T(8,128)(2,1)S(1)} %get-tuple-element.18), channel_id=1, source_target_pairs={{0,4},{4,8},{8,12},{12,0},{1,5},{5,9},{9,13},{13,1},{2,6},{6,10},{... | collective-permute-start | bytes 319496 | tf_op jit(solution)/shard_map/ppermute | solution.py:412
  6.6 2.6 %collective-permute-start.3 = (bf16[208,256]{1,0:T(8,128)(2,1)S(1)}, bf16[208,256]{1,0:T(8,128)(2,1)S(1)}, u32[]{:S(2)}, u32[]{:S(2)}) collective-permute-start(bf16[208,256]{1,0:T(8,128)(2,1)S(1)} %get-tuple-element.19), channel_id=1, source_target_pairs={{0,8},{4,12},{8,0},{12,4},{1,9},{5,13},{9,1},{13,5},{2,10},{6,14},... | collective-permute-start | bytes 319496 | tf_op jit(solution)/shard_map/ppermute | solution.py:412
  9.2 1.3 %collective-permute-start.4 = (bf16[208,256]{1,0:T(8,128)(2,1)S(1)}, bf16[208,256]{1,0:T(8,128)(2,1)S(1)}, u32[]{:S(2)}, u32[]{:S(2)}) collective-permute-start(bf16[208,256]{1,0:T(8,128)(2,1)S(1)} %get-tuple-element.20), channel_id=1, source_target_pairs={{0,12},{4,0},{8,4},{12,8},{1,13},{5,1},{9,5},{13,9},{2,14},{6,2},{... | collective-permute-start | bytes 319496 | tf_op jit(solution)/shard_map/ppermute | solution.py:412
  10.5 1.8 %constant_dynamic-slice_fusion = bf16[128,8,2,1,2,256]{5,1,4,3,2,0:T(8,128)(2,1)S(1)} fusion(bf16[128,8,2,2,2,256]{5,1,4,3,2,0:T(8,128)(2,1)} %bitcast.17, s32[]{:T(128)S(6)} %select_n.4), kind=kLoop, calls=%fused_computation.3 | loop fusion | bytes 4194308 | tf_op jit(solution)/shard_map/jit(dynamic_index_in_dim)/dynamic_slice | solution.py:429
  12.3 0.1 copy.7
  12.5 0.7 %copy.8 = bf16[64,8,8,256]{3,1,2,0:T(8,128)(2,1)S(1)} copy(bf16[64,8,8,256]{3,2,1,0:T(8,128)(2,1)S(1)} %bitcast.16) | data formatting | bytes 4194304
  13.2 0.1 collective-permute-start.1
  13.3 0.0 collective-permute-done.refs_1_.refs_0_
  13.3 0.5 %collective-permute-start.2 = (bf16[208,256]{1,0:T(8,128)(2,1)S(1)}, bf16[208,256]{1,0:T(8,128)(2,1)S(1)}, u32[]{:S(2)}, u32[]{:S(2)}) collective-permute-start(bf16[208,256]{1,0:T(8,128)(2,1)S(1)} %collective-permute-done.refs_1_.refs_0_), channel_id=1, source_target_pairs={{0,1},{1,0},{2,3},{3,2},{4,5},{5,4},{6,7},{7,6},{8,9},{9,8},{10,11... | collective-permute-start | bytes 319496 | tf_op jit(solution)/shard_map/ppermute | solution.py:412
  13.8 2.5 %collective-permute-done.3.refs_4_.refs_1_ = bf16[208,256]{1,0:T(8,128)(2,1)S(1)} collective-permute-done((bf16[208,256]{1,0:T(8,128)(2,1)S(1)}, bf16[208,256]{1,0:T(8,128)(2,1)S(1)}, u32[]{:S(2)}, u32[]{:S(2)}) %collective-permute-start.3) | collective-permute-done | bytes 106528 | tf_op jit(solution)/shard_map/ppermute | solution.py:412
  16.3 0.0 collective-permute-start.5
  16.3 0.0 collective-permute-done.4.refs_5_.refs_2_
  16.3 0.5 %collective-permute-start.6 = (bf16[208,256]{1,0:T(8,128)(2,1)S(1)}, bf16[208,256]{1,0:T(8,128)(2,1)S(1)}, u32[]{:S(2)}, u32[]{:S(2)}) collective-permute-start(bf16[208,256]{1,0:T(8,128)(2,1)S(1)} %collective-permute-done.4.refs_5_.refs_2_), channel_id=1, source_target_pairs={{0,1},{1,0},{2,3},{3,2},{4,5},{5,4},{6,7},{7,6},{8,9},{9,8},{10,11... | collective-permute-start | bytes 319496 | tf_op jit(solution)/shard_map/ppermute | solution.py:412
  16.8 1.6 %collective-permute-start.11 = (bf16[624,256]{1,0:T(8,128)(2,1)S(1)}, bf16[624,256]{1,0:T(8,128)(2,1)S(1)}, u32[]{:S(2)}, u32[]{:S(2)}) collective-permute-start(bf16[624,256]{1,0:T(8,128)(2,1)S(1)} %stack.18), channel_id=1, source_target_pairs={{0,2},{2,0},{1,3},{3,1},{4,6},{6,4},{5,7},{7,5},{8,10},{10,8},{9,1... | collective-permute-start | bytes 958472 | tf_op jit(solution)/shard_map/ppermute | solution.py:412
  18.4 0.0 collective-permute-done.1.refs_2_
  18.4 0.0 collective-permute-done.2.refs_3_
  18.4 0.0 collective-permute-done.5.refs_6_
  18.4 0.0 collective-permute-done.6.refs_7_
  18.4 2.0 %forward.1.refs_8_ = f32[8,128]{1,0:T(8,128)S(1)} custom-call(bf16[208,256]{1,0:T(8,128)(2,1)S(1)} %after.1.refs_0_, bf16[208,256]{1,0:T(8,128)(2,1)S(1)} %collective-permute-done.refs_1_.refs_0_, bf16[208,256]{1,0:T(8,128)(2,1)S(1)} %collective-permute-done.1.refs_2_, bf16[208,256]{1,0:T(8,128)(2,1)S(1)} %collective-permute-done.2.refs_3_, ...), custom_call_target="tpu_custom_call" | custom-call | tf_op jit(solution)/shard_map/forward/pallas_call | solution.py:262
  20.4 3.8 %collective-permute-start.9 = (f32[8,128]{1,0:T(8,128)S(1)}, f32[8,128]{1,0:T(8,128)S(1)}, u32[]{:S(2)}, u32[]{:S(2)}) collective-permute-start(f32[8,128]{1,0:T(8,128)S(1)} %forward.1.refs_8_), channel_id=1, source_target_pairs={{0,12},{4,0},{8,4},{12,8},{1,13},{5,1},{9,5},{13,9},{2,14},{6,2},{... | collective-permute-start | bytes 12296 | tf_op jit(solution)/shard_map/ppermute | solution.py:412
  24.2 0.0 collective-permute-start.8
  24.3 0.6 %collective-permute-start.7 = (f32[8,128]{1,0:T(8,128)S(1)}, f32[8,128]{1,0:T(8,128)S(1)}, u32[]{:S(2)}, u32[]{:S(2)}) collective-permute-start(f32[8,128]{1,0:T(8,128)S(1)} %forward.1.refs_8_), channel_id=1, source_target_pairs={{0,4},{4,8},{8,12},{12,0},{1,5},{5,9},{9,13},{13,1},{2,6},{6,10},{... | collective-permute-start | bytes 12296 | tf_op jit(solution)/shard_map/ppermute | solution.py:412
  24.9 0.9 %collective-permute-start.10 = (bf16[208,256]{1,0:T(8,128)(2,1)S(1)}, bf16[208,256]{1,0:T(8,128)(2,1)S(1)}, u32[]{:S(2)}, u32[]{:S(2)}) collective-permute-start(bf16[208,256]{1,0:T(8,128)(2,1)S(1)} %get-tuple-element.17.x_ref), channel_id=1, source_target_pairs={{0,2},{2,0},{1,3},{3,1},{4,6},{6,4},{5,7},{7,5},{8,10},{10,8},{9,1... | collective-permute-start | bytes 319496 | tf_op jit(solution)/shard_map/ppermute | solution.py:412
  25.7 0.7 %prepare0.2 = (bf16[384,2048]{1,0:T(8,128)(2,1)S(1)}, bf16[128,384]{1,0:T(8,128)(2,1)S(1)}, bf16[128,384]{1,0:T(8,128)(2,1)S(1)}, f32[8,384]{1,0:T(8,128)S(1)}) custom-call(bf16[208,256]{1,0:T(8,128)(2,1)S(1)} %after.1.refs_0_, bf16[208,256]{1,0:T(8,128)(2,1)S(1)} %collective-permute-done.refs_1_.refs_0_, ...), custom_call_target="tpu_custom_call" | custom-call | bytes 294912 | tf_op jit(solution)/shard_map/prepare0/pallas_call | solution.py:303
  26.5 0.0 collective-permute-done.9
  26.5 2.3 %collective-permute-done.8 = f32[8,128]{1,0:T(8,128)S(1)} collective-permute-done((f32[8,128]{1,0:T(8,128)S(1)}, f32[8,128]{1,0:T(8,128)S(1)}, u32[]{:S(2)}, u32[]{:S(2)}) %collective-permute-start.8) | collective-permute-done | bytes 4128 | tf_op jit(solution)/shard_map/ppermute | solution.py:412
  28.8 0.9 %collective-permute-done.7 = f32[8,128]{1,0:T(8,128)S(1)} collective-permute-done((f32[8,128]{1,0:T(8,128)S(1)}, f32[8,128]{1,0:T(8,128)S(1)}, u32[]{:S(2)}, u32[]{:S(2)}) %collective-permute-start.7) | collective-permute-done | bytes 4128 | tf_op jit(solution)/shard_map/ppermute | solution.py:412
  29.7 0.0 collective-permute-done.10.refs_0_
  29.7 0.0 collective-permute-done.11.refs_1_
  29.7 0.1 collective-permute-start.12
  29.8 1.2 %collective-permute-start.13 = (f32[8,128]{1,0:T(8,128)S(1)}, f32[8,128]{1,0:T(8,128)S(1)}, u32[]{:S(2)}, u32[]{:S(2)}) collective-permute-start(f32[8,128]{1,0:T(8,128)S(1)} %add_add_fusion.obs_ref.refs_2_), channel_id=1, source_target_pairs={{0,2},{2,0},{1,3},{3,1},{4,6},{6,4},{5,7},{7,5},{8,10},{10,8},{9,1... | collective-permute-start | bytes 12296 | tf_op jit(solution)/shard_map/ppermute | solution.py:412
  31.0 1.9 %own_adjoint.1.before_ref = f32[256,2048]{1,0:T(8,128)S(1)} custom-call(s32[3]{0:T(128)S(1)} %pad_add_fusion.1.where_ref, bf16[384,2048]{1,0:T(8,128)(2,1)S(1)} %get-tuple-element.21.f8_ref, bf16[128,384]{1,0:T(8,128)(2,1)S(1)} %get-tuple-element.22.own_ref, bf16[128,384]{1,0:T(8,128)(2,1)S(1)} %get-tuple-element.23.to_r_ref, ...), custom_call_target="tpu_custom_call" | custom-call | flops 805306368 | bytes 1572864 | tf_op jit(solution)/shard_map/own_adjoint/pallas_call | solution.py:348
  32.9 0.0 collective-permute-done.12.refs_1_
  32.9 0.7 %prepare0.3 = (bf16[384,2048]{1,0:T(8,128)(2,1)S(1)}, bf16[128,384]{1,0:T(8,128)(2,1)S(1)}, bf16[128,384]{1,0:T(8,128)(2,1)S(1)}, f32[8,384]{1,0:T(8,128)S(1)}) custom-call(bf16[832,256]{1,0:T(8,128)(2,1)S(1)} %stack.19.refs_0_, bf16[832,256]{1,0:T(8,128)(2,1)S(1)} %collective-permute-done.12.refs_1_), custom_call_target="tpu_custom_call" | custom-call | bytes 294912 | tf_op jit(solution)/shard_map/prepare0/pallas_call | solution.py:303
  33.6 0.0 collective-permute-done.13.refs_0_
  33.7 3.0 %adjoint.1 = f32[1024,512]{1,0:T(8,128)} custom-call(s32[3]{0:T(128)S(1)} %pad_add_fusion.1.where_ref, f32[256,2048]{1,0:T(8,128)S(1)} %own_adjoint.1.before_ref, bf16[384,2048]{1,0:T(8,128)(2,1)S(1)} %get-tuple-element.25.f8_ref, bf16[128,384]{1,0:T(8,128)(2,1)S(1)} %get-tuple-element.26.own_ref, bf16[128,384]{1,0:T(8,128)(2,1)S(1)} %get-tuple-element.27.to_r_ref, ...), custom_call_target="tpu_custom_call" | custom-call | tf_op jit(solution)/shard_map/adjoint/pallas_call | solution.py:395
  (4 shorter events, 0.1 us)
Async XLA Ops:
  3.5 9.7 %collective-permute-start = (bf16[208,256]{1,0:T(8,128)(2,1)S(1)}, bf16[208,256]{1,0:T(8,128)(2,1)S(1)}, u32[]{:S(2)}, u32[]{:S(2)}) collective-permute-start(bf16[208,256]{1,0:T(8,128)(2,1)S(1)} %get-tuple-element.18), channel_id=1, source_target_pairs={{0,4},{4,8},{8,12},{12,0},{1,5},{5,9},{9,13},{13,1},{2,6},{6,10},{... | collective-permute-start | bytes 319496 | tf_op jit(solution)/shard_map/ppermute | solution.py:412
  6.6 9.7 %collective-permute-start.3 = (bf16[208,256]{1,0:T(8,128)(2,1)S(1)}, bf16[208,256]{1,0:T(8,128)(2,1)S(1)}, u32[]{:S(2)}, u32[]{:S(2)}) collective-permute-start(bf16[208,256]{1,0:T(8,128)(2,1)S(1)} %get-tuple-element.19), channel_id=1, source_target_pairs={{0,8},{4,12},{8,0},{12,4},{1,9},{5,13},{9,1},{13,5},{2,10},{6,14},... | collective-permute-start | bytes 319496 | tf_op jit(solution)/shard_map/ppermute | solution.py:412
  9.2 7.1 %collective-permute-start.4 = (bf16[208,256]{1,0:T(8,128)(2,1)S(1)}, bf16[208,256]{1,0:T(8,128)(2,1)S(1)}, u32[]{:S(2)}, u32[]{:S(2)}) collective-permute-start(bf16[208,256]{1,0:T(8,128)(2,1)S(1)} %get-tuple-element.20), channel_id=1, source_target_pairs={{0,12},{4,0},{8,4},{12,8},{1,13},{5,1},{9,5},{13,9},{2,14},{6,2},{... | collective-permute-start | bytes 319496 | tf_op jit(solution)/shard_map/ppermute | solution.py:412
  13.2 5.2 %collective-permute-start.1 = (bf16[208,256]{1,0:T(8,128)(2,1)S(1)}, bf16[208,256]{1,0:T(8,128)(2,1)S(1)}, u32[]{:S(2)}, u32[]{:S(2)}) collective-permute-start(bf16[208,256]{1,0:T(8,128)(2,1)S(1)} %after.1.refs_0_), channel_id=1, source_target_pairs={{0,1},{1,0},{2,3},{3,2},{4,5},{5,4},{6,7},{7,6},{8,9},{9,8},{10,11... | collective-permute-start | bytes 319496 | tf_op jit(solution)/shard_map/ppermute | solution.py:412
  13.3 5.1 %collective-permute-start.2 = (bf16[208,256]{1,0:T(8,128)(2,1)S(1)}, bf16[208,256]{1,0:T(8,128)(2,1)S(1)}, u32[]{:S(2)}, u32[]{:S(2)}) collective-permute-start(bf16[208,256]{1,0:T(8,128)(2,1)S(1)} %collective-permute-done.refs_1_.refs_0_), channel_id=1, source_target_pairs={{0,1},{1,0},{2,3},{3,2},{4,5},{5,4},{6,7},{7,6},{8,9},{9,8},{10,11... | collective-permute-start | bytes 319496 | tf_op jit(solution)/shard_map/ppermute | solution.py:412
  16.3 2.1 %collective-permute-start.5 = (bf16[208,256]{1,0:T(8,128)(2,1)S(1)}, bf16[208,256]{1,0:T(8,128)(2,1)S(1)}, u32[]{:S(2)}, u32[]{:S(2)}) collective-permute-start(bf16[208,256]{1,0:T(8,128)(2,1)S(1)} %collective-permute-done.3.refs_4_.refs_1_), channel_id=1, source_target_pairs={{0,1},{1,0},{2,3},{3,2},{4,5},{5,4},{6,7},{7,6},{8,9},{9,8},{10,11... | collective-permute-start | bytes 319496 | tf_op jit(solution)/shard_map/ppermute | solution.py:412
  16.3 2.1 %collective-permute-start.6 = (bf16[208,256]{1,0:T(8,128)(2,1)S(1)}, bf16[208,256]{1,0:T(8,128)(2,1)S(1)}, u32[]{:S(2)}, u32[]{:S(2)}) collective-permute-start(bf16[208,256]{1,0:T(8,128)(2,1)S(1)} %collective-permute-done.4.refs_5_.refs_2_), channel_id=1, source_target_pairs={{0,1},{1,0},{2,3},{3,2},{4,5},{5,4},{6,7},{7,6},{8,9},{9,8},{10,11... | collective-permute-start | bytes 319496 | tf_op jit(solution)/shard_map/ppermute | solution.py:412
  16.8 12.8 %collective-permute-start.11 = (bf16[624,256]{1,0:T(8,128)(2,1)S(1)}, bf16[624,256]{1,0:T(8,128)(2,1)S(1)}, u32[]{:S(2)}, u32[]{:S(2)}) collective-permute-start(bf16[624,256]{1,0:T(8,128)(2,1)S(1)} %stack.18), channel_id=1, source_target_pairs={{0,2},{2,0},{1,3},{3,1},{4,6},{6,4},{5,7},{7,5},{8,10},{10,8},{9,1... | collective-permute-start | bytes 958472 | tf_op jit(solution)/shard_map/ppermute | solution.py:412
  20.4 6.0 %collective-permute-start.9 = (f32[8,128]{1,0:T(8,128)S(1)}, f32[8,128]{1,0:T(8,128)S(1)}, u32[]{:S(2)}, u32[]{:S(2)}) collective-permute-start(f32[8,128]{1,0:T(8,128)S(1)} %forward.1.refs_8_), channel_id=1, source_target_pairs={{0,12},{4,0},{8,4},{12,8},{1,13},{5,1},{9,5},{13,9},{2,14},{6,2},{... | collective-permute-start | bytes 12296 | tf_op jit(solution)/shard_map/ppermute | solution.py:412
  24.2 4.5 %collective-permute-start.8 = (f32[8,128]{1,0:T(8,128)S(1)}, f32[8,128]{1,0:T(8,128)S(1)}, u32[]{:S(2)}, u32[]{:S(2)}) collective-permute-start(f32[8,128]{1,0:T(8,128)S(1)} %forward.1.refs_8_), channel_id=1, source_target_pairs={{0,8},{4,12},{8,0},{12,4},{1,9},{5,13},{9,1},{13,5},{2,10},{6,14},... | collective-permute-start | bytes 12296 | tf_op jit(solution)/shard_map/ppermute | solution.py:412
  24.3 5.4 %collective-permute-start.7 = (f32[8,128]{1,0:T(8,128)S(1)}, f32[8,128]{1,0:T(8,128)S(1)}, u32[]{:S(2)}, u32[]{:S(2)}) collective-permute-start(f32[8,128]{1,0:T(8,128)S(1)} %forward.1.refs_8_), channel_id=1, source_target_pairs={{0,4},{4,8},{8,12},{12,0},{1,5},{5,9},{9,13},{13,1},{2,6},{6,10},{... | collective-permute-start | bytes 12296 | tf_op jit(solution)/shard_map/ppermute | solution.py:412
  24.9 4.8 %collective-permute-start.10 = (bf16[208,256]{1,0:T(8,128)(2,1)S(1)}, bf16[208,256]{1,0:T(8,128)(2,1)S(1)}, u32[]{:S(2)}, u32[]{:S(2)}) collective-permute-start(bf16[208,256]{1,0:T(8,128)(2,1)S(1)} %get-tuple-element.17.x_ref), channel_id=1, source_target_pairs={{0,2},{2,0},{1,3},{3,1},{4,6},{6,4},{5,7},{7,5},{8,10},{10,8},{9,1... | collective-permute-start | bytes 319496 | tf_op jit(solution)/shard_map/ppermute | solution.py:412
  29.7 3.2 %collective-permute-start.12 = (bf16[832,256]{1,0:T(8,128)(2,1)S(1)}, bf16[832,256]{1,0:T(8,128)(2,1)S(1)}, u32[]{:S(2)}, u32[]{:S(2)}) collective-permute-start(bf16[832,256]{1,0:T(8,128)(2,1)S(1)} %stack.19.refs_0_), channel_id=1, source_target_pairs={{0,1},{1,0},{2,3},{3,2},{4,5},{5,4},{6,7},{7,6},{8,9},{9,8},{10,11... | collective-permute-start | bytes 1277960 | tf_op jit(solution)/shard_map/ppermute | solution.py:412
  29.8 3.9 %collective-permute-start.13 = (f32[8,128]{1,0:T(8,128)S(1)}, f32[8,128]{1,0:T(8,128)S(1)}, u32[]{:S(2)}, u32[]{:S(2)}) collective-permute-start(f32[8,128]{1,0:T(8,128)S(1)} %add_add_fusion.obs_ref.refs_2_), channel_id=1, source_target_pairs={{0,2},{2,0},{1,3},{3,1},{4,6},{6,4},{5,7},{7,5},{8,10},{10,8},{9,1... | collective-permute-start | bytes 12296 | tf_op jit(solution)/shard_map/ppermute | solution.py:412

commit v6 on v5

--- a/solution.py
+++ b/solution.py
@@ -10,10 +10,11 @@
 F32 = jnp.float32
 BF16 = jnp.bfloat16
 I32 = jnp.int32
+QUARTERS = 4
 META = 16
 VMEM_LIMIT = 48 * 1024 * 1024
 GROUPS = ((0,), (1, 2, 3))
-EARLY = 0
+EARLY = 1
 FORWARD_BYTES = 0
 
 
@@ -107,7 +108,7 @@
     values = jnp.where(row_m == 0, local_row + 1.0, values)
     values = jnp.where(row_m == 1, values + (tm * w2).astype(F32), values)
     values = jnp.where(row_m == 2, (r_of + me * receptors).astype(F32), values)
-    fp = fp_ref[...]
+    fp = fp_ref[...].reshape(cols, fp_ref.shape[2])
     for w in range(w2):
         slot_w = jnp.where(w_of == w, slot, -1)
         pick = mask(iota((padded, cols), 0) == slot_w).astype(BF16)
@@ -147,7 +148,7 @@
         out_specs=[vm] * n,
         compiler_params=pltpu.CompilerParams(vmem_limit_bytes=VMEM_LIMIT),
         name="pack",
-    )(where, small, footprint.reshape(receptors * slots * w2, cells))
+    )(where, small, footprint.reshape(receptors * slots, w2, cells))
 
 
 def slots_of(bufs, rows):
@@ -372,16 +373,27 @@
             cfg, where_ref[2], obs_ref, own_ref[:, lanes], to_r_ref[:, lanes], weight_ref[:, lanes], a_ref, lanes
         )
     copies = []
-    for j in range(kd):
-        a = a_ref[2 * j * local : 2 * (j + 1) * local, :]
+    part = local // QUARTERS
+    rows = part * hours
+    for q in range(QUARTERS):
+        a = jnp.concatenate(
+            [a_ref[i * local + q * part : i * local + (q + 1) * part, :] for i in range(2 * kd)], axis=0
+        )
         for h in range(hours):
             sums = nn(a, f8_ref[:, h * cells : (h + 1) * cells])
-            both = sums[0:local] + sums[local : 2 * local]
-            both = both + before_ref[j * local : (j + 1) * local, h * cells : (h + 1) * cells]
-            for t in range(per_k):
-                tiles_ref.at[j * per_k + t][pl.ds(h, local, stride=hours), :] = both[:, t * 128 : (t + 1) * 128]
-        for t in range(j * per_k, (j + 1) * per_k):
-            copy = pltpu.make_async_copy(tiles_ref.at[t], out_ref.at[:, pl.ds(t * 128, 128)], sems.at[t])
+            for j in range(kd):
+                both = sums[2 * j * part : (2 * j + 1) * part] + sums[(2 * j + 1) * part : (2 * j + 2) * part]
+                at = j * local + q * part
+                both = both + before_ref[at : at + part, h * cells : (h + 1) * cells]
+                for t in range(per_k):
+                    tile = tiles_ref.at[j * per_k + t]
+                    tile[pl.ds(q * rows + h, part, stride=hours), :] = both[:, t * 128 : (t + 1) * 128]
+        for t in range(kd * per_k):
+            copy = pltpu.make_async_copy(
+                tiles_ref.at[t, pl.ds(q * rows, rows)],
+                out_ref.at[pl.ds(q * rows, rows), pl.ds(t * 128, 128)],
+                sems.at[t, q],
+            )
             copy.start()
             copies.append(copy)
     for copy in copies:
@@ -400,7 +412,7 @@
         scratch_shapes=[
             pltpu.VMEM((2 * kd * local, total), BF16),
             pltpu.VMEM((kd * cells // 128, local * hours, 128), F32),
-            pltpu.SemaphoreType.DMA((kd * cells // 128,)),
+            pltpu.SemaphoreType.DMA((kd * cells // 128, QUARTERS)),
         ],
         compiler_params=pltpu.CompilerParams(vmem_limit_bytes=VMEM_LIMIT),
         name="adjoint",
@@ -410,6 +422,12 @@
 def shift(x, axis, d):
     n = lax.axis_size(axis)
     return lax.ppermute(x, axis, [(i, (i + d) % n) for i in range(n)])
+
+
+def swap(x, axis, bits):
+    n = lax.axis_size(axis)
+    assert n & (n - 1) == 0
+    return lax.ppermute(x, axis, [(i, i ^ bits) for i in range(n)])
 
 
 def shards(probes, footprint, blocks, hour_start, obs_weight, placement):
@@ -447,7 +465,7 @@
     partial = forward(cfg, own, probes_t, (8, rp), [b for group in across for b in group[:EARLY]])
     observed = partial
     for d in range(1, n):
-        observed = observed + shift(partial, "rcp", d)
+        observed = observed + swap(partial, "rcp", d)
     operands = prepare(cfg, 0, own, 1, rp, [], partial)
     before = own_adjoint(cfg, where, operands, observed)
     gate, operands = operands[3], []

time: 36.9 us -> 35.6 us (0.965)
  waiting for transfers between devices: 5.74 us -> 4.28 us
  starting transfers between devices: 16.2 us -> 16.6 us
    ppermute x14 -> x11, waiting for transfers between devices: 5.74 us -> 1.15 us  [shift(): return lax.ppermute(x, axis, [(i, (i + d) % n) for i in range(n)])]
    ppermute x0 -> x3, starting transfers between devices: none -> 4.44 us  [swap(): return lax.ppermute(x, axis, [(i, i ^ bits) for i in range(n)])]
    ppermute x14 -> x11, starting transfers between devices: 16.2 us -> 12.1 us  [shift(): return lax.ppermute(x, axis, [(i, (i + d) % n) for i in range(n)])]
    ppermute x0 -> x3, waiting for transfers between devices: none -> 3.13 us  [swap(): return lax.ppermute(x, axis, [(i, i ^ bits) for i in range(n)])]
    reshape x1 -> x0, local copies, waits for them, and re-layouts: 1.05 us -> none  [pack(): footprint.reshape(receptors * slots * w2, cells)]
    unnamed x1 -> x3, local copies, waits for them, and re-layouts: 0.68 us -> 1.62 us
  transfers between devices with their start and end apart: 14 -> 14, of which waited for: 3 -> 4; matrix products, arithmetic and copies ran while one was open for 7% -> 7% of each run, Pallas kernels for 15% -> 15%
where the time goes in v6:
time: 35.6 us; the launch traced here: 35.4 us
  starting transfers between devices  16.6 us (47%)
  Pallas kernels  10 us (28%)
  waiting for transfers between devices  4.28 us (12%)
  local copies, waits for them, and re-layouts  3.55 us (10%)
  other arithmetic  0.84 us (2%)
    ppermute x11, starting transfers between devices, shift(): return lax.ppermute(x, axis, [(i, (i + d) % n) for i in range(n)])  12.1 us
    ppermute x3, starting transfers between devices, swap(): return lax.ppermute(x, axis, [(i, i ^ bits) for i in range(n)])  4.44 us
    ppermute x3, waiting for transfers between devices, swap(): return lax.ppermute(x, axis, [(i, i ^ bits) for i in range(n)])  3.13 us
    pallas_call x1, Pallas kernels, adjoint(): pl.pallas_call(functools.partial(adjoint_kernel, cfg), out_shape=jax.Shap...  2.93 us
    pallas_call x1, Pallas kernels, forward(): pl.pallas_call(functools.partial(forward_kernel, cfg, counts), out_shape=...  2.03 us
    dynamic_slice x2, local copies, waits for them, and re-layouts, shards(): lax.dynamic_index_in_dim(probes.reshape(local, hours, nreg, ntm, kd, cell...  1.93 us
    pallas_call x1, Pallas kernels, own_adjoint(): pl.pallas_call(functools.partial(own_adjoint_kernel, cfg), out_shape=jax....  1.9 us
    unnamed x3, local copies, waits for them, and re-layouts  1.62 us
  transfers between devices with their start and end apart: 14, of which 4 were waited for; matrix products, arithmetic and copies ran while one was open for 7% of the time, Pallas kernels for 15%

profile of v6, /device:TPU:0, one launch (start us, length us, event | category | flops | bytes accessed | tf_op | source)
XLA Modules:
  0.0 35.4 jit_solution(7287923140638139759)
XLA Ops:
  0.0 0.1 pad_add_fusion.1.where_ref
  0.1 0.8 %pad_add_fusion.small_ref = f32[24,512]{1,0:T(8,128)S(1)} fusion(f32[1,16]{1,0:T(1,128)} %bitcast.21, s32[1,16]{1,0:T(1,128)} %bitcast.22, s32[1,512]{1,0:T(1,128)} %bitcast.20, s32[16,16]{1,0:T(8,128)} %param.8), kind=kLoop, calls=%fused_computation | loop fusion | flops 49152 | bytes 52352 | tf_op jit(solution)/shard_map/add | solution.py:142
  0.8 0.0 copy-start
  0.8 0.9 %copy-done = bf16[16,16,2,256]{3,2,1,0:T(2,128)(2,1)S(1)} copy-done((bf16[16,16,2,256]{3,2,1,0:T(2,128)(2,1)S(1)}, bf16[16,16,2,256]{3,2,1,0:T(2,128)(2,1)}, u32[]{:S(2)}) %copy-start) | copy-done | bytes 262168
  1.8 1.6 %pack.1 = (bf16[208,256]{1,0:T(8,128)(2,1)S(1)}, bf16[208,256]{1,0:T(8,128)(2,1)S(1)}, bf16[208,256]{1,0:T(8,128)(2,1)S(1)}, bf16[208,256]{1,0:T(8,128)(2,1)S(1)}) custom-call(s32[3]{0:T(128)S(1)} %pad_add_fusion.1.where_ref, f32[24,512]{1,0:T(8,128)S(1)} %pad_add_fusion.small_ref, bf16[256,2,256]{2,1,0:T(2,128)(2,1)S(1)} %bitcast.17), custom_call_target="tpu_custom_call" | custom-call | tf_op jit(solution)/shard_map/pack/pallas_call | solution.py:144
  3.4 3.1 %collective-permute-start = (bf16[208,256]{1,0:T(8,128)(2,1)S(1)}, bf16[208,256]{1,0:T(8,128)(2,1)S(1)}, u32[]{:S(2)}, u32[]{:S(2)}) collective-permute-start(bf16[208,256]{1,0:T(8,128)(2,1)S(1)} %get-tuple-element.18), channel_id=1, source_target_pairs={{0,4},{4,8},{8,12},{12,0},{1,5},{5,9},{9,13},{13,1},{2,6},{6,10},{... | collective-permute-start | bytes 319496 | tf_op jit(solution)/shard_map/ppermute | solution.py:424
  6.5 2.6 %collective-permute-start.3 = (bf16[208,256]{1,0:T(8,128)(2,1)S(1)}, bf16[208,256]{1,0:T(8,128)(2,1)S(1)}, u32[]{:S(2)}, u32[]{:S(2)}) collective-permute-start(bf16[208,256]{1,0:T(8,128)(2,1)S(1)} %get-tuple-element.19), channel_id=1, source_target_pairs={{0,8},{4,12},{8,0},{12,4},{1,9},{5,13},{9,1},{13,5},{2,10},{6,14},... | collective-permute-start | bytes 319496 | tf_op jit(solution)/shard_map/ppermute | solution.py:424
  9.1 1.3 %collective-permute-start.4 = (bf16[208,256]{1,0:T(8,128)(2,1)S(1)}, bf16[208,256]{1,0:T(8,128)(2,1)S(1)}, u32[]{:S(2)}, u32[]{:S(2)}) collective-permute-start(bf16[208,256]{1,0:T(8,128)(2,1)S(1)} %get-tuple-element.20), channel_id=1, source_target_pairs={{0,12},{4,0},{8,4},{12,8},{1,13},{5,1},{9,5},{13,9},{2,14},{6,2},{... | collective-permute-start | bytes 319496 | tf_op jit(solution)/shard_map/ppermute | solution.py:424
  10.4 1.5 %collective-permute-start.7 = (bf16[208,256]{1,0:T(8,128)(2,1)S(1)}, bf16[208,256]{1,0:T(8,128)(2,1)S(1)}, u32[]{:S(2)}, u32[]{:S(2)}) collective-permute-start(bf16[208,256]{1,0:T(8,128)(2,1)S(1)} %get-tuple-element.17.x_ref), channel_id=1, source_target_pairs={{0,2},{2,0},{1,3},{3,1},{4,6},{6,4},{5,7},{7,5},{8,10},{10,8},{9,1... | collective-permute-start | bytes 319496 | tf_op jit(solution)/shard_map/ppermute | solution.py:424
  11.9 1.8 %constant_dynamic-slice_fusion = bf16[128,8,2,1,2,256]{5,1,4,3,2,0:T(8,128)(2,1)S(1)} fusion(bf16[128,8,2,2,2,256]{5,1,4,3,2,0:T(8,128)(2,1)} %bitcast.19, s32[]{:T(128)S(6)} %select_n.4), kind=kLoop, calls=%fused_computation.3 | loop fusion | bytes 4194308 | tf_op jit(solution)/shard_map/jit(dynamic_index_in_dim)/dynamic_slice | solution.py:447
  13.7 0.1 copy.7
  13.9 0.7 %copy.8 = bf16[64,8,8,256]{3,1,2,0:T(8,128)(2,1)S(1)} copy(bf16[64,8,8,256]{3,2,1,0:T(8,128)(2,1)S(1)} %bitcast.18) | data formatting | bytes 4194304
  14.6 0.1 collective-permute-start.1
  14.6 0.0 collective-permute-done.refs_1_.refs_0_
  14.7 0.5 %collective-permute-start.2 = (bf16[208,256]{1,0:T(8,128)(2,1)S(1)}, bf16[208,256]{1,0:T(8,128)(2,1)S(1)}, u32[]{:S(2)}, u32[]{:S(2)}) collective-permute-start(bf16[208,256]{1,0:T(8,128)(2,1)S(1)} %collective-permute-done.refs_1_.refs_0_), channel_id=1, source_target_pairs={{0,1},{1,0},{2,3},{3,2},{4,5},{5,4},{6,7},{7,6},{8,9},{9,8},{10,11... | collective-permute-start | bytes 319496 | tf_op jit(solution)/shard_map/ppermute | solution.py:424
  15.1 1.0 %collective-permute-done.3.refs_4_.refs_1_ = bf16[208,256]{1,0:T(8,128)(2,1)S(1)} collective-permute-done((bf16[208,256]{1,0:T(8,128)(2,1)S(1)}, bf16[208,256]{1,0:T(8,128)(2,1)S(1)}, u32[]{:S(2)}, u32[]{:S(2)}) %collective-permute-start.3) | collective-permute-done | bytes 106528 | tf_op jit(solution)/shard_map/ppermute | solution.py:424
  16.2 0.0 collective-permute-start.5
  16.2 0.0 collective-permute-done.4.refs_5_.refs_2_
  16.2 0.5 %collective-permute-start.6 = (bf16[208,256]{1,0:T(8,128)(2,1)S(1)}, bf16[208,256]{1,0:T(8,128)(2,1)S(1)}, u32[]{:S(2)}, u32[]{:S(2)}) collective-permute-start(bf16[208,256]{1,0:T(8,128)(2,1)S(1)} %collective-permute-done.4.refs_5_.refs_2_), channel_id=1, source_target_pairs={{0,1},{1,0},{2,3},{3,2},{4,5},{5,4},{6,7},{7,6},{8,9},{9,8},{10,11... | collective-permute-start | bytes 319496 | tf_op jit(solution)/shard_map/ppermute | solution.py:424
  16.7 0.0 collective-permute-done.7.refs_9_.refs_0_
  16.7 1.6 %collective-permute-start.11 = (bf16[624,256]{1,0:T(8,128)(2,1)S(1)}, bf16[624,256]{1,0:T(8,128)(2,1)S(1)}, u32[]{:S(2)}, u32[]{:S(2)}) collective-permute-start(bf16[624,256]{1,0:T(8,128)(2,1)S(1)} %stack.18), channel_id=1, source_target_pairs={{0,2},{2,0},{1,3},{3,1},{4,6},{6,4},{5,7},{7,5},{8,10},{10,8},{9,1... | collective-permute-start | bytes 958472 | tf_op jit(solution)/shard_map/ppermute | solution.py:424
  18.3 0.0 collective-permute-done.1.refs_2_
  18.3 0.0 collective-permute-done.2.refs_3_
  18.3 0.0 collective-permute-done.5.refs_6_
  18.3 0.0 collective-permute-done.6.refs_7_
  18.3 2.0 %forward.1.refs_8_ = f32[8,128]{1,0:T(8,128)S(1)} custom-call(bf16[208,256]{1,0:T(8,128)(2,1)S(1)} %after.1.refs_0_, bf16[208,256]{1,0:T(8,128)(2,1)S(1)} %collective-permute-done.refs_1_.refs_0_, bf16[208,256]{1,0:T(8,128)(2,1)S(1)} %collective-permute-done.1.refs_2_, bf16[208,256]{1,0:T(8,128)(2,1)S(1)} %collective-permute-done.2.refs_3_, ...), custom_call_target="tpu_custom_call" | custom-call | tf_op jit(solution)/shard_map/forward/pallas_call | solution.py:263
  20.4 3.8 %collective-permute-start.10 = (f32[8,128]{1,0:T(8,128)S(1)}, f32[8,128]{1,0:T(8,128)S(1)}, u32[]{:S(2)}, u32[]{:S(2)}) collective-permute-start(f32[8,128]{1,0:T(8,128)S(1)} %forward.1.refs_8_), channel_id=1, source_target_pairs={{0,12},{4,8},{8,4},{12,0},{1,13},{5,9},{9,5},{13,1},{2,14},{6,10},... | collective-permute-start | bytes 12296 | tf_op jit(solution)/shard_map/ppermute | solution.py:430
  24.2 0.0 collective-permute-start.9
  24.2 0.6 %collective-permute-start.8 = (f32[8,128]{1,0:T(8,128)S(1)}, f32[8,128]{1,0:T(8,128)S(1)}, u32[]{:S(2)}, u32[]{:S(2)}) collective-permute-start(f32[8,128]{1,0:T(8,128)S(1)} %forward.1.refs_8_), channel_id=1, source_target_pairs={{0,4},{4,0},{8,12},{12,8},{1,5},{5,1},{9,13},{13,9},{2,6},{6,2},{1... | collective-permute-start | bytes 12296 | tf_op jit(solution)/shard_map/ppermute | solution.py:430
  24.8 0.7 %prepare0.2 = (bf16[384,2048]{1,0:T(8,128)(2,1)S(1)}, bf16[128,384]{1,0:T(8,128)(2,1)S(1)}, bf16[128,384]{1,0:T(8,128)(2,1)S(1)}, f32[8,384]{1,0:T(8,128)S(1)}) custom-call(bf16[208,256]{1,0:T(8,128)(2,1)S(1)} %after.1.refs_0_, bf16[208,256]{1,0:T(8,128)(2,1)S(1)} %collective-permute-done.refs_1_.refs_0_, ...), custom_call_target="tpu_custom_call" | custom-call | bytes 294912 | tf_op jit(solution)/shard_map/prepare0/pallas_call | solution.py:304
  25.5 0.3 collective-permute-done.10
  25.8 2.9 %collective-permute-done.9 = f32[8,128]{1,0:T(8,128)S(1)} collective-permute-done((f32[8,128]{1,0:T(8,128)S(1)}, f32[8,128]{1,0:T(8,128)S(1)}, u32[]{:S(2)}, u32[]{:S(2)}) %collective-permute-start.9) | collective-permute-done | bytes 4128 | tf_op jit(solution)/shard_map/ppermute | solution.py:430
  28.7 0.0 collective-permute-done.8
  28.7 0.0 collective-permute-done.11.refs_1_
  28.7 0.1 collective-permute-start.12
  28.8 0.9 %collective-permute-start.13 = (f32[8,128]{1,0:T(8,128)S(1)}, f32[8,128]{1,0:T(8,128)S(1)}, u32[]{:S(2)}, u32[]{:S(2)}) collective-permute-start(f32[8,128]{1,0:T(8,128)S(1)} %add_add_fusion.obs_ref.refs_2_), channel_id=1, source_target_pairs={{0,2},{2,0},{1,3},{3,1},{4,6},{6,4},{5,7},{7,5},{8,10},{10,8},{9,1... | collective-permute-start | bytes 12296 | tf_op jit(solution)/shard_map/ppermute | solution.py:424
  29.7 1.9 %own_adjoint.1.before_ref = f32[256,2048]{1,0:T(8,128)S(1)} custom-call(s32[3]{0:T(128)S(1)} %pad_add_fusion.1.where_ref, bf16[384,2048]{1,0:T(8,128)(2,1)S(1)} %get-tuple-element.21.f8_ref, bf16[128,384]{1,0:T(8,128)(2,1)S(1)} %get-tuple-element.22.own_ref, bf16[128,384]{1,0:T(8,128)(2,1)S(1)} %get-tuple-element.23.to_r_ref, ...), custom_call_target="tpu_custom_call" | custom-call | flops 805306368 | bytes 1572864 | tf_op jit(solution)/shard_map/own_adjoint/pallas_call | solution.py:349
  31.6 0.0 collective-permute-done.12.refs_1_
  31.6 0.7 %prepare0.3 = (bf16[384,2048]{1,0:T(8,128)(2,1)S(1)}, bf16[128,384]{1,0:T(8,128)(2,1)S(1)}, bf16[128,384]{1,0:T(8,128)(2,1)S(1)}, f32[8,384]{1,0:T(8,128)S(1)}) custom-call(bf16[832,256]{1,0:T(8,128)(2,1)S(1)} %stack.19.refs_0_, bf16[832,256]{1,0:T(8,128)(2,1)S(1)} %collective-permute-done.12.refs_1_), custom_call_target="tpu_custom_call" | custom-call | bytes 294912 | tf_op jit(solution)/shard_map/prepare0/pallas_call | solution.py:304
  32.4 0.1 collective-permute-done.13.refs_0_
  32.5 2.9 %adjoint.1 = f32[1024,512]{1,0:T(8,128)} custom-call(s32[3]{0:T(128)S(1)} %pad_add_fusion.1.where_ref, f32[256,2048]{1,0:T(8,128)S(1)} %own_adjoint.1.before_ref, bf16[384,2048]{1,0:T(8,128)(2,1)S(1)} %get-tuple-element.25.f8_ref, bf16[128,384]{1,0:T(8,128)(2,1)S(1)} %get-tuple-element.26.own_ref, bf16[128,384]{1,0:T(8,128)(2,1)S(1)} %get-tuple-element.27.to_r_ref, ...), custom_call_target="tpu_custom_call" | custom-call | tf_op jit(solution)/shard_map/adjoint/pallas_call | solution.py:407
  (4 shorter events, 0.1 us)
Async XLA Ops:
  0.8 1.0 %copy-start = (bf16[16,16,2,256]{3,2,1,0:T(2,128)(2,1)S(1)}, bf16[16,16,2,256]{3,2,1,0:T(2,128)(2,1)}, u32[]{:S(2)}) copy-start(bf16[16,16,2,256]{3,2,1,0:T(2,128)(2,1)} %param.7) | copy-start | bytes 786436
  3.4 11.2 %collective-permute-start = (bf16[208,256]{1,0:T(8,128)(2,1)S(1)}, bf16[208,256]{1,0:T(8,128)(2,1)S(1)}, u32[]{:S(2)}, u32[]{:S(2)}) collective-permute-start(bf16[208,256]{1,0:T(8,128)(2,1)S(1)} %get-tuple-element.18), channel_id=1, source_target_pairs={{0,4},{4,8},{8,12},{12,0},{1,5},{5,9},{9,13},{13,1},{2,6},{6,10},{... | collective-permute-start | bytes 319496 | tf_op jit(solution)/shard_map/ppermute | solution.py:424
  6.5 9.7 %collective-permute-start.3 = (bf16[208,256]{1,0:T(8,128)(2,1)S(1)}, bf16[208,256]{1,0:T(8,128)(2,1)S(1)}, u32[]{:S(2)}, u32[]{:S(2)}) collective-permute-start(bf16[208,256]{1,0:T(8,128)(2,1)S(1)} %get-tuple-element.19), channel_id=1, source_target_pairs={{0,8},{4,12},{8,0},{12,4},{1,9},{5,13},{9,1},{13,5},{2,10},{6,14},... | collective-permute-start | bytes 319496 | tf_op jit(solution)/shard_map/ppermute | solution.py:424
  9.1 7.1 %collective-permute-start.4 = (bf16[208,256]{1,0:T(8,128)(2,1)S(1)}, bf16[208,256]{1,0:T(8,128)(2,1)S(1)}, u32[]{:S(2)}, u32[]{:S(2)}) collective-permute-start(bf16[208,256]{1,0:T(8,128)(2,1)S(1)} %get-tuple-element.20), channel_id=1, source_target_pairs={{0,12},{4,0},{8,4},{12,8},{1,13},{5,1},{9,5},{13,9},{2,14},{6,2},{... | collective-permute-start | bytes 319496 | tf_op jit(solution)/shard_map/ppermute | solution.py:424
  10.4 6.3 %collective-permute-start.7 = (bf16[208,256]{1,0:T(8,128)(2,1)S(1)}, bf16[208,256]{1,0:T(8,128)(2,1)S(1)}, u32[]{:S(2)}, u32[]{:S(2)}) collective-permute-start(bf16[208,256]{1,0:T(8,128)(2,1)S(1)} %get-tuple-element.17.x_ref), channel_id=1, source_target_pairs={{0,2},{2,0},{1,3},{3,1},{4,6},{6,4},{5,7},{7,5},{8,10},{10,8},{9,1... | collective-permute-start | bytes 319496 | tf_op jit(solution)/shard_map/ppermute | solution.py:424
  14.6 3.7 %collective-permute-start.1 = (bf16[208,256]{1,0:T(8,128)(2,1)S(1)}, bf16[208,256]{1,0:T(8,128)(2,1)S(1)}, u32[]{:S(2)}, u32[]{:S(2)}) collective-permute-start(bf16[208,256]{1,0:T(8,128)(2,1)S(1)} %after.1.refs_0_), channel_id=1, source_target_pairs={{0,1},{1,0},{2,3},{3,2},{4,5},{5,4},{6,7},{7,6},{8,9},{9,8},{10,11... | collective-permute-start | bytes 319496 | tf_op jit(solution)/shard_map/ppermute | solution.py:424
  14.7 3.6 %collective-permute-start.2 = (bf16[208,256]{1,0:T(8,128)(2,1)S(1)}, bf16[208,256]{1,0:T(8,128)(2,1)S(1)}, u32[]{:S(2)}, u32[]{:S(2)}) collective-permute-start(bf16[208,256]{1,0:T(8,128)(2,1)S(1)} %collective-permute-done.refs_1_.refs_0_), channel_id=1, source_target_pairs={{0,1},{1,0},{2,3},{3,2},{4,5},{5,4},{6,7},{7,6},{8,9},{9,8},{10,11... | collective-permute-start | bytes 319496 | tf_op jit(solution)/shard_map/ppermute | solution.py:424
  16.2 2.1 %collective-permute-start.5 = (bf16[208,256]{1,0:T(8,128)(2,1)S(1)}, bf16[208,256]{1,0:T(8,128)(2,1)S(1)}, u32[]{:S(2)}, u32[]{:S(2)}) collective-permute-start(bf16[208,256]{1,0:T(8,128)(2,1)S(1)} %collective-permute-done.3.refs_4_.refs_1_), channel_id=1, source_target_pairs={{0,1},{1,0},{2,3},{3,2},{4,5},{5,4},{6,7},{7,6},{8,9},{9,8},{10,11... | collective-permute-start | bytes 319496 | tf_op jit(solution)/shard_map/ppermute | solution.py:424
  16.2 2.1 %collective-permute-start.6 = (bf16[208,256]{1,0:T(8,128)(2,1)S(1)}, bf16[208,256]{1,0:T(8,128)(2,1)S(1)}, u32[]{:S(2)}, u32[]{:S(2)}) collective-permute-start(bf16[208,256]{1,0:T(8,128)(2,1)S(1)} %collective-permute-done.4.refs_5_.refs_2_), channel_id=1, source_target_pairs={{0,1},{1,0},{2,3},{3,2},{4,5},{5,4},{6,7},{7,6},{8,9},{9,8},{10,11... | collective-permute-start | bytes 319496 | tf_op jit(solution)/shard_map/ppermute | solution.py:424
  16.7 11.9 %collective-permute-start.11 = (bf16[624,256]{1,0:T(8,128)(2,1)S(1)}, bf16[624,256]{1,0:T(8,128)(2,1)S(1)}, u32[]{:S(2)}, u32[]{:S(2)}) collective-permute-start(bf16[624,256]{1,0:T(8,128)(2,1)S(1)} %stack.18), channel_id=1, source_target_pairs={{0,2},{2,0},{1,3},{3,1},{4,6},{6,4},{5,7},{7,5},{8,10},{10,8},{9,1... | collective-permute-start | bytes 958472 | tf_op jit(solution)/shard_map/ppermute | solution.py:424
  20.4 5.4 %collective-permute-start.10 = (f32[8,128]{1,0:T(8,128)S(1)}, f32[8,128]{1,0:T(8,128)S(1)}, u32[]{:S(2)}, u32[]{:S(2)}) collective-permute-start(f32[8,128]{1,0:T(8,128)S(1)} %forward.1.refs_8_), channel_id=1, source_target_pairs={{0,12},{4,8},{8,4},{12,0},{1,13},{5,9},{9,5},{13,1},{2,14},{6,10},... | collective-permute-start | bytes 12296 | tf_op jit(solution)/shard_map/ppermute | solution.py:430
  24.2 4.5 %collective-permute-start.9 = (f32[8,128]{1,0:T(8,128)S(1)}, f32[8,128]{1,0:T(8,128)S(1)}, u32[]{:S(2)}, u32[]{:S(2)}) collective-permute-start(f32[8,128]{1,0:T(8,128)S(1)} %forward.1.refs_8_), channel_id=1, source_target_pairs={{0,8},{4,12},{8,0},{12,4},{1,9},{5,13},{9,1},{13,5},{2,10},{6,14},... | collective-permute-start | bytes 12296 | tf_op jit(solution)/shard_map/ppermute | solution.py:430
  24.2 4.5 %collective-permute-start.8 = (f32[8,128]{1,0:T(8,128)S(1)}, f32[8,128]{1,0:T(8,128)S(1)}, u32[]{:S(2)}, u32[]{:S(2)}) collective-permute-start(f32[8,128]{1,0:T(8,128)S(1)} %forward.1.refs_8_), channel_id=1, source_target_pairs={{0,4},{4,0},{8,12},{12,8},{1,5},{5,1},{9,13},{13,9},{2,6},{6,2},{1... | collective-permute-start | bytes 12296 | tf_op jit(solution)/shard_map/ppermute | solution.py:430
  28.7 2.9 %collective-permute-start.12 = (bf16[832,256]{1,0:T(8,128)(2,1)S(1)}, bf16[832,256]{1,0:T(8,128)(2,1)S(1)}, u32[]{:S(2)}, u32[]{:S(2)}) collective-permute-start(bf16[832,256]{1,0:T(8,128)(2,1)S(1)} %stack.19.refs_0_), channel_id=1, source_target_pairs={{0,1},{1,0},{2,3},{3,2},{4,5},{5,4},{6,7},{7,6},{8,9},{9,8},{10,11... | collective-permute-start | bytes 1277960 | tf_op jit(solution)/shard_map/ppermute | solution.py:424
  28.8 3.7 %collective-permute-start.13 = (f32[8,128]{1,0:T(8,128)S(1)}, f32[8,128]{1,0:T(8,128)S(1)}, u32[]{:S(2)}, u32[]{:S(2)}) collective-permute-start(f32[8,128]{1,0:T(8,128)S(1)} %add_add_fusion.obs_ref.refs_2_), channel_id=1, source_target_pairs={{0,2},{2,0},{1,3},{3,1},{4,6},{6,4},{5,7},{7,5},{8,10},{10,8},{9,1... | collective-permute-start | bytes 12296 | tf_op jit(solution)/shard_map/ppermute | solution.py:424

commit v7 on v6

--- a/solution.py
+++ b/solution.py
@@ -230,29 +230,29 @@
     local, k, rows, capp = cfg["local"], cfg["k_core"], cfg["rows"], cfg["capp"]
     half = cfg["n"] // 2 * capp
     out_ref, f8_ref = refs[-2:]
+    probes_ref = refs[sum(sum(sides_n) for sides_n in counts)]
     at = 0
-    firsts = []
+    metas = []
     for i, sides_n in enumerate(counts):
         sides = []
         for count in sides_n:
             sides.append(slots_of(refs[at : at + count], rows))
             at += count
-        metas = [load_meta(cfg, placed) for placed in sides]
-        spread_hours(cfg, sides, metas, f8_ref, i * half)
-        firsts.append(metas[0][0:8])
-    probes_ref = refs[at]
-    meta = jnp.concatenate(firsts, axis=1)
-    used = meta.shape[1]
-    own = iota((local, used), 0) + 1 == meta[0:1].astype(I32)
-    row = iota((8, used), 0)
-    dots = jnp.zeros((8, used), F32)
-    f8 = f8_ref[...]
-    x = nt(probes_ref[...], f8)
-    for j in range(k):
-        y = jnp.sum(jnp.where(own, x[j * local : (j + 1) * local], 0.0), axis=0, keepdims=True)
-        dots = jnp.where(row == j, y, dots)
-    to_r = mask(iota((out_ref.shape[1], used), 0) == meta[2:3].astype(I32)).astype(BF16)
-    out_ref[...] = add_three(nt(three(dots), to_r))
+        side_metas = [load_meta(cfg, placed) for placed in sides]
+        spread_hours(cfg, sides, side_metas, f8_ref, i * half)
+        metas.append(side_metas[0])
+    row = iota((8, half), 0)
+    total = 0.0
+    for i, meta in enumerate(metas):
+        own = iota((local, half), 0) + 1 == meta[0:1].astype(I32)
+        x = nt(probes_ref[...], f8_ref[i * half : (i + 1) * half, :])
+        dots = jnp.zeros((8, half), F32)
+        for j in range(k):
+            y = jnp.sum(jnp.where(own, x[j * local : (j + 1) * local], 0.0), axis=0, keepdims=True)
+            dots = jnp.where(row == j, y, dots)
+        to_r = mask(iota((out_ref.shape[1], half), 0) == meta[2:3].astype(I32)).astype(BF16)
+        total = total + add_three(nt(three(dots), to_r))
+    out_ref[...] = total
 
 
 def forward(cfg, own, probes_t, out_shape, unread):

time: 35.6 us -> 35.5 us (level)
  no operation moved by 1% of the time
where the time goes in v7:
time: 35.5 us; the launch traced here: 35.2 us
  starting transfers between devices  16.5 us (46%)
  Pallas kernels  9.87 us (28%)
  waiting for transfers between devices  4.29 us (12%)
  local copies, waits for them, and re-layouts  3.55 us (10%)
  other arithmetic  0.84 us (2%)
    ppermute x11, starting transfers between devices, shift(): return lax.ppermute(x, axis, [(i, (i + d) % n) for i in range(n)])  12.1 us
    ppermute x3, starting transfers between devices, swap(): return lax.ppermute(x, axis, [(i, i ^ bits) for i in range(n)])  4.43 us
    ppermute x3, waiting for transfers between devices, swap(): return lax.ppermute(x, axis, [(i, i ^ bits) for i in range(n)])  3.12 us
    pallas_call x1, Pallas kernels, adjoint(): pl.pallas_call(functools.partial(adjoint_kernel, cfg), out_shape=jax.Shap...  2.93 us
    dynamic_slice x2, local copies, waits for them, and re-layouts, shards(): lax.dynamic_index_in_dim(probes.reshape(local, hours, nreg, ntm, kd, cell...  1.93 us
    pallas_call x1, Pallas kernels, own_adjoint(): pl.pallas_call(functools.partial(own_adjoint_kernel, cfg), out_shape=jax....  1.9 us
    pallas_call x1, Pallas kernels, forward(): pl.pallas_call(functools.partial(forward_kernel, cfg, counts), out_shape=...  1.89 us
    unnamed x3, local copies, waits for them, and re-layouts  1.62 us
  transfers between devices with their start and end apart: 14, of which 4 were waited for; matrix products, arithmetic and copies ran while one was open for 7% of the time, Pallas kernels for 15%

profile of v7, /device:TPU:0, one launch (start us, length us, event | category | flops | bytes accessed | tf_op | source)
XLA Modules:
  0.0 35.2 jit_solution(7210114375424904658)
XLA Ops:
  0.0 0.1 pad_add_fusion.1.where_ref
  0.1 0.8 %pad_add_fusion.small_ref = f32[24,512]{1,0:T(8,128)S(1)} fusion(f32[1,16]{1,0:T(1,128)} %bitcast.21, s32[1,16]{1,0:T(1,128)} %bitcast.22, s32[1,512]{1,0:T(1,128)} %bitcast.20, s32[16,16]{1,0:T(8,128)} %param.8), kind=kLoop, calls=%fused_computation | loop fusion | flops 49152 | bytes 52352 | tf_op jit(solution)/shard_map/add | solution.py:142
  0.8 0.0 copy-start
  0.8 0.9 %copy-done = bf16[16,16,2,256]{3,2,1,0:T(2,128)(2,1)S(1)} copy-done((bf16[16,16,2,256]{3,2,1,0:T(2,128)(2,1)S(1)}, bf16[16,16,2,256]{3,2,1,0:T(2,128)(2,1)}, u32[]{:S(2)}) %copy-start) | copy-done | bytes 262168
  1.8 1.6 %pack.1 = (bf16[208,256]{1,0:T(8,128)(2,1)S(1)}, bf16[208,256]{1,0:T(8,128)(2,1)S(1)}, bf16[208,256]{1,0:T(8,128)(2,1)S(1)}, bf16[208,256]{1,0:T(8,128)(2,1)S(1)}) custom-call(s32[3]{0:T(128)S(1)} %pad_add_fusion.1.where_ref, f32[24,512]{1,0:T(8,128)S(1)} %pad_add_fusion.small_ref, bf16[256,2,256]{2,1,0:T(2,128)(2,1)S(1)} %bitcast.17), custom_call_target="tpu_custom_call" | custom-call | tf_op jit(solution)/shard_map/pack/pallas_call | solution.py:144
  3.4 3.1 %collective-permute-start = (bf16[208,256]{1,0:T(8,128)(2,1)S(1)}, bf16[208,256]{1,0:T(8,128)(2,1)S(1)}, u32[]{:S(2)}, u32[]{:S(2)}) collective-permute-start(bf16[208,256]{1,0:T(8,128)(2,1)S(1)} %get-tuple-element.18), channel_id=1, source_target_pairs={{0,4},{4,8},{8,12},{12,0},{1,5},{5,9},{9,13},{13,1},{2,6},{6,10},{... | collective-permute-start | bytes 319496 | tf_op jit(solution)/shard_map/ppermute | solution.py:424
  6.5 2.6 %collective-permute-start.3 = (bf16[208,256]{1,0:T(8,128)(2,1)S(1)}, bf16[208,256]{1,0:T(8,128)(2,1)S(1)}, u32[]{:S(2)}, u32[]{:S(2)}) collective-permute-start(bf16[208,256]{1,0:T(8,128)(2,1)S(1)} %get-tuple-element.19), channel_id=1, source_target_pairs={{0,8},{4,12},{8,0},{12,4},{1,9},{5,13},{9,1},{13,5},{2,10},{6,14},... | collective-permute-start | bytes 319496 | tf_op jit(solution)/shard_map/ppermute | solution.py:424
  9.1 1.3 %collective-permute-start.4 = (bf16[208,256]{1,0:T(8,128)(2,1)S(1)}, bf16[208,256]{1,0:T(8,128)(2,1)S(1)}, u32[]{:S(2)}, u32[]{:S(2)}) collective-permute-start(bf16[208,256]{1,0:T(8,128)(2,1)S(1)} %get-tuple-element.20), channel_id=1, source_target_pairs={{0,12},{4,0},{8,4},{12,8},{1,13},{5,1},{9,5},{13,9},{2,14},{6,2},{... | collective-permute-start | bytes 319496 | tf_op jit(solution)/shard_map/ppermute | solution.py:424
  10.4 1.5 %collective-permute-start.7 = (bf16[208,256]{1,0:T(8,128)(2,1)S(1)}, bf16[208,256]{1,0:T(8,128)(2,1)S(1)}, u32[]{:S(2)}, u32[]{:S(2)}) collective-permute-start(bf16[208,256]{1,0:T(8,128)(2,1)S(1)} %get-tuple-element.17.x_ref), channel_id=1, source_target_pairs={{0,2},{2,0},{1,3},{3,1},{4,6},{6,4},{5,7},{7,5},{8,10},{10,8},{9,1... | collective-permute-start | bytes 319496 | tf_op jit(solution)/shard_map/ppermute | solution.py:424
  11.9 1.8 %constant_dynamic-slice_fusion = bf16[128,8,2,1,2,256]{5,1,4,3,2,0:T(8,128)(2,1)S(1)} fusion(bf16[128,8,2,2,2,256]{5,1,4,3,2,0:T(8,128)(2,1)} %bitcast.19, s32[]{:T(128)S(6)} %select_n.4), kind=kLoop, calls=%fused_computation.3 | loop fusion | bytes 4194308 | tf_op jit(solution)/shard_map/jit(dynamic_index_in_dim)/dynamic_slice | solution.py:447
  13.7 0.1 copy.7
  13.9 0.7 %copy.8 = bf16[64,8,8,256]{3,1,2,0:T(8,128)(2,1)S(1)} copy(bf16[64,8,8,256]{3,2,1,0:T(8,128)(2,1)S(1)} %bitcast.18) | data formatting | bytes 4194304
  14.6 0.1 collective-permute-start.1
  14.6 0.0 collective-permute-done.refs_1_.refs_0_
  14.7 0.5 %collective-permute-start.2 = (bf16[208,256]{1,0:T(8,128)(2,1)S(1)}, bf16[208,256]{1,0:T(8,128)(2,1)S(1)}, u32[]{:S(2)}, u32[]{:S(2)}) collective-permute-start(bf16[208,256]{1,0:T(8,128)(2,1)S(1)} %collective-permute-done.refs_1_.refs_0_), channel_id=1, source_target_pairs={{0,1},{1,0},{2,3},{3,2},{4,5},{5,4},{6,7},{7,6},{8,9},{9,8},{10,11... | collective-permute-start | bytes 319496 | tf_op jit(solution)/shard_map/ppermute | solution.py:424
  15.1 1.0 %collective-permute-done.3.refs_4_.refs_1_ = bf16[208,256]{1,0:T(8,128)(2,1)S(1)} collective-permute-done((bf16[208,256]{1,0:T(8,128)(2,1)S(1)}, bf16[208,256]{1,0:T(8,128)(2,1)S(1)}, u32[]{:S(2)}, u32[]{:S(2)}) %collective-permute-start.3) | collective-permute-done | bytes 106528 | tf_op jit(solution)/shard_map/ppermute | solution.py:424
  16.2 0.0 collective-permute-start.5
  16.2 0.0 collective-permute-done.4.refs_5_.refs_2_
  16.2 0.5 %collective-permute-start.6 = (bf16[208,256]{1,0:T(8,128)(2,1)S(1)}, bf16[208,256]{1,0:T(8,128)(2,1)S(1)}, u32[]{:S(2)}, u32[]{:S(2)}) collective-permute-start(bf16[208,256]{1,0:T(8,128)(2,1)S(1)} %collective-permute-done.4.refs_5_.refs_2_), channel_id=1, source_target_pairs={{0,1},{1,0},{2,3},{3,2},{4,5},{5,4},{6,7},{7,6},{8,9},{9,8},{10,11... | collective-permute-start | bytes 319496 | tf_op jit(solution)/shard_map/ppermute | solution.py:424
  16.7 0.0 collective-permute-done.7.refs_9_.refs_0_
  16.7 1.6 %collective-permute-start.11 = (bf16[624,256]{1,0:T(8,128)(2,1)S(1)}, bf16[624,256]{1,0:T(8,128)(2,1)S(1)}, u32[]{:S(2)}, u32[]{:S(2)}) collective-permute-start(bf16[624,256]{1,0:T(8,128)(2,1)S(1)} %stack.18), channel_id=1, source_target_pairs={{0,2},{2,0},{1,3},{3,1},{4,6},{6,4},{5,7},{7,5},{8,10},{10,8},{9,1... | collective-permute-start | bytes 958472 | tf_op jit(solution)/shard_map/ppermute | solution.py:424
  18.3 0.0 collective-permute-done.1.refs_2_
  18.3 0.0 collective-permute-done.2.refs_3_
  18.3 0.0 collective-permute-done.5.refs_6_
  18.3 0.0 collective-permute-done.6.refs_7_
  18.3 1.9 %forward.1.refs_8_ = f32[8,128]{1,0:T(8,128)S(1)} custom-call(bf16[208,256]{1,0:T(8,128)(2,1)S(1)} %after.1.refs_0_, bf16[208,256]{1,0:T(8,128)(2,1)S(1)} %collective-permute-done.refs_1_.refs_0_, bf16[208,256]{1,0:T(8,128)(2,1)S(1)} %collective-permute-done.1.refs_2_, bf16[208,256]{1,0:T(8,128)(2,1)S(1)} %collective-permute-done.2.refs_3_, ...), custom_call_target="tpu_custom_call" | custom-call | tf_op jit(solution)/shard_map/forward/pallas_call | solution.py:263
  20.2 3.8 %collective-permute-start.10 = (f32[8,128]{1,0:T(8,128)S(1)}, f32[8,128]{1,0:T(8,128)S(1)}, u32[]{:S(2)}, u32[]{:S(2)}) collective-permute-start(f32[8,128]{1,0:T(8,128)S(1)} %forward.1.refs_8_), channel_id=1, source_target_pairs={{0,12},{4,8},{8,4},{12,0},{1,13},{5,9},{9,5},{13,1},{2,14},{6,10},... | collective-permute-start | bytes 12296 | tf_op jit(solution)/shard_map/ppermute | solution.py:430
  24.0 0.0 collective-permute-start.9
  24.0 0.6 %collective-permute-start.8 = (f32[8,128]{1,0:T(8,128)S(1)}, f32[8,128]{1,0:T(8,128)S(1)}, u32[]{:S(2)}, u32[]{:S(2)}) collective-permute-start(f32[8,128]{1,0:T(8,128)S(1)} %forward.1.refs_8_), channel_id=1, source_target_pairs={{0,4},{4,0},{8,12},{12,8},{1,5},{5,1},{9,13},{13,9},{2,6},{6,2},{1... | collective-permute-start | bytes 12296 | tf_op jit(solution)/shard_map/ppermute | solution.py:430
  24.6 0.7 %prepare0.2 = (bf16[384,2048]{1,0:T(8,128)(2,1)S(1)}, bf16[128,384]{1,0:T(8,128)(2,1)S(1)}, bf16[128,384]{1,0:T(8,128)(2,1)S(1)}, f32[8,384]{1,0:T(8,128)S(1)}) custom-call(bf16[208,256]{1,0:T(8,128)(2,1)S(1)} %after.1.refs_0_, bf16[208,256]{1,0:T(8,128)(2,1)S(1)} %collective-permute-done.refs_1_.refs_0_, ...), custom_call_target="tpu_custom_call" | custom-call | bytes 294912 | tf_op jit(solution)/shard_map/prepare0/pallas_call | solution.py:304
  25.4 0.2 collective-permute-done.10
  25.6 2.9 %collective-permute-done.9 = f32[8,128]{1,0:T(8,128)S(1)} collective-permute-done((f32[8,128]{1,0:T(8,128)S(1)}, f32[8,128]{1,0:T(8,128)S(1)}, u32[]{:S(2)}, u32[]{:S(2)}) %collective-permute-start.9) | collective-permute-done | bytes 4128 | tf_op jit(solution)/shard_map/ppermute | solution.py:430
  28.5 0.0 collective-permute-done.8
  28.5 0.0 collective-permute-done.11.refs_1_
  28.6 0.1 collective-permute-start.12
  28.6 0.9 %collective-permute-start.13 = (f32[8,128]{1,0:T(8,128)S(1)}, f32[8,128]{1,0:T(8,128)S(1)}, u32[]{:S(2)}, u32[]{:S(2)}) collective-permute-start(f32[8,128]{1,0:T(8,128)S(1)} %add_add_fusion.obs_ref.refs_2_), channel_id=1, source_target_pairs={{0,2},{2,0},{1,3},{3,1},{4,6},{6,4},{5,7},{7,5},{8,10},{10,8},{9,1... | collective-permute-start | bytes 12296 | tf_op jit(solution)/shard_map/ppermute | solution.py:424
  29.5 1.9 %own_adjoint.1.before_ref = f32[256,2048]{1,0:T(8,128)S(1)} custom-call(s32[3]{0:T(128)S(1)} %pad_add_fusion.1.where_ref, bf16[384,2048]{1,0:T(8,128)(2,1)S(1)} %get-tuple-element.21.f8_ref, bf16[128,384]{1,0:T(8,128)(2,1)S(1)} %get-tuple-element.22.own_ref, bf16[128,384]{1,0:T(8,128)(2,1)S(1)} %get-tuple-element.23.to_r_ref, ...), custom_call_target="tpu_custom_call" | custom-call | flops 805306368 | bytes 1572864 | tf_op jit(solution)/shard_map/own_adjoint/pallas_call | solution.py:349
  31.4 0.0 collective-permute-done.12.refs_1_
  31.5 0.7 %prepare0.3 = (bf16[384,2048]{1,0:T(8,128)(2,1)S(1)}, bf16[128,384]{1,0:T(8,128)(2,1)S(1)}, bf16[128,384]{1,0:T(8,128)(2,1)S(1)}, f32[8,384]{1,0:T(8,128)S(1)}) custom-call(bf16[832,256]{1,0:T(8,128)(2,1)S(1)} %stack.19.refs_0_, bf16[832,256]{1,0:T(8,128)(2,1)S(1)} %collective-permute-done.12.refs_1_), custom_call_target="tpu_custom_call" | custom-call | bytes 294912 | tf_op jit(solution)/shard_map/prepare0/pallas_call | solution.py:304
  32.2 0.1 collective-permute-done.13.refs_0_
  32.3 2.9 %adjoint.1 = f32[1024,512]{1,0:T(8,128)} custom-call(s32[3]{0:T(128)S(1)} %pad_add_fusion.1.where_ref, f32[256,2048]{1,0:T(8,128)S(1)} %own_adjoint.1.before_ref, bf16[384,2048]{1,0:T(8,128)(2,1)S(1)} %get-tuple-element.25.f8_ref, bf16[128,384]{1,0:T(8,128)(2,1)S(1)} %get-tuple-element.26.own_ref, bf16[128,384]{1,0:T(8,128)(2,1)S(1)} %get-tuple-element.27.to_r_ref, ...), custom_call_target="tpu_custom_call" | custom-call | tf_op jit(solution)/shard_map/adjoint/pallas_call | solution.py:407
  (4 shorter events, 0.1 us)
Async XLA Ops:
  0.8 1.0 %copy-start = (bf16[16,16,2,256]{3,2,1,0:T(2,128)(2,1)S(1)}, bf16[16,16,2,256]{3,2,1,0:T(2,128)(2,1)}, u32[]{:S(2)}) copy-start(bf16[16,16,2,256]{3,2,1,0:T(2,128)(2,1)} %param.7) | copy-start | bytes 786436
  3.4 11.2 %collective-permute-start = (bf16[208,256]{1,0:T(8,128)(2,1)S(1)}, bf16[208,256]{1,0:T(8,128)(2,1)S(1)}, u32[]{:S(2)}, u32[]{:S(2)}) collective-permute-start(bf16[208,256]{1,0:T(8,128)(2,1)S(1)} %get-tuple-element.18), channel_id=1, source_target_pairs={{0,4},{4,8},{8,12},{12,0},{1,5},{5,9},{9,13},{13,1},{2,6},{6,10},{... | collective-permute-start | bytes 319496 | tf_op jit(solution)/shard_map/ppermute | solution.py:424
  6.5 9.7 %collective-permute-start.3 = (bf16[208,256]{1,0:T(8,128)(2,1)S(1)}, bf16[208,256]{1,0:T(8,128)(2,1)S(1)}, u32[]{:S(2)}, u32[]{:S(2)}) collective-permute-start(bf16[208,256]{1,0:T(8,128)(2,1)S(1)} %get-tuple-element.19), channel_id=1, source_target_pairs={{0,8},{4,12},{8,0},{12,4},{1,9},{5,13},{9,1},{13,5},{2,10},{6,14},... | collective-permute-start | bytes 319496 | tf_op jit(solution)/shard_map/ppermute | solution.py:424
  9.1 7.1 %collective-permute-start.4 = (bf16[208,256]{1,0:T(8,128)(2,1)S(1)}, bf16[208,256]{1,0:T(8,128)(2,1)S(1)}, u32[]{:S(2)}, u32[]{:S(2)}) collective-permute-start(bf16[208,256]{1,0:T(8,128)(2,1)S(1)} %get-tuple-element.20), channel_id=1, source_target_pairs={{0,12},{4,0},{8,4},{12,8},{1,13},{5,1},{9,5},{13,9},{2,14},{6,2},{... | collective-permute-start | bytes 319496 | tf_op jit(solution)/shard_map/ppermute | solution.py:424
  10.4 6.3 %collective-permute-start.7 = (bf16[208,256]{1,0:T(8,128)(2,1)S(1)}, bf16[208,256]{1,0:T(8,128)(2,1)S(1)}, u32[]{:S(2)}, u32[]{:S(2)}) collective-permute-start(bf16[208,256]{1,0:T(8,128)(2,1)S(1)} %get-tuple-element.17.x_ref), channel_id=1, source_target_pairs={{0,2},{2,0},{1,3},{3,1},{4,6},{6,4},{5,7},{7,5},{8,10},{10,8},{9,1... | collective-permute-start | bytes 319496 | tf_op jit(solution)/shard_map/ppermute | solution.py:424
  14.6 3.7 %collective-permute-start.1 = (bf16[208,256]{1,0:T(8,128)(2,1)S(1)}, bf16[208,256]{1,0:T(8,128)(2,1)S(1)}, u32[]{:S(2)}, u32[]{:S(2)}) collective-permute-start(bf16[208,256]{1,0:T(8,128)(2,1)S(1)} %after.1.refs_0_), channel_id=1, source_target_pairs={{0,1},{1,0},{2,3},{3,2},{4,5},{5,4},{6,7},{7,6},{8,9},{9,8},{10,11... | collective-permute-start | bytes 319496 | tf_op jit(solution)/shard_map/ppermute | solution.py:424
  14.7 3.6 %collective-permute-start.2 = (bf16[208,256]{1,0:T(8,128)(2,1)S(1)}, bf16[208,256]{1,0:T(8,128)(2,1)S(1)}, u32[]{:S(2)}, u32[]{:S(2)}) collective-permute-start(bf16[208,256]{1,0:T(8,128)(2,1)S(1)} %collective-permute-done.refs_1_.refs_0_), channel_id=1, source_target_pairs={{0,1},{1,0},{2,3},{3,2},{4,5},{5,4},{6,7},{7,6},{8,9},{9,8},{10,11... | collective-permute-start | bytes 319496 | tf_op jit(solution)/shard_map/ppermute | solution.py:424
  16.2 2.1 %collective-permute-start.5 = (bf16[208,256]{1,0:T(8,128)(2,1)S(1)}, bf16[208,256]{1,0:T(8,128)(2,1)S(1)}, u32[]{:S(2)}, u32[]{:S(2)}) collective-permute-start(bf16[208,256]{1,0:T(8,128)(2,1)S(1)} %collective-permute-done.3.refs_4_.refs_1_), channel_id=1, source_target_pairs={{0,1},{1,0},{2,3},{3,2},{4,5},{5,4},{6,7},{7,6},{8,9},{9,8},{10,11... | collective-permute-start | bytes 319496 | tf_op jit(solution)/shard_map/ppermute | solution.py:424
  16.2 2.1 %collective-permute-start.6 = (bf16[208,256]{1,0:T(8,128)(2,1)S(1)}, bf16[208,256]{1,0:T(8,128)(2,1)S(1)}, u32[]{:S(2)}, u32[]{:S(2)}) collective-permute-start(bf16[208,256]{1,0:T(8,128)(2,1)S(1)} %collective-permute-done.4.refs_5_.refs_2_), channel_id=1, source_target_pairs={{0,1},{1,0},{2,3},{3,2},{4,5},{5,4},{6,7},{7,6},{8,9},{9,8},{10,11... | collective-permute-start | bytes 319496 | tf_op jit(solution)/shard_map/ppermute | solution.py:424
  16.7 11.8 %collective-permute-start.11 = (bf16[624,256]{1,0:T(8,128)(2,1)S(1)}, bf16[624,256]{1,0:T(8,128)(2,1)S(1)}, u32[]{:S(2)}, u32[]{:S(2)}) collective-permute-start(bf16[624,256]{1,0:T(8,128)(2,1)S(1)} %stack.18), channel_id=1, source_target_pairs={{0,2},{2,0},{1,3},{3,1},{4,6},{6,4},{5,7},{7,5},{8,10},{10,8},{9,1... | collective-permute-start | bytes 958472 | tf_op jit(solution)/shard_map/ppermute | solution.py:424
  20.2 5.4 %collective-permute-start.10 = (f32[8,128]{1,0:T(8,128)S(1)}, f32[8,128]{1,0:T(8,128)S(1)}, u32[]{:S(2)}, u32[]{:S(2)}) collective-permute-start(f32[8,128]{1,0:T(8,128)S(1)} %forward.1.refs_8_), channel_id=1, source_target_pairs={{0,12},{4,8},{8,4},{12,0},{1,13},{5,9},{9,5},{13,1},{2,14},{6,10},... | collective-permute-start | bytes 12296 | tf_op jit(solution)/shard_map/ppermute | solution.py:430
  24.0 4.5 %collective-permute-start.9 = (f32[8,128]{1,0:T(8,128)S(1)}, f32[8,128]{1,0:T(8,128)S(1)}, u32[]{:S(2)}, u32[]{:S(2)}) collective-permute-start(f32[8,128]{1,0:T(8,128)S(1)} %forward.1.refs_8_), channel_id=1, source_target_pairs={{0,8},{4,12},{8,0},{12,4},{1,9},{5,13},{9,1},{13,5},{2,10},{6,14},... | collective-permute-start | bytes 12296 | tf_op jit(solution)/shard_map/ppermute | solution.py:430
  24.0 4.5 %collective-permute-start.8 = (f32[8,128]{1,0:T(8,128)S(1)}, f32[8,128]{1,0:T(8,128)S(1)}, u32[]{:S(2)}, u32[]{:S(2)}) collective-permute-start(f32[8,128]{1,0:T(8,128)S(1)} %forward.1.refs_8_), channel_id=1, source_target_pairs={{0,4},{4,0},{8,12},{12,8},{1,5},{5,1},{9,13},{13,9},{2,6},{6,2},{1... | collective-permute-start | bytes 12296 | tf_op jit(solution)/shard_map/ppermute | solution.py:430
  28.6 2.9 %collective-permute-start.12 = (bf16[832,256]{1,0:T(8,128)(2,1)S(1)}, bf16[832,256]{1,0:T(8,128)(2,1)S(1)}, u32[]{:S(2)}, u32[]{:S(2)}) collective-permute-start(bf16[832,256]{1,0:T(8,128)(2,1)S(1)} %stack.19.refs_0_), channel_id=1, source_target_pairs={{0,1},{1,0},{2,3},{3,2},{4,5},{5,4},{6,7},{7,6},{8,9},{9,8},{10,11... | collective-permute-start | bytes 1277960 | tf_op jit(solution)/shard_map/ppermute | solution.py:424
  28.6 3.7 %collective-permute-start.13 = (f32[8,128]{1,0:T(8,128)S(1)}, f32[8,128]{1,0:T(8,128)S(1)}, u32[]{:S(2)}, u32[]{:S(2)}) collective-permute-start(f32[8,128]{1,0:T(8,128)S(1)} %add_add_fusion.obs_ref.refs_2_), channel_id=1, source_target_pairs={{0,2},{2,0},{1,3},{3,1},{4,6},{6,4},{5,7},{7,5},{8,10},{10,8},{9,1... | collective-permute-start | bytes 12296 | tf_op jit(solution)/shard_map/ppermute | solution.py:424

commit v8 on v7

--- a/solution.py
+++ b/solution.py
@@ -111,8 +111,8 @@
     fp = fp_ref[...].reshape(cols, fp_ref.shape[2])
     for w in range(w2):
         slot_w = jnp.where(w_of == w, slot, -1)
-        pick = mask(iota((padded, cols), 0) == slot_w).astype(BF16)
-        moved = nn(pick, fp).astype(BF16)
+        pick = mask(iota((used if w else padded, cols), 0) == slot_w).astype(BF16)
+        moved = nn(pick[0:used], fp).astype(BF16)
         for d in range(n):
             outs[d][w * capp : (w + 1) * capp, :] = moved[d * capp : (d + 1) * capp]
         if w == 0:

time: 35.5 us -> 35.3 us (level)
  no operation moved by 1% of the time
where the time goes in v8:
time: 35.3 us; the launch traced here: 35.1 us
  starting transfers between devices  16.5 us (47%)
  Pallas kernels  9.82 us (28%)
  waiting for transfers between devices  4.28 us (12%)
  local copies, waits for them, and re-layouts  3.55 us (10%)
  other arithmetic  0.84 us (2%)
    ppermute x11, starting transfers between devices, shift(): return lax.ppermute(x, axis, [(i, (i + d) % n) for i in range(n)])  12.1 us
    ppermute x3, starting transfers between devices, swap(): return lax.ppermute(x, axis, [(i, i ^ bits) for i in range(n)])  4.42 us
    ppermute x3, waiting for transfers between devices, swap(): return lax.ppermute(x, axis, [(i, i ^ bits) for i in range(n)])  3.12 us
    pallas_call x1, Pallas kernels, adjoint(): pl.pallas_call(functools.partial(adjoint_kernel, cfg), out_shape=jax.Shap...  2.93 us
    dynamic_slice x2, local copies, waits for them, and re-layouts, shards(): lax.dynamic_index_in_dim(probes.reshape(local, hours, nreg, ntm, kd, cell...  1.93 us
    pallas_call x1, Pallas kernels, own_adjoint(): pl.pallas_call(functools.partial(own_adjoint_kernel, cfg), out_shape=jax....  1.9 us
    pallas_call x1, Pallas kernels, forward(): pl.pallas_call(functools.partial(forward_kernel, cfg, counts), out_shape=...  1.89 us
    unnamed x3, local copies, waits for them, and re-layouts  1.62 us
  transfers between devices with their start and end apart: 14, of which 4 were waited for; matrix products, arithmetic and copies ran while one was open for 7% of the time, Pallas kernels for 15%

profile of v8, /device:TPU:0, one launch (start us, length us, event | category | flops | bytes accessed | tf_op | source)
XLA Modules:
  0.0 35.1 jit_solution(5027798127806712524)
XLA Ops:
  0.0 0.1 pad_add_fusion.1.where_ref
  0.1 0.8 %pad_add_fusion.small_ref = f32[24,512]{1,0:T(8,128)S(1)} fusion(f32[1,16]{1,0:T(1,128)} %bitcast.21, s32[1,16]{1,0:T(1,128)} %bitcast.22, s32[1,512]{1,0:T(1,128)} %bitcast.20, s32[16,16]{1,0:T(8,128)} %param.8), kind=kLoop, calls=%fused_computation | loop fusion | flops 49152 | bytes 52352 | tf_op jit(solution)/shard_map/add | solution.py:142
  0.8 0.0 copy-start
  0.8 0.9 %copy-done = bf16[16,16,2,256]{3,2,1,0:T(2,128)(2,1)S(1)} copy-done((bf16[16,16,2,256]{3,2,1,0:T(2,128)(2,1)S(1)}, bf16[16,16,2,256]{3,2,1,0:T(2,128)(2,1)}, u32[]{:S(2)}) %copy-start) | copy-done | bytes 262168
  1.8 1.6 %pack.1 = (bf16[208,256]{1,0:T(8,128)(2,1)S(1)}, bf16[208,256]{1,0:T(8,128)(2,1)S(1)}, bf16[208,256]{1,0:T(8,128)(2,1)S(1)}, bf16[208,256]{1,0:T(8,128)(2,1)S(1)}) custom-call(s32[3]{0:T(128)S(1)} %pad_add_fusion.1.where_ref, f32[24,512]{1,0:T(8,128)S(1)} %pad_add_fusion.small_ref, bf16[256,2,256]{2,1,0:T(2,128)(2,1)S(1)} %bitcast.17), custom_call_target="tpu_custom_call" | custom-call | tf_op jit(solution)/shard_map/pack/pallas_call | solution.py:144
  3.4 3.0 %collective-permute-start = (bf16[208,256]{1,0:T(8,128)(2,1)S(1)}, bf16[208,256]{1,0:T(8,128)(2,1)S(1)}, u32[]{:S(2)}, u32[]{:S(2)}) collective-permute-start(bf16[208,256]{1,0:T(8,128)(2,1)S(1)} %get-tuple-element.18), channel_id=1, source_target_pairs={{0,4},{4,8},{8,12},{12,0},{1,5},{5,9},{9,13},{13,1},{2,6},{6,10},{... | collective-permute-start | bytes 319496 | tf_op jit(solution)/shard_map/ppermute | solution.py:424
  6.4 2.6 %collective-permute-start.3 = (bf16[208,256]{1,0:T(8,128)(2,1)S(1)}, bf16[208,256]{1,0:T(8,128)(2,1)S(1)}, u32[]{:S(2)}, u32[]{:S(2)}) collective-permute-start(bf16[208,256]{1,0:T(8,128)(2,1)S(1)} %get-tuple-element.19), channel_id=1, source_target_pairs={{0,8},{4,12},{8,0},{12,4},{1,9},{5,13},{9,1},{13,5},{2,10},{6,14},... | collective-permute-start | bytes 319496 | tf_op jit(solution)/shard_map/ppermute | solution.py:424
  9.0 1.3 %collective-permute-start.4 = (bf16[208,256]{1,0:T(8,128)(2,1)S(1)}, bf16[208,256]{1,0:T(8,128)(2,1)S(1)}, u32[]{:S(2)}, u32[]{:S(2)}) collective-permute-start(bf16[208,256]{1,0:T(8,128)(2,1)S(1)} %get-tuple-element.20), channel_id=1, source_target_pairs={{0,12},{4,0},{8,4},{12,8},{1,13},{5,1},{9,5},{13,9},{2,14},{6,2},{... | collective-permute-start | bytes 319496 | tf_op jit(solution)/shard_map/ppermute | solution.py:424
  10.3 1.5 %collective-permute-start.7 = (bf16[208,256]{1,0:T(8,128)(2,1)S(1)}, bf16[208,256]{1,0:T(8,128)(2,1)S(1)}, u32[]{:S(2)}, u32[]{:S(2)}) collective-permute-start(bf16[208,256]{1,0:T(8,128)(2,1)S(1)} %get-tuple-element.17.x_ref), channel_id=1, source_target_pairs={{0,2},{2,0},{1,3},{3,1},{4,6},{6,4},{5,7},{7,5},{8,10},{10,8},{9,1... | collective-permute-start | bytes 319496 | tf_op jit(solution)/shard_map/ppermute | solution.py:424
  11.8 1.8 %constant_dynamic-slice_fusion = bf16[128,8,2,1,2,256]{5,1,4,3,2,0:T(8,128)(2,1)S(1)} fusion(bf16[128,8,2,2,2,256]{5,1,4,3,2,0:T(8,128)(2,1)} %bitcast.19, s32[]{:T(128)S(6)} %select_n.4), kind=kLoop, calls=%fused_computation.3 | loop fusion | bytes 4194308 | tf_op jit(solution)/shard_map/jit(dynamic_index_in_dim)/dynamic_slice | solution.py:447
  13.6 0.1 copy.7
  13.8 0.7 %copy.8 = bf16[64,8,8,256]{3,1,2,0:T(8,128)(2,1)S(1)} copy(bf16[64,8,8,256]{3,2,1,0:T(8,128)(2,1)S(1)} %bitcast.18) | data formatting | bytes 4194304
  14.5 0.1 collective-permute-start.1
  14.5 0.0 collective-permute-done.refs_1_.refs_0_
  14.6 0.5 %collective-permute-start.2 = (bf16[208,256]{1,0:T(8,128)(2,1)S(1)}, bf16[208,256]{1,0:T(8,128)(2,1)S(1)}, u32[]{:S(2)}, u32[]{:S(2)}) collective-permute-start(bf16[208,256]{1,0:T(8,128)(2,1)S(1)} %collective-permute-done.refs_1_.refs_0_), channel_id=1, source_target_pairs={{0,1},{1,0},{2,3},{3,2},{4,5},{5,4},{6,7},{7,6},{8,9},{9,8},{10,11... | collective-permute-start | bytes 319496 | tf_op jit(solution)/shard_map/ppermute | solution.py:424
  15.0 1.0 %collective-permute-done.3.refs_4_.refs_1_ = bf16[208,256]{1,0:T(8,128)(2,1)S(1)} collective-permute-done((bf16[208,256]{1,0:T(8,128)(2,1)S(1)}, bf16[208,256]{1,0:T(8,128)(2,1)S(1)}, u32[]{:S(2)}, u32[]{:S(2)}) %collective-permute-start.3) | collective-permute-done | bytes 106528 | tf_op jit(solution)/shard_map/ppermute | solution.py:424
  16.1 0.0 collective-permute-start.5
  16.1 0.0 collective-permute-done.4.refs_5_.refs_2_
  16.1 0.5 %collective-permute-start.6 = (bf16[208,256]{1,0:T(8,128)(2,1)S(1)}, bf16[208,256]{1,0:T(8,128)(2,1)S(1)}, u32[]{:S(2)}, u32[]{:S(2)}) collective-permute-start(bf16[208,256]{1,0:T(8,128)(2,1)S(1)} %collective-permute-done.4.refs_5_.refs_2_), channel_id=1, source_target_pairs={{0,1},{1,0},{2,3},{3,2},{4,5},{5,4},{6,7},{7,6},{8,9},{9,8},{10,11... | collective-permute-start | bytes 319496 | tf_op jit(solution)/shard_map/ppermute | solution.py:424
  16.6 0.0 collective-permute-done.7.refs_9_.refs_0_
  16.6 1.6 %collective-permute-start.11 = (bf16[624,256]{1,0:T(8,128)(2,1)S(1)}, bf16[624,256]{1,0:T(8,128)(2,1)S(1)}, u32[]{:S(2)}, u32[]{:S(2)}) collective-permute-start(bf16[624,256]{1,0:T(8,128)(2,1)S(1)} %stack.18), channel_id=1, source_target_pairs={{0,2},{2,0},{1,3},{3,1},{4,6},{6,4},{5,7},{7,5},{8,10},{10,8},{9,1... | collective-permute-start | bytes 958472 | tf_op jit(solution)/shard_map/ppermute | solution.py:424
  18.2 0.0 collective-permute-done.1.refs_2_
  18.2 0.0 collective-permute-done.2.refs_3_
  18.2 0.0 collective-permute-done.5.refs_6_
  18.2 0.0 collective-permute-done.6.refs_7_
  18.2 1.9 %forward.1.refs_8_ = f32[8,128]{1,0:T(8,128)S(1)} custom-call(bf16[208,256]{1,0:T(8,128)(2,1)S(1)} %after.1.refs_0_, bf16[208,256]{1,0:T(8,128)(2,1)S(1)} %collective-permute-done.refs_1_.refs_0_, bf16[208,256]{1,0:T(8,128)(2,1)S(1)} %collective-permute-done.1.refs_2_, bf16[208,256]{1,0:T(8,128)(2,1)S(1)} %collective-permute-done.2.refs_3_, ...), custom_call_target="tpu_custom_call" | custom-call | tf_op jit(solution)/shard_map/forward/pallas_call | solution.py:263
  20.1 3.8 %collective-permute-start.10 = (f32[8,128]{1,0:T(8,128)S(1)}, f32[8,128]{1,0:T(8,128)S(1)}, u32[]{:S(2)}, u32[]{:S(2)}) collective-permute-start(f32[8,128]{1,0:T(8,128)S(1)} %forward.1.refs_8_), channel_id=1, source_target_pairs={{0,12},{4,8},{8,4},{12,0},{1,13},{5,9},{9,5},{13,1},{2,14},{6,10},... | collective-permute-start | bytes 12296 | tf_op jit(solution)/shard_map/ppermute | solution.py:430
  23.9 0.0 collective-permute-start.9
  23.9 0.6 %collective-permute-start.8 = (f32[8,128]{1,0:T(8,128)S(1)}, f32[8,128]{1,0:T(8,128)S(1)}, u32[]{:S(2)}, u32[]{:S(2)}) collective-permute-start(f32[8,128]{1,0:T(8,128)S(1)} %forward.1.refs_8_), channel_id=1, source_target_pairs={{0,4},{4,0},{8,12},{12,8},{1,5},{5,1},{9,13},{13,9},{2,6},{6,2},{1... | collective-permute-start | bytes 12296 | tf_op jit(solution)/shard_map/ppermute | solution.py:430
  24.5 0.7 %prepare0.2 = (bf16[384,2048]{1,0:T(8,128)(2,1)S(1)}, bf16[128,384]{1,0:T(8,128)(2,1)S(1)}, bf16[128,384]{1,0:T(8,128)(2,1)S(1)}, f32[8,384]{1,0:T(8,128)S(1)}) custom-call(bf16[208,256]{1,0:T(8,128)(2,1)S(1)} %after.1.refs_0_, bf16[208,256]{1,0:T(8,128)(2,1)S(1)} %collective-permute-done.refs_1_.refs_0_, ...), custom_call_target="tpu_custom_call" | custom-call | bytes 294912 | tf_op jit(solution)/shard_map/prepare0/pallas_call | solution.py:304
  25.3 0.2 collective-permute-done.10
  25.5 2.9 %collective-permute-done.9 = f32[8,128]{1,0:T(8,128)S(1)} collective-permute-done((f32[8,128]{1,0:T(8,128)S(1)}, f32[8,128]{1,0:T(8,128)S(1)}, u32[]{:S(2)}, u32[]{:S(2)}) %collective-permute-start.9) | collective-permute-done | bytes 4128 | tf_op jit(solution)/shard_map/ppermute | solution.py:430
  28.4 0.0 collective-permute-done.8
  28.4 0.0 collective-permute-done.11.refs_1_
  28.5 0.1 collective-permute-start.12
  28.5 0.9 %collective-permute-start.13 = (f32[8,128]{1,0:T(8,128)S(1)}, f32[8,128]{1,0:T(8,128)S(1)}, u32[]{:S(2)}, u32[]{:S(2)}) collective-permute-start(f32[8,128]{1,0:T(8,128)S(1)} %add_add_fusion.obs_ref.refs_2_), channel_id=1, source_target_pairs={{0,2},{2,0},{1,3},{3,1},{4,6},{6,4},{5,7},{7,5},{8,10},{10,8},{9,1... | collective-permute-start | bytes 12296 | tf_op jit(solution)/shard_map/ppermute | solution.py:424
  29.4 1.9 %own_adjoint.1.before_ref = f32[256,2048]{1,0:T(8,128)S(1)} custom-call(s32[3]{0:T(128)S(1)} %pad_add_fusion.1.where_ref, bf16[384,2048]{1,0:T(8,128)(2,1)S(1)} %get-tuple-element.21.f8_ref, bf16[128,384]{1,0:T(8,128)(2,1)S(1)} %get-tuple-element.22.own_ref, bf16[128,384]{1,0:T(8,128)(2,1)S(1)} %get-tuple-element.23.to_r_ref, ...), custom_call_target="tpu_custom_call" | custom-call | flops 805306368 | bytes 1572864 | tf_op jit(solution)/shard_map/own_adjoint/pallas_call | solution.py:349
  31.3 0.0 collective-permute-done.12.refs_1_
  31.4 0.7 %prepare0.3 = (bf16[384,2048]{1,0:T(8,128)(2,1)S(1)}, bf16[128,384]{1,0:T(8,128)(2,1)S(1)}, bf16[128,384]{1,0:T(8,128)(2,1)S(1)}, f32[8,384]{1,0:T(8,128)S(1)}) custom-call(bf16[832,256]{1,0:T(8,128)(2,1)S(1)} %stack.19.refs_0_, bf16[832,256]{1,0:T(8,128)(2,1)S(1)} %collective-permute-done.12.refs_1_), custom_call_target="tpu_custom_call" | custom-call | bytes 294912 | tf_op jit(solution)/shard_map/prepare0/pallas_call | solution.py:304
  32.1 0.1 collective-permute-done.13.refs_0_
  32.2 2.9 %adjoint.1 = f32[1024,512]{1,0:T(8,128)} custom-call(s32[3]{0:T(128)S(1)} %pad_add_fusion.1.where_ref, f32[256,2048]{1,0:T(8,128)S(1)} %own_adjoint.1.before_ref, bf16[384,2048]{1,0:T(8,128)(2,1)S(1)} %get-tuple-element.25.f8_ref, bf16[128,384]{1,0:T(8,128)(2,1)S(1)} %get-tuple-element.26.own_ref, bf16[128,384]{1,0:T(8,128)(2,1)S(1)} %get-tuple-element.27.to_r_ref, ...), custom_call_target="tpu_custom_call" | custom-call | tf_op jit(solution)/shard_map/adjoint/pallas_call | solution.py:407
  (4 shorter events, 0.1 us)
Async XLA Ops:
  0.8 1.0 %copy-start = (bf16[16,16,2,256]{3,2,1,0:T(2,128)(2,1)S(1)}, bf16[16,16,2,256]{3,2,1,0:T(2,128)(2,1)}, u32[]{:S(2)}) copy-start(bf16[16,16,2,256]{3,2,1,0:T(2,128)(2,1)} %param.7) | copy-start | bytes 786436
  3.4 11.2 %collective-permute-start = (bf16[208,256]{1,0:T(8,128)(2,1)S(1)}, bf16[208,256]{1,0:T(8,128)(2,1)S(1)}, u32[]{:S(2)}, u32[]{:S(2)}) collective-permute-start(bf16[208,256]{1,0:T(8,128)(2,1)S(1)} %get-tuple-element.18), channel_id=1, source_target_pairs={{0,4},{4,8},{8,12},{12,0},{1,5},{5,9},{9,13},{13,1},{2,6},{6,10},{... | collective-permute-start | bytes 319496 | tf_op jit(solution)/shard_map/ppermute | solution.py:424
  6.4 9.7 %collective-permute-start.3 = (bf16[208,256]{1,0:T(8,128)(2,1)S(1)}, bf16[208,256]{1,0:T(8,128)(2,1)S(1)}, u32[]{:S(2)}, u32[]{:S(2)}) collective-permute-start(bf16[208,256]{1,0:T(8,128)(2,1)S(1)} %get-tuple-element.19), channel_id=1, source_target_pairs={{0,8},{4,12},{8,0},{12,4},{1,9},{5,13},{9,1},{13,5},{2,10},{6,14},... | collective-permute-start | bytes 319496 | tf_op jit(solution)/shard_map/ppermute | solution.py:424
  9.0 7.1 %collective-permute-start.4 = (bf16[208,256]{1,0:T(8,128)(2,1)S(1)}, bf16[208,256]{1,0:T(8,128)(2,1)S(1)}, u32[]{:S(2)}, u32[]{:S(2)}) collective-permute-start(bf16[208,256]{1,0:T(8,128)(2,1)S(1)} %get-tuple-element.20), channel_id=1, source_target_pairs={{0,12},{4,0},{8,4},{12,8},{1,13},{5,1},{9,5},{13,9},{2,14},{6,2},{... | collective-permute-start | bytes 319496 | tf_op jit(solution)/shard_map/ppermute | solution.py:424
  10.3 6.3 %collective-permute-start.7 = (bf16[208,256]{1,0:T(8,128)(2,1)S(1)}, bf16[208,256]{1,0:T(8,128)(2,1)S(1)}, u32[]{:S(2)}, u32[]{:S(2)}) collective-permute-start(bf16[208,256]{1,0:T(8,128)(2,1)S(1)} %get-tuple-element.17.x_ref), channel_id=1, source_target_pairs={{0,2},{2,0},{1,3},{3,1},{4,6},{6,4},{5,7},{7,5},{8,10},{10,8},{9,1... | collective-permute-start | bytes 319496 | tf_op jit(solution)/shard_map/ppermute | solution.py:424
  14.5 3.7 %collective-permute-start.1 = (bf16[208,256]{1,0:T(8,128)(2,1)S(1)}, bf16[208,256]{1,0:T(8,128)(2,1)S(1)}, u32[]{:S(2)}, u32[]{:S(2)}) collective-permute-start(bf16[208,256]{1,0:T(8,128)(2,1)S(1)} %after.1.refs_0_), channel_id=1, source_target_pairs={{0,1},{1,0},{2,3},{3,2},{4,5},{5,4},{6,7},{7,6},{8,9},{9,8},{10,11... | collective-permute-start | bytes 319496 | tf_op jit(solution)/shard_map/ppermute | solution.py:424
  14.6 3.6 %collective-permute-start.2 = (bf16[208,256]{1,0:T(8,128)(2,1)S(1)}, bf16[208,256]{1,0:T(8,128)(2,1)S(1)}, u32[]{:S(2)}, u32[]{:S(2)}) collective-permute-start(bf16[208,256]{1,0:T(8,128)(2,1)S(1)} %collective-permute-done.refs_1_.refs_0_), channel_id=1, source_target_pairs={{0,1},{1,0},{2,3},{3,2},{4,5},{5,4},{6,7},{7,6},{8,9},{9,8},{10,11... | collective-permute-start | bytes 319496 | tf_op jit(solution)/shard_map/ppermute | solution.py:424
  16.1 2.1 %collective-permute-start.5 = (bf16[208,256]{1,0:T(8,128)(2,1)S(1)}, bf16[208,256]{1,0:T(8,128)(2,1)S(1)}, u32[]{:S(2)}, u32[]{:S(2)}) collective-permute-start(bf16[208,256]{1,0:T(8,128)(2,1)S(1)} %collective-permute-done.3.refs_4_.refs_1_), channel_id=1, source_target_pairs={{0,1},{1,0},{2,3},{3,2},{4,5},{5,4},{6,7},{7,6},{8,9},{9,8},{10,11... | collective-permute-start | bytes 319496 | tf_op jit(solution)/shard_map/ppermute | solution.py:424
  16.1 2.1 %collective-permute-start.6 = (bf16[208,256]{1,0:T(8,128)(2,1)S(1)}, bf16[208,256]{1,0:T(8,128)(2,1)S(1)}, u32[]{:S(2)}, u32[]{:S(2)}) collective-permute-start(bf16[208,256]{1,0:T(8,128)(2,1)S(1)} %collective-permute-done.4.refs_5_.refs_2_), channel_id=1, source_target_pairs={{0,1},{1,0},{2,3},{3,2},{4,5},{5,4},{6,7},{7,6},{8,9},{9,8},{10,11... | collective-permute-start | bytes 319496 | tf_op jit(solution)/shard_map/ppermute | solution.py:424
  16.6 11.8 %collective-permute-start.11 = (bf16[624,256]{1,0:T(8,128)(2,1)S(1)}, bf16[624,256]{1,0:T(8,128)(2,1)S(1)}, u32[]{:S(2)}, u32[]{:S(2)}) collective-permute-start(bf16[624,256]{1,0:T(8,128)(2,1)S(1)} %stack.18), channel_id=1, source_target_pairs={{0,2},{2,0},{1,3},{3,1},{4,6},{6,4},{5,7},{7,5},{8,10},{10,8},{9,1... | collective-permute-start | bytes 958472 | tf_op jit(solution)/shard_map/ppermute | solution.py:424
  20.1 5.4 %collective-permute-start.10 = (f32[8,128]{1,0:T(8,128)S(1)}, f32[8,128]{1,0:T(8,128)S(1)}, u32[]{:S(2)}, u32[]{:S(2)}) collective-permute-start(f32[8,128]{1,0:T(8,128)S(1)} %forward.1.refs_8_), channel_id=1, source_target_pairs={{0,12},{4,8},{8,4},{12,0},{1,13},{5,9},{9,5},{13,1},{2,14},{6,10},... | collective-permute-start | bytes 12296 | tf_op jit(solution)/shard_map/ppermute | solution.py:430
  23.9 4.5 %collective-permute-start.9 = (f32[8,128]{1,0:T(8,128)S(1)}, f32[8,128]{1,0:T(8,128)S(1)}, u32[]{:S(2)}, u32[]{:S(2)}) collective-permute-start(f32[8,128]{1,0:T(8,128)S(1)} %forward.1.refs_8_), channel_id=1, source_target_pairs={{0,8},{4,12},{8,0},{12,4},{1,9},{5,13},{9,1},{13,5},{2,10},{6,14},... | collective-permute-start | bytes 12296 | tf_op jit(solution)/shard_map/ppermute | solution.py:430
  23.9 4.5 %collective-permute-start.8 = (f32[8,128]{1,0:T(8,128)S(1)}, f32[8,128]{1,0:T(8,128)S(1)}, u32[]{:S(2)}, u32[]{:S(2)}) collective-permute-start(f32[8,128]{1,0:T(8,128)S(1)} %forward.1.refs_8_), channel_id=1, source_target_pairs={{0,4},{4,0},{8,12},{12,8},{1,5},{5,1},{9,13},{13,9},{2,6},{6,2},{1... | collective-permute-start | bytes 12296 | tf_op jit(solution)/shard_map/ppermute | solution.py:430
  28.5 2.9 %collective-permute-start.12 = (bf16[832,256]{1,0:T(8,128)(2,1)S(1)}, bf16[832,256]{1,0:T(8,128)(2,1)S(1)}, u32[]{:S(2)}, u32[]{:S(2)}) collective-permute-start(bf16[832,256]{1,0:T(8,128)(2,1)S(1)} %stack.19.refs_0_), channel_id=1, source_target_pairs={{0,1},{1,0},{2,3},{3,2},{4,5},{5,4},{6,7},{7,6},{8,9},{9,8},{10,11... | collective-permute-start | bytes 1277960 | tf_op jit(solution)/shard_map/ppermute | solution.py:424
  28.5 3.7 %collective-permute-start.13 = (f32[8,128]{1,0:T(8,128)S(1)}, f32[8,128]{1,0:T(8,128)S(1)}, u32[]{:S(2)}, u32[]{:S(2)}) collective-permute-start(f32[8,128]{1,0:T(8,128)S(1)} %add_add_fusion.obs_ref.refs_2_), channel_id=1, source_target_pairs={{0,2},{2,0},{1,3},{3,1},{4,6},{6,4},{5,7},{7,5},{8,10},{10,8},{9,1... | collective-permute-start | bytes 12296 | tf_op jit(solution)/shard_map/ppermute | solution.py:424

commit v9 on v8

--- a/solution.py
+++ b/solution.py
@@ -464,7 +464,7 @@
     rp = up(n * receptors, 128)
     partial = forward(cfg, own, probes_t, (8, rp), [b for group in across for b in group[:EARLY]])
     observed = partial
-    for d in range(1, n):
+    for d in (2, 1, *range(3, n)):
         observed = observed + swap(partial, "rcp", d)
     operands = prepare(cfg, 0, own, 1, rp, [], partial)
     before = own_adjoint(cfg, where, operands, observed)

time: 35.3 us -> 35.3 us (level)
  transfers between devices with their start and end apart: 14 -> 14, of which waited for: 4 -> 5; matrix products, arithmetic and copies ran while one was open for 7% -> 7% of each run, Pallas kernels for 15% -> 15%
where the time goes in v9:
time: 35.3 us; the launch traced here: 35.1 us
  starting transfers between devices  16.5 us (47%)
  Pallas kernels  9.82 us (28%)
  waiting for transfers between devices  4.28 us (12%)
  local copies, waits for them, and re-layouts  3.55 us (10%)
  other arithmetic  0.84 us (2%)
    ppermute x11, starting transfers between devices, shift(): return lax.ppermute(x, axis, [(i, (i + d) % n) for i in range(n)])  12.1 us
    ppermute x3, starting transfers between devices, swap(): return lax.ppermute(x, axis, [(i, i ^ bits) for i in range(n)])  4.42 us
    ppermute x3, waiting for transfers between devices, swap(): return lax.ppermute(x, axis, [(i, i ^ bits) for i in range(n)])  3.12 us
    pallas_call x1, Pallas kernels, adjoint(): pl.pallas_call(functools.partial(adjoint_kernel, cfg), out_shape=jax.Shap...  2.93 us
    dynamic_slice x2, local copies, waits for them, and re-layouts, shards(): lax.dynamic_index_in_dim(probes.reshape(local, hours, nreg, ntm, kd, cell...  1.93 us
    pallas_call x1, Pallas kernels, own_adjoint(): pl.pallas_call(functools.partial(own_adjoint_kernel, cfg), out_shape=jax....  1.9 us
    pallas_call x1, Pallas kernels, forward(): pl.pallas_call(functools.partial(forward_kernel, cfg, counts), out_shape=...  1.89 us
    unnamed x3, local copies, waits for them, and re-layouts  1.62 us
  transfers between devices with their start and end apart: 14, of which 5 were waited for; matrix products, arithmetic and copies ran while one was open for 7% of the time, Pallas kernels for 15%

profile of v9, /device:TPU:0, one launch (start us, length us, event | category | flops | bytes accessed | tf_op | source)
XLA Modules:
  0.0 35.1 jit_solution(9348049278557327830)
XLA Ops:
  0.0 0.1 pad_add_fusion.1.where_ref
  0.1 0.8 %pad_add_fusion.small_ref = f32[24,512]{1,0:T(8,128)S(1)} fusion(f32[1,16]{1,0:T(1,128)} %bitcast.21, s32[1,16]{1,0:T(1,128)} %bitcast.22, s32[1,512]{1,0:T(1,128)} %bitcast.20, s32[16,16]{1,0:T(8,128)} %param.8), kind=kLoop, calls=%fused_computation | loop fusion | flops 49152 | bytes 52352 | tf_op jit(solution)/shard_map/add | solution.py:142
  0.8 0.0 copy-start
  0.8 0.9 %copy-done = bf16[16,16,2,256]{3,2,1,0:T(2,128)(2,1)S(1)} copy-done((bf16[16,16,2,256]{3,2,1,0:T(2,128)(2,1)S(1)}, bf16[16,16,2,256]{3,2,1,0:T(2,128)(2,1)}, u32[]{:S(2)}) %copy-start) | copy-done | bytes 262168
  1.8 1.6 %pack.1 = (bf16[208,256]{1,0:T(8,128)(2,1)S(1)}, bf16[208,256]{1,0:T(8,128)(2,1)S(1)}, bf16[208,256]{1,0:T(8,128)(2,1)S(1)}, bf16[208,256]{1,0:T(8,128)(2,1)S(1)}) custom-call(s32[3]{0:T(128)S(1)} %pad_add_fusion.1.where_ref, f32[24,512]{1,0:T(8,128)S(1)} %pad_add_fusion.small_ref, bf16[256,2,256]{2,1,0:T(2,128)(2,1)S(1)} %bitcast.17), custom_call_target="tpu_custom_call" | custom-call | tf_op jit(solution)/shard_map/pack/pallas_call | solution.py:144
  3.4 3.0 %collective-permute-start = (bf16[208,256]{1,0:T(8,128)(2,1)S(1)}, bf16[208,256]{1,0:T(8,128)(2,1)S(1)}, u32[]{:S(2)}, u32[]{:S(2)}) collective-permute-start(bf16[208,256]{1,0:T(8,128)(2,1)S(1)} %get-tuple-element.18), channel_id=1, source_target_pairs={{0,4},{4,8},{8,12},{12,0},{1,5},{5,9},{9,13},{13,1},{2,6},{6,10},{... | collective-permute-start | bytes 319496 | tf_op jit(solution)/shard_map/ppermute | solution.py:424
  6.4 2.6 %collective-permute-start.3 = (bf16[208,256]{1,0:T(8,128)(2,1)S(1)}, bf16[208,256]{1,0:T(8,128)(2,1)S(1)}, u32[]{:S(2)}, u32[]{:S(2)}) collective-permute-start(bf16[208,256]{1,0:T(8,128)(2,1)S(1)} %get-tuple-element.19), channel_id=1, source_target_pairs={{0,8},{4,12},{8,0},{12,4},{1,9},{5,13},{9,1},{13,5},{2,10},{6,14},... | collective-permute-start | bytes 319496 | tf_op jit(solution)/shard_map/ppermute | solution.py:424
  9.0 1.3 %collective-permute-start.4 = (bf16[208,256]{1,0:T(8,128)(2,1)S(1)}, bf16[208,256]{1,0:T(8,128)(2,1)S(1)}, u32[]{:S(2)}, u32[]{:S(2)}) collective-permute-start(bf16[208,256]{1,0:T(8,128)(2,1)S(1)} %get-tuple-element.20), channel_id=1, source_target_pairs={{0,12},{4,0},{8,4},{12,8},{1,13},{5,1},{9,5},{13,9},{2,14},{6,2},{... | collective-permute-start | bytes 319496 | tf_op jit(solution)/shard_map/ppermute | solution.py:424
  10.3 1.5 %collective-permute-start.7 = (bf16[208,256]{1,0:T(8,128)(2,1)S(1)}, bf16[208,256]{1,0:T(8,128)(2,1)S(1)}, u32[]{:S(2)}, u32[]{:S(2)}) collective-permute-start(bf16[208,256]{1,0:T(8,128)(2,1)S(1)} %get-tuple-element.17.x_ref), channel_id=1, source_target_pairs={{0,2},{2,0},{1,3},{3,1},{4,6},{6,4},{5,7},{7,5},{8,10},{10,8},{9,1... | collective-permute-start | bytes 319496 | tf_op jit(solution)/shard_map/ppermute | solution.py:424
  11.8 1.8 %constant_dynamic-slice_fusion = bf16[128,8,2,1,2,256]{5,1,4,3,2,0:T(8,128)(2,1)S(1)} fusion(bf16[128,8,2,2,2,256]{5,1,4,3,2,0:T(8,128)(2,1)} %bitcast.19, s32[]{:T(128)S(6)} %select_n.4), kind=kLoop, calls=%fused_computation.3 | loop fusion | bytes 4194308 | tf_op jit(solution)/shard_map/jit(dynamic_index_in_dim)/dynamic_slice | solution.py:447
  13.6 0.1 copy.7
  13.8 0.7 %copy.8 = bf16[64,8,8,256]{3,1,2,0:T(8,128)(2,1)S(1)} copy(bf16[64,8,8,256]{3,2,1,0:T(8,128)(2,1)S(1)} %bitcast.18) | data formatting | bytes 4194304
  14.5 0.1 collective-permute-start.1
  14.5 0.0 collective-permute-done.refs_1_.refs_0_
  14.6 0.5 %collective-permute-start.2 = (bf16[208,256]{1,0:T(8,128)(2,1)S(1)}, bf16[208,256]{1,0:T(8,128)(2,1)S(1)}, u32[]{:S(2)}, u32[]{:S(2)}) collective-permute-start(bf16[208,256]{1,0:T(8,128)(2,1)S(1)} %collective-permute-done.refs_1_.refs_0_), channel_id=1, source_target_pairs={{0,1},{1,0},{2,3},{3,2},{4,5},{5,4},{6,7},{7,6},{8,9},{9,8},{10,11... | collective-permute-start | bytes 319496 | tf_op jit(solution)/shard_map/ppermute | solution.py:424
  15.0 1.0 %collective-permute-done.3.refs_4_.refs_1_ = bf16[208,256]{1,0:T(8,128)(2,1)S(1)} collective-permute-done((bf16[208,256]{1,0:T(8,128)(2,1)S(1)}, bf16[208,256]{1,0:T(8,128)(2,1)S(1)}, u32[]{:S(2)}, u32[]{:S(2)}) %collective-permute-start.3) | collective-permute-done | bytes 106528 | tf_op jit(solution)/shard_map/ppermute | solution.py:424
  16.1 0.0 collective-permute-start.5
  16.1 0.0 collective-permute-done.4.refs_5_.refs_2_
  16.1 0.5 %collective-permute-start.6 = (bf16[208,256]{1,0:T(8,128)(2,1)S(1)}, bf16[208,256]{1,0:T(8,128)(2,1)S(1)}, u32[]{:S(2)}, u32[]{:S(2)}) collective-permute-start(bf16[208,256]{1,0:T(8,128)(2,1)S(1)} %collective-permute-done.4.refs_5_.refs_2_), channel_id=1, source_target_pairs={{0,1},{1,0},{2,3},{3,2},{4,5},{5,4},{6,7},{7,6},{8,9},{9,8},{10,11... | collective-permute-start | bytes 319496 | tf_op jit(solution)/shard_map/ppermute | solution.py:424
  16.6 0.0 collective-permute-done.7.refs_9_.refs_0_
  16.6 1.6 %collective-permute-start.11 = (bf16[624,256]{1,0:T(8,128)(2,1)S(1)}, bf16[624,256]{1,0:T(8,128)(2,1)S(1)}, u32[]{:S(2)}, u32[]{:S(2)}) collective-permute-start(bf16[624,256]{1,0:T(8,128)(2,1)S(1)} %stack.18), channel_id=1, source_target_pairs={{0,2},{2,0},{1,3},{3,1},{4,6},{6,4},{5,7},{7,5},{8,10},{10,8},{9,1... | collective-permute-start | bytes 958472 | tf_op jit(solution)/shard_map/ppermute | solution.py:424
  18.2 0.0 collective-permute-done.1.refs_2_
  18.2 0.0 collective-permute-done.2.refs_3_
  18.2 0.0 collective-permute-done.5.refs_6_
  18.2 0.0 collective-permute-done.6.refs_7_
  18.2 1.9 %forward.1.refs_8_ = f32[8,128]{1,0:T(8,128)S(1)} custom-call(bf16[208,256]{1,0:T(8,128)(2,1)S(1)} %after.1.refs_0_, bf16[208,256]{1,0:T(8,128)(2,1)S(1)} %collective-permute-done.refs_1_.refs_0_, bf16[208,256]{1,0:T(8,128)(2,1)S(1)} %collective-permute-done.1.refs_2_, bf16[208,256]{1,0:T(8,128)(2,1)S(1)} %collective-permute-done.2.refs_3_, ...), custom_call_target="tpu_custom_call" | custom-call | tf_op jit(solution)/shard_map/forward/pallas_call | solution.py:263
  20.1 3.8 %collective-permute-start.10 = (f32[8,128]{1,0:T(8,128)S(1)}, f32[8,128]{1,0:T(8,128)S(1)}, u32[]{:S(2)}, u32[]{:S(2)}) collective-permute-start(f32[8,128]{1,0:T(8,128)S(1)} %forward.1.refs_8_), channel_id=1, source_target_pairs={{0,12},{4,8},{8,4},{12,0},{1,13},{5,9},{9,5},{13,1},{2,14},{6,10},... | collective-permute-start | bytes 12296 | tf_op jit(solution)/shard_map/ppermute | solution.py:430
  23.9 0.0 collective-permute-start.9
  23.9 0.6 %collective-permute-start.8 = (f32[8,128]{1,0:T(8,128)S(1)}, f32[8,128]{1,0:T(8,128)S(1)}, u32[]{:S(2)}, u32[]{:S(2)}) collective-permute-start(f32[8,128]{1,0:T(8,128)S(1)} %forward.1.refs_8_), channel_id=1, source_target_pairs={{0,8},{4,12},{8,0},{12,4},{1,9},{5,13},{9,1},{13,5},{2,10},{6,14},... | collective-permute-start | bytes 12296 | tf_op jit(solution)/shard_map/ppermute | solution.py:430
  24.5 0.7 %prepare0.2 = (bf16[384,2048]{1,0:T(8,128)(2,1)S(1)}, bf16[128,384]{1,0:T(8,128)(2,1)S(1)}, bf16[128,384]{1,0:T(8,128)(2,1)S(1)}, f32[8,384]{1,0:T(8,128)S(1)}) custom-call(bf16[208,256]{1,0:T(8,128)(2,1)S(1)} %after.1.refs_0_, bf16[208,256]{1,0:T(8,128)(2,1)S(1)} %collective-permute-done.refs_1_.refs_0_, ...), custom_call_target="tpu_custom_call" | custom-call | bytes 294912 | tf_op jit(solution)/shard_map/prepare0/pallas_call | solution.py:304
  25.3 0.2 collective-permute-done.10
  25.5 2.0 %collective-permute-done.9 = f32[8,128]{1,0:T(8,128)S(1)} collective-permute-done((f32[8,128]{1,0:T(8,128)S(1)}, f32[8,128]{1,0:T(8,128)S(1)}, u32[]{:S(2)}, u32[]{:S(2)}) %collective-permute-start.9) | collective-permute-done | bytes 4128 | tf_op jit(solution)/shard_map/ppermute | solution.py:430
  27.5 0.9 %collective-permute-done.8 = f32[8,128]{1,0:T(8,128)S(1)} collective-permute-done((f32[8,128]{1,0:T(8,128)S(1)}, f32[8,128]{1,0:T(8,128)S(1)}, u32[]{:S(2)}, u32[]{:S(2)}) %collective-permute-start.8) | collective-permute-done | bytes 4128 | tf_op jit(solution)/shard_map/ppermute | solution.py:430
  28.4 0.0 collective-permute-done.11.refs_1_
  28.4 0.1 collective-permute-start.12
  28.5 0.9 %collective-permute-start.13 = (f32[8,128]{1,0:T(8,128)S(1)}, f32[8,128]{1,0:T(8,128)S(1)}, u32[]{:S(2)}, u32[]{:S(2)}) collective-permute-start(f32[8,128]{1,0:T(8,128)S(1)} %add_add_fusion.obs_ref.refs_2_), channel_id=1, source_target_pairs={{0,2},{2,0},{1,3},{3,1},{4,6},{6,4},{5,7},{7,5},{8,10},{10,8},{9,1... | collective-permute-start | bytes 12296 | tf_op jit(solution)/shard_map/ppermute | solution.py:424
  29.4 1.9 %own_adjoint.1.before_ref = f32[256,2048]{1,0:T(8,128)S(1)} custom-call(s32[3]{0:T(128)S(1)} %pad_add_fusion.1.where_ref, bf16[384,2048]{1,0:T(8,128)(2,1)S(1)} %get-tuple-element.21.f8_ref, bf16[128,384]{1,0:T(8,128)(2,1)S(1)} %get-tuple-element.22.own_ref, bf16[128,384]{1,0:T(8,128)(2,1)S(1)} %get-tuple-element.23.to_r_ref, ...), custom_call_target="tpu_custom_call" | custom-call | flops 805306368 | bytes 1572864 | tf_op jit(solution)/shard_map/own_adjoint/pallas_call | solution.py:349
  31.3 0.0 collective-permute-done.12.refs_1_
  31.4 0.7 %prepare0.3 = (bf16[384,2048]{1,0:T(8,128)(2,1)S(1)}, bf16[128,384]{1,0:T(8,128)(2,1)S(1)}, bf16[128,384]{1,0:T(8,128)(2,1)S(1)}, f32[8,384]{1,0:T(8,128)S(1)}) custom-call(bf16[832,256]{1,0:T(8,128)(2,1)S(1)} %stack.19.refs_0_, bf16[832,256]{1,0:T(8,128)(2,1)S(1)} %collective-permute-done.12.refs_1_), custom_call_target="tpu_custom_call" | custom-call | bytes 294912 | tf_op jit(solution)/shard_map/prepare0/pallas_call | solution.py:304
  32.1 0.1 collective-permute-done.13.refs_0_
  32.2 2.9 %adjoint.1 = f32[1024,512]{1,0:T(8,128)} custom-call(s32[3]{0:T(128)S(1)} %pad_add_fusion.1.where_ref, f32[256,2048]{1,0:T(8,128)S(1)} %own_adjoint.1.before_ref, bf16[384,2048]{1,0:T(8,128)(2,1)S(1)} %get-tuple-element.25.f8_ref, bf16[128,384]{1,0:T(8,128)(2,1)S(1)} %get-tuple-element.26.own_ref, bf16[128,384]{1,0:T(8,128)(2,1)S(1)} %get-tuple-element.27.to_r_ref, ...), custom_call_target="tpu_custom_call" | custom-call | tf_op jit(solution)/shard_map/adjoint/pallas_call | solution.py:407
  (4 shorter events, 0.1 us)
Async XLA Ops:
  0.8 1.0 %copy-start = (bf16[16,16,2,256]{3,2,1,0:T(2,128)(2,1)S(1)}, bf16[16,16,2,256]{3,2,1,0:T(2,128)(2,1)}, u32[]{:S(2)}) copy-start(bf16[16,16,2,256]{3,2,1,0:T(2,128)(2,1)} %param.7) | copy-start | bytes 786436
  3.4 11.2 %collective-permute-start = (bf16[208,256]{1,0:T(8,128)(2,1)S(1)}, bf16[208,256]{1,0:T(8,128)(2,1)S(1)}, u32[]{:S(2)}, u32[]{:S(2)}) collective-permute-start(bf16[208,256]{1,0:T(8,128)(2,1)S(1)} %get-tuple-element.18), channel_id=1, source_target_pairs={{0,4},{4,8},{8,12},{12,0},{1,5},{5,9},{9,13},{13,1},{2,6},{6,10},{... | collective-permute-start | bytes 319496 | tf_op jit(solution)/shard_map/ppermute | solution.py:424
  6.4 9.7 %collective-permute-start.3 = (bf16[208,256]{1,0:T(8,128)(2,1)S(1)}, bf16[208,256]{1,0:T(8,128)(2,1)S(1)}, u32[]{:S(2)}, u32[]{:S(2)}) collective-permute-start(bf16[208,256]{1,0:T(8,128)(2,1)S(1)} %get-tuple-element.19), channel_id=1, source_target_pairs={{0,8},{4,12},{8,0},{12,4},{1,9},{5,13},{9,1},{13,5},{2,10},{6,14},... | collective-permute-start | bytes 319496 | tf_op jit(solution)/shard_map/ppermute | solution.py:424
  9.0 7.1 %collective-permute-start.4 = (bf16[208,256]{1,0:T(8,128)(2,1)S(1)}, bf16[208,256]{1,0:T(8,128)(2,1)S(1)}, u32[]{:S(2)}, u32[]{:S(2)}) collective-permute-start(bf16[208,256]{1,0:T(8,128)(2,1)S(1)} %get-tuple-element.20), channel_id=1, source_target_pairs={{0,12},{4,0},{8,4},{12,8},{1,13},{5,1},{9,5},{13,9},{2,14},{6,2},{... | collective-permute-start | bytes 319496 | tf_op jit(solution)/shard_map/ppermute | solution.py:424
  10.3 6.3 %collective-permute-start.7 = (bf16[208,256]{1,0:T(8,128)(2,1)S(1)}, bf16[208,256]{1,0:T(8,128)(2,1)S(1)}, u32[]{:S(2)}, u32[]{:S(2)}) collective-permute-start(bf16[208,256]{1,0:T(8,128)(2,1)S(1)} %get-tuple-element.17.x_ref), channel_id=1, source_target_pairs={{0,2},{2,0},{1,3},{3,1},{4,6},{6,4},{5,7},{7,5},{8,10},{10,8},{9,1... | collective-permute-start | bytes 319496 | tf_op jit(solution)/shard_map/ppermute | solution.py:424
  14.5 3.7 %collective-permute-start.1 = (bf16[208,256]{1,0:T(8,128)(2,1)S(1)}, bf16[208,256]{1,0:T(8,128)(2,1)S(1)}, u32[]{:S(2)}, u32[]{:S(2)}) collective-permute-start(bf16[208,256]{1,0:T(8,128)(2,1)S(1)} %after.1.refs_0_), channel_id=1, source_target_pairs={{0,1},{1,0},{2,3},{3,2},{4,5},{5,4},{6,7},{7,6},{8,9},{9,8},{10,11... | collective-permute-start | bytes 319496 | tf_op jit(solution)/shard_map/ppermute | solution.py:424
  14.6 3.6 %collective-permute-start.2 = (bf16[208,256]{1,0:T(8,128)(2,1)S(1)}, bf16[208,256]{1,0:T(8,128)(2,1)S(1)}, u32[]{:S(2)}, u32[]{:S(2)}) collective-permute-start(bf16[208,256]{1,0:T(8,128)(2,1)S(1)} %collective-permute-done.refs_1_.refs_0_), channel_id=1, source_target_pairs={{0,1},{1,0},{2,3},{3,2},{4,5},{5,4},{6,7},{7,6},{8,9},{9,8},{10,11... | collective-permute-start | bytes 319496 | tf_op jit(solution)/shard_map/ppermute | solution.py:424
  16.1 2.1 %collective-permute-start.5 = (bf16[208,256]{1,0:T(8,128)(2,1)S(1)}, bf16[208,256]{1,0:T(8,128)(2,1)S(1)}, u32[]{:S(2)}, u32[]{:S(2)}) collective-permute-start(bf16[208,256]{1,0:T(8,128)(2,1)S(1)} %collective-permute-done.3.refs_4_.refs_1_), channel_id=1, source_target_pairs={{0,1},{1,0},{2,3},{3,2},{4,5},{5,4},{6,7},{7,6},{8,9},{9,8},{10,11... | collective-permute-start | bytes 319496 | tf_op jit(solution)/shard_map/ppermute | solution.py:424
  16.1 2.1 %collective-permute-start.6 = (bf16[208,256]{1,0:T(8,128)(2,1)S(1)}, bf16[208,256]{1,0:T(8,128)(2,1)S(1)}, u32[]{:S(2)}, u32[]{:S(2)}) collective-permute-start(bf16[208,256]{1,0:T(8,128)(2,1)S(1)} %collective-permute-done.4.refs_5_.refs_2_), channel_id=1, source_target_pairs={{0,1},{1,0},{2,3},{3,2},{4,5},{5,4},{6,7},{7,6},{8,9},{9,8},{10,11... | collective-permute-start | bytes 319496 | tf_op jit(solution)/shard_map/ppermute | solution.py:424
  16.6 11.8 %collective-permute-start.11 = (bf16[624,256]{1,0:T(8,128)(2,1)S(1)}, bf16[624,256]{1,0:T(8,128)(2,1)S(1)}, u32[]{:S(2)}, u32[]{:S(2)}) collective-permute-start(bf16[624,256]{1,0:T(8,128)(2,1)S(1)} %stack.18), channel_id=1, source_target_pairs={{0,2},{2,0},{1,3},{3,1},{4,6},{6,4},{5,7},{7,5},{8,10},{10,8},{9,1... | collective-permute-start | bytes 958472 | tf_op jit(solution)/shard_map/ppermute | solution.py:424
  20.1 5.4 %collective-permute-start.10 = (f32[8,128]{1,0:T(8,128)S(1)}, f32[8,128]{1,0:T(8,128)S(1)}, u32[]{:S(2)}, u32[]{:S(2)}) collective-permute-start(f32[8,128]{1,0:T(8,128)S(1)} %forward.1.refs_8_), channel_id=1, source_target_pairs={{0,12},{4,8},{8,4},{12,0},{1,13},{5,9},{9,5},{13,1},{2,14},{6,10},... | collective-permute-start | bytes 12296 | tf_op jit(solution)/shard_map/ppermute | solution.py:430
  23.9 3.6 %collective-permute-start.9 = (f32[8,128]{1,0:T(8,128)S(1)}, f32[8,128]{1,0:T(8,128)S(1)}, u32[]{:S(2)}, u32[]{:S(2)}) collective-permute-start(f32[8,128]{1,0:T(8,128)S(1)} %forward.1.refs_8_), channel_id=1, source_target_pairs={{0,4},{4,0},{8,12},{12,8},{1,5},{5,1},{9,13},{13,9},{2,6},{6,2},{1... | collective-permute-start | bytes 12296 | tf_op jit(solution)/shard_map/ppermute | solution.py:430
  23.9 4.5 %collective-permute-start.8 = (f32[8,128]{1,0:T(8,128)S(1)}, f32[8,128]{1,0:T(8,128)S(1)}, u32[]{:S(2)}, u32[]{:S(2)}) collective-permute-start(f32[8,128]{1,0:T(8,128)S(1)} %forward.1.refs_8_), channel_id=1, source_target_pairs={{0,8},{4,12},{8,0},{12,4},{1,9},{5,13},{9,1},{13,5},{2,10},{6,14},... | collective-permute-start | bytes 12296 | tf_op jit(solution)/shard_map/ppermute | solution.py:430
  28.4 2.9 %collective-permute-start.12 = (bf16[832,256]{1,0:T(8,128)(2,1)S(1)}, bf16[832,256]{1,0:T(8,128)(2,1)S(1)}, u32[]{:S(2)}, u32[]{:S(2)}) collective-permute-start(bf16[832,256]{1,0:T(8,128)(2,1)S(1)} %stack.19.refs_0_), channel_id=1, source_target_pairs={{0,1},{1,0},{2,3},{3,2},{4,5},{5,4},{6,7},{7,6},{8,9},{9,8},{10,11... | collective-permute-start | bytes 1277960 | tf_op jit(solution)/shard_map/ppermute | solution.py:424
  28.5 3.7 %collective-permute-start.13 = (f32[8,128]{1,0:T(8,128)S(1)}, f32[8,128]{1,0:T(8,128)S(1)}, u32[]{:S(2)}, u32[]{:S(2)}) collective-permute-start(f32[8,128]{1,0:T(8,128)S(1)} %add_add_fusion.obs_ref.refs_2_), channel_id=1, source_target_pairs={{0,2},{2,0},{1,3},{3,1},{4,6},{6,4},{5,7},{7,5},{8,10},{10,8},{9,1... | collective-permute-start | bytes 12296 | tf_op jit(solution)/shard_map/ppermute | solution.py:424
